TPU v7x, 32 devices: a whole 2x2x4 slice. The times are simulated.
32 devices in a mesh: dp: 8 (over y, x, core), seq: 4 (over z).
Axes of the slice: x: 2, y: 2, z: 4, core: 2. Of those that a mesh axis runs over, the one named last changes fastest.
Arguments:
- tokens: bfloat16 [16384, 768], P(('dp', 'seq')), may hold values from -6 to 6
- clip_lengths: int32 [8, 4], P('dp'), may hold values from 1 to 1537, as said below
- ln1_gain: float32 [768], replicated, may hold values from 0.25 to 1.75
- ln1_shift: float32 [768], replicated, may hold values from -3 to 3
- w_qkv: bfloat16 [768, 2304], replicated, may hold values from -0.21875 to 0.21875
- bias_query: float32 [768], replicated, may hold values from -3 to 3
- bias_value: float32 [768], replicated, may hold values from -3 to 3
- w_out: bfloat16 [768, 768], replicated, may hold values from -1.75 to 1.75
- bias_out: float32 [768], replicated, may hold values from -3 to 3
- ln2_gain: float32 [768], replicated, may hold values from 0.25 to 1.75
- ln2_shift: float32 [768], replicated, may hold values from -3 to 3
- w_up: bfloat16 [768, 3072], replicated, may hold values from -0.21875 to 0.21875
- bias_up: float32 [3072], replicated, may hold values from -3 to 3
- w_down: bfloat16 [3072, 768], replicated, may hold values from -0.109375 to 0.109375
- bias_down: float32 [768], replicated, may hold values from -3 to 3
- cotangent: bfloat16 [16384, 768], P(('dp', 'seq')), may hold values from -6 to 6
Outputs:
- block_out: bfloat16 [16384, 768], P(('dp', 'seq'))
- grad_tokens: bfloat16 [16384, 768], P(('dp', 'seq'))
- grad_ln1_gain: float32 [768], P('dp')
- grad_ln1_shift: float32 [768], P('dp')
- grad_w_qkv: float32 [768, 2304], P('dp')
- grad_bias_query: float32 [768], P('dp')
- grad_bias_value: float32 [768], P('dp')
- grad_w_out: float32 [768, 768], P('dp')
- grad_bias_out: float32 [768], P('dp')
- grad_ln2_gain: float32 [768], P('dp')
- grad_ln2_shift: float32 [768], P('dp')
- grad_w_up: float32 [768, 3072], P('dp')
- grad_bias_up: float32 [3072], P('dp')
- grad_w_down: float32 [3072, 768], P('dp')
- grad_bias_down: float32 [768], P('dp')
Inputs may be any that keep to these rules, and one draw needn't show every extreme that they name: `clip_lengths`: each row's 4 lengths sum to 2048. In each row one clip, at a place drawn from the seed, has 1537 patches and another has a single patch; the others share the rest.
All inputs are finite; a program needn't handle non-finite values.
Results may differ from a plain program's by a relative error of at most 0.012.
Values may be sent and summed in bfloat16 or wider, within the bound.
A program may use at most 192 MiB of HBM per device.

v0:
```python
import functools
import math

import jax
import jax.numpy as jnp
from jax import lax
from jax.experimental import pallas as pl
from jax.experimental.pallas import tpu as pltpu
from jax.sharding import PartitionSpec as P

HDIM = 64
LANES = 128
STATS = 16
F32 = jnp.float32
BF16 = jnp.bfloat16
VMEM_BYTES = 56 << 20
NT = (((1,), (1,)), ((), ()))
NN = (((1,), (0,)), ((), ()))

epsilon = 1e-06
masked_score = -1e30


def dot_as(left, right, dims):
    return lax.dot_general(left, right, dims, preferred_element_type=F32)


def matmul(left, right):
    return dot_as(left, right, NN)


def inner_rows(left, right):
    return dot_as(left, right, (((0,), (0,)), ((), ())))


def inner_cols(left, right):
    return dot_as(left, right, NT)


def layer_norm(values, gain, shift):
    center = values - jnp.mean(values, -1, keepdims=True)
    inverse = lax.rsqrt(jnp.mean(center * center, -1, keepdims=True) + epsilon)
    normed = center * inverse
    return (normed * gain + shift, normed, inverse)


def norm_back(grad_out, normed, inverse, gain):
    scaled = grad_out * gain
    grad_in = inverse * (
        scaled
        - jnp.mean(scaled, -1, keepdims=True)
        - normed * jnp.mean(scaled * normed, -1, keepdims=True)
    )
    return (grad_in, jnp.sum(grad_out * normed, 0), jnp.sum(grad_out, 0))


def pick(table, index):
    found = jnp.int32(table[0])
    for i, value in enumerate(table[1:], 1):
        found = jnp.where(index == i, jnp.int32(value), found)
    return found


def place_of_device():
    dp, z = lax.axis_index("dp"), lax.axis_index("seq")
    return lax.div(dp, jnp.int32(4)), lax.rem(dp, jnp.int32(4)), z


def greet(devices):
    barrier = pltpu.get_barrier_semaphore()
    for device in devices:
        pl.semaphore_signal(barrier, inc=1, device_id=device, device_id_type=pl.DeviceIdType.MESH)
    pl.semaphore_wait(barrier, len(devices))


def remote(source, target, sent, landed, device):
    return pltpu.make_async_remote_copy(
        src_ref=source,
        dst_ref=target,
        send_sem=sent,
        recv_sem=landed,
        device_id=device,
        device_id_type=pl.DeviceIdType.MESH,
    )


def routes(plane, place):
    y, j, z = place_of_device()
    targets = [(y * 4 + pick(place[h], z), pick(plane, j)) for h in range(2)]
    sources = [
        (
            y * 4 + pick([plane.index(p) for p in range(4)], z),
            pick([place[h].index(p) for p in range(4)], j),
        )
        for h in range(2)
    ]
    return targets, sources


def moves(source, target, sent, landed, devices):
    half = source.shape[0] // 2
    return [
        remote(
            source.at[pl.ds(h * half, half)],
            target.at[pl.ds(h * half, half)],
            sent.at[h],
            landed.at[h],
            devices[h],
        )
        for h in range(2)
    ]


def head_lanes(rows, head):
    lane = lax.broadcasted_iota(jnp.int32, (rows, LANES), 1)
    return (lane < HDIM) if head == 0 else (lane >= HDIM)


def place_stats(stat, rows, pair, values):
    lane = lax.broadcasted_iota(jnp.int32, (values[0].shape[0], LANES), 1)
    old = stat[rows, :]
    stat[rows, :] = jnp.where(
        lane == 2 * pair, values[0], jnp.where(lane == 2 * pair + 1, values[1], old)
    )


def attend_kernel(sub, ways, q_ref, k_ref, v_ref, mark_q, mark_k, *refs):
    pair = pl.program_id(0)
    if ways is None:
        out_ref, chance_ref, lse_ref, stat = refs
    else:
        home_ref, out_ref, chance_ref, lse_ref, here_ref, stat, sent, landed = refs
        targets, sources = routes(*ways)

        @pl.when(pair == 0)
        def _():
            greet(targets + sources)
            for copy in moves(home_ref, here_ref, sent, landed, targets):
                copy.start()

    keys = jnp.concatenate([k_ref[...], mark_k[...]], 1)
    values = v_ref[...]

    def step(i, carry):
        rows = pl.ds(pl.multiple_of(i * sub, sub), sub)
        query = q_ref[rows, :] * jnp.asarray(1.0 / math.sqrt(HDIM), BF16)
        outs, totals = [], []
        for head in range(2):
            own = jnp.where(head_lanes(sub, head), query, jnp.zeros_like(query))
            scores = dot_as(jnp.concatenate([own, mark_q[rows, :]], 1), keys, NT)
            highest = jnp.max(scores, -1, keepdims=True)
            powers = jnp.exp(scores - highest)
            total = jnp.sum(powers, -1, keepdims=True)
            chances = (powers * (1.0 / total)).astype(BF16)
            chance_ref[head, rows, :] = chances
            outs.append(dot_as(chances, values, NN))
            totals.append(highest + jnp.log(total))
        out_ref[rows, :] = jnp.where(head_lanes(sub, 0), outs[0], outs[1]).astype(BF16)
        place_stats(stat, rows, pair, totals)
        return carry

    lax.fori_loop(0, q_ref.shape[0] // sub, step, 0)

    @pl.when(pair == pl.num_programs(0) - 1)
    def _():
        lse_ref[...] = jnp.transpose(stat[...])[:STATS]
        if ways is not None:
            for copy in moves(home_ref, here_ref, sent, landed, targets):
                copy.wait()


def grad_query_kernel(
    sub, chance_ref, grad_ref, out_ref, k_ref, v_ref, dq_ref, delta_ref, stat
):
    pair = pl.program_id(0)
    keys, values = k_ref[...], v_ref[...]

    def step(i, carry):
        rows = pl.ds(pl.multiple_of(i * sub, sub), sub)
        grad = grad_ref[rows, :]
        product = grad.astype(F32) * out_ref[rows, :].astype(F32)
        outs, deltas = [], []
        for head in range(2):
            own = head_lanes(sub, head)
            delta = jnp.sum(jnp.where(own, product, 0.0), -1, keepdims=True)
            grad_chances = dot_as(jnp.where(own, grad, jnp.zeros_like(grad)), values, NT)
            scores = (chance_ref[head, rows, :].astype(F32) * (grad_chances - delta)).astype(BF16)
            outs.append(dot_as(scores, keys, NN))
            deltas.append(delta)
        both = jnp.where(head_lanes(sub, 0), outs[0], outs[1])
        dq_ref[rows, :] = (both * (1.0 / math.sqrt(HDIM))).astype(BF16)
        place_stats(stat, rows, pair, deltas)
        return carry

    lax.fori_loop(0, grad_ref.shape[0] // sub, step, 0)

    @pl.when(pair == pl.num_programs(0) - 1)
    def _():
        delta_ref[...] = jnp.transpose(stat[...])[:STATS]


def grad_key_kernel(sub, pieces, k_ref, v_ref, q_ref, *refs):
    g_refs = refs[:pieces]
    lse_refs, delta_refs = refs[pieces : 2 * pieces], refs[2 * pieces : 3 * pieces]
    mark_k, mark_q, dk_ref, dv_ref = refs[3 * pieces :]
    pair = pl.program_id(0)
    queries = q_ref[...]
    grads = jnp.concatenate([ref[...] for ref in g_refs], 0)
    scaled = jnp.concatenate(
        [queries * jnp.asarray(1.0 / math.sqrt(HDIM), BF16), mark_q[...]], 1
    )

    def stats(which, head):
        return jnp.concatenate([ref[pl.ds(2 * pair + head, 1), :] for ref in which], 1)

    log_totals = [stats(lse_refs, head) for head in range(2)]
    deltas = [stats(delta_refs, head) for head in range(2)]

    def step(i, carry):
        rows = pl.ds(pl.multiple_of(i * sub, sub), sub)
        key, value = k_ref[rows, :], v_ref[rows, :]
        dks, dvs = [], []
        for head in range(2):
            own = head_lanes(sub, head)
            key_own = jnp.where(own, key, jnp.zeros_like(key))
            value_own = jnp.where(own, value, jnp.zeros_like(value))
            scores = dot_as(jnp.concatenate([key_own, mark_k[rows, :]], 1), scaled, NT)
            chances = jnp.exp(scores - log_totals[head])
            grad_chances = dot_as(value_own, grads, NT)
            grad_scores = (chances * (grad_chances - deltas[head])).astype(BF16)
            dvs.append(dot_as(chances.astype(BF16), grads, NN))
            dks.append(dot_as(grad_scores, queries, NN))
        first = head_lanes(sub, 0)
        dk = jnp.where(first, dks[0], dks[1]) * (1.0 / math.sqrt(HDIM))
        dk_ref[rows, :] = dk.astype(BF16)
        dv_ref[rows, :] = jnp.where(first, dvs[0], dvs[1]).astype(BF16)
        return carry

    lax.fori_loop(0, k_ref.shape[0] // sub, step, 0)


def columns(rows, first):
    return pl.BlockSpec((rows, LANES), lambda t: (0, first + t))


def whole(array):
    return pl.BlockSpec(array.shape, lambda t: (0,) * array.ndim)


def kernel_call(kernel, name, grid, in_specs, out_specs, out_shape, scratch, flops, moved, **params):
    return pl.pallas_call(
        kernel,
        grid=grid,
        in_specs=in_specs,
        out_specs=out_specs,
        out_shape=out_shape,
        scratch_shapes=scratch,
        compiler_params=pltpu.CompilerParams(vmem_limit_bytes=VMEM_BYTES, **params),
        cost_estimate=pl.CostEstimate(flops=flops, bytes_accessed=moved, transcendentals=0),
        name=name,
    )


def attend(plan, own, projected, mark_q, mark_k, cotangent, sub=256):
    rows, width = mark_q.shape[0], own.shape[1] // 3
    length, pairs = projected.shape[0], width // LANES
    stats = jax.ShapeDtypeStruct((STATS, rows), F32)
    anywhere = pl.BlockSpec(memory_space=pl.ANY)
    ways = plan.ways
    moving = [] if ways is None else [cotangent]
    params = {} if ways is None else {"collective_id": 1, "has_side_effects": True}
    results = kernel_call(
        functools.partial(attend_kernel, sub, ways),
        "attend",
        (pairs,),
        [
            columns(rows, 0),
            columns(length, pairs),
            columns(length, 2 * pairs),
            whole(mark_q),
            whole(mark_k),
        ]
        + [anywhere] * len(moving),
        [
            columns(rows, 0),
            pl.BlockSpec((2, rows, length), lambda t: (t, 0, 0)),
            whole(stats),
        ]
        + [anywhere] * len(moving),
        [
            jax.ShapeDtypeStruct((rows, width), BF16),
            jax.ShapeDtypeStruct((2 * pairs, rows, length), BF16),
            stats,
        ]
        + [jax.ShapeDtypeStruct(array.shape, array.dtype) for array in moving],
        [pltpu.VMEM((rows, LANES), F32)] + [pltpu.SemaphoreType.DMA((2,))] * (2 * len(moving)),
        24 * rows * length * width,
        4 * pairs * rows * length,
        **params,
    )(own, projected, projected, mark_q, mark_k, *moving)
    return tuple(results) if moving else tuple(results) + (cotangent,)


def grad_query(chances, grad, attended, projected, sub=256):
    rows, width = grad.shape
    length, pairs = projected.shape[0], width // LANES
    stats = jax.ShapeDtypeStruct((STATS, rows), F32)
    return kernel_call(
        functools.partial(grad_query_kernel, sub),
        "grad_query",
        (pairs,),
        [
            pl.BlockSpec((2, rows, length), lambda t: (t, 0, 0)),
            columns(rows, 0),
            columns(rows, 0),
            columns(length, pairs),
            columns(length, 2 * pairs),
        ],
        [columns(rows, 0), whole(stats)],
        [jax.ShapeDtypeStruct((rows, width), BF16), stats],
        [pltpu.VMEM((rows, LANES), F32)],
        16 * rows * length * width,
        4 * pairs * rows * length,
    )(chances, grad, attended, projected, projected)


def grad_key_value(own, projected, grads, log_totals, deltas, mark_k, mark_q, sub=256):
    rows, width = grads[0].shape
    pieces, pairs = len(grads), width // LANES
    length = rows * pieces
    result = jax.ShapeDtypeStruct((rows, width), BF16)
    return kernel_call(
        functools.partial(grad_key_kernel, sub, pieces),
        "grad_key_value",
        (pairs,),
        [columns(rows, pairs), columns(rows, 2 * pairs), columns(length, 0)]
        + [columns(rows, 0)] * pieces
        + [whole(log_totals[0])] * (2 * pieces)
        + [whole(mark_k), whole(mark_q)],
        [columns(rows, 0)] * 2,
        [result] * 2,
        [],
        32 * rows * length * width,
        8 * length * width,
    )(own, own, projected, *grads, *log_totals, *deltas, mark_k, mark_q)


def grad_weight_kernel(parts, index_ref, left_ref, right_ref, keep_ref, send_ref, turned):
    @pl.when(pl.program_id(0) == 0)
    def _():
        turned[...] = jnp.transpose(left_ref[...])

    total = dot_as(turned[...], right_ref[...], NN)
    rows = total.shape[0] // parts
    me = index_ref[0]
    for part in range(parts):
        place = part ^ me
        block = total[part * rows : (part + 1) * rows].astype(BF16)

        @pl.when(place % 2 == 0)
        def _():
            keep_ref[place // 2] = block

        @pl.when(place % 2 == 1)
        def _():
            send_ref[place // 2] = block


def grad_weight_wide(left, right, me, parts, tile):
    length, height = left.shape
    width = right.shape[1]
    rows = height // parts
    half = jax.ShapeDtypeStruct((parts // 2, rows, width), BF16)
    out = pl.BlockSpec((parts // 2, rows, tile), lambda n, at: (0, 0, n))
    return pl.pallas_call(
        functools.partial(grad_weight_kernel, parts),
        grid_spec=pltpu.PrefetchScalarGridSpec(
            num_scalar_prefetch=1,
            grid=(width // tile,),
            in_specs=[
                pl.BlockSpec((length, height), lambda n, at: (0, 0)),
                pl.BlockSpec((length, tile), lambda n, at: (0, n)),
            ],
            out_specs=[out, out],
            scratch_shapes=[pltpu.VMEM((height, length), BF16)],
        ),
        out_shape=[half, half],
        compiler_params=pltpu.CompilerParams(vmem_limit_bytes=VMEM_BYTES),
        cost_estimate=pl.CostEstimate(
            flops=2 * length * height * width, bytes_accessed=2 * height * width, transcendentals=0
        ),
        name="grad_weight_wide",
    )(me, left, right)


def grad_weight_tall_kernel(index_ref, left_ref, right_ref, out_ref):
    out_ref[0] = inner_rows(left_ref[...], right_ref[...]).astype(BF16)


def grad_weight_tall(left, right, me, parts):
    length, height = left.shape
    width = right.shape[1]
    rows = height // parts

    def half(which):
        return pl.pallas_call(
            grad_weight_tall_kernel,
            grid_spec=pltpu.PrefetchScalarGridSpec(
                num_scalar_prefetch=1,
                grid=(parts // 2,),
                in_specs=[
                    pl.BlockSpec((length, rows), lambda b, at: (0, (2 * b + which) ^ at[0])),
                    pl.BlockSpec((length, width), lambda b, at: (0, 0)),
                ],
                out_specs=pl.BlockSpec((1, rows, width), lambda b, at: (b, 0, 0)),
            ),
            out_shape=jax.ShapeDtypeStruct((parts // 2, rows, width), BF16),
            compiler_params=pltpu.CompilerParams(vmem_limit_bytes=VMEM_BYTES),
            cost_estimate=pl.CostEstimate(
                flops=length * height * width, bytes_accessed=height * width, transcendentals=0
            ),
            name="grad_weight_tall",
        )(me, left, right)

    return half(0), half(1)


def start_kernel(
    plane,
    place,
    tokens_ref,
    lengths_ref,
    gain_ref,
    shift_ref,
    w_ref,
    bias_ref,
    projected_ref,
    hidden_ref,
    here_ref,
    found_ref,
    rows,
    staged,
    sent,
    landed,
    out_sem,
):
    y, j, z = place_of_device()
    dp = lax.axis_index("dp")
    half = tokens_ref.shape[0] // 2
    part = half // 2
    targets, sources = routes(plane, place)
    core, across = (dp + 1 - 2 * lax.rem(dp, jnp.int32(2)), z), (
        y * 4 + lax.rem(j + 2, jnp.int32(4)),
        z,
    )
    greet(targets + sources + [core, across])

    def span(i):
        return pl.ds(pl.multiple_of(lax.rem(i, 2) * half + lax.div(i, 2) * part, part), part)

    def moved(i, h):
        at = pl.ds(h * half + (i // 2) * part, part)
        return remote(
            tokens_ref.at[at], rows.at[0, at], sent.at[0, i], landed.at[0, i], targets[h]
        )

    def lengths():
        return remote(lengths_ref, found_ref, sent.at[4, 0], landed.at[4, 0], targets[0])

    def forward(i, origin, piece, device):
        at = span(i)
        return remote(
            rows.at[origin, at], rows.at[piece, at], sent.at[piece, i], landed.at[piece, i], device
        )

    def to_hbm(piece, i):
        at = pl.ds(pl.multiple_of(piece * 2 * half + span(i).start, part), part)
        return pltpu.make_async_copy(
            staged.at[at], projected_ref.at[at], out_sem.at[piece, i]
        )

    def project(piece, i):
        at = span(i)
        values = rows[piece, at, :].astype(F32)
        hidden = layer_norm(values, gain_ref[...], shift_ref[...])[0].astype(BF16)
        out = pl.ds(pl.multiple_of(piece * 2 * half + at.start, part), part)
        staged[out, :] = (dot_as(hidden, w_ref[...], NN) + bias_ref[...]).astype(BF16)
        to_hbm(piece, i).start()
        return hidden

    for i in range(4):
        moved(i, i % 2).start()
    lengths().start()

    def first(i, carry):
        at = span(i)
        remote(
            rows.at[0, at], rows.at[0, at], sent.at[0, i], landed.at[0, i], core
        ).wait_recv()
        forward(i, 0, 2, across).start()
        forward(i, 0, 1, core).start()
        hidden_ref[at, :] = project(0, i)
        here_ref[at, :] = rows[0, at, :]
        return carry

    lax.fori_loop(0, 4, first, 0)

    def second(i, carry):
        forward(i, 0, 1, core).wait_recv()
        project(1, i)
        forward(i, 0, 2, across).wait_recv()
        forward(i, 2, 3, core).start()
        project(2, i)
        return carry

    lax.fori_loop(0, 4, second, 0)

    def third(i, carry):
        forward(i, 2, 3, core).wait_recv()
        project(3, i)
        return carry

    lax.fori_loop(0, 4, third, 0)
    lengths().wait()
    for i in range(4):
        moved(i, i % 2).wait_send()

    def last(i, carry):
        forward(i, 0, 2, across).wait_send()
        forward(i, 0, 1, core).wait_send()
        forward(i, 2, 3, core).wait_send()
        for piece in range(4):
            to_hbm(piece, i).wait()
        return carry

    lax.fori_loop(0, 4, last, 0)


def start_work(plan, tokens, clip_lengths, gain, shift, weight, bias):
    rows, width = tokens.shape
    lengths = jnp.zeros((8, LANES), jnp.int32)
    lengths = lax.dynamic_update_slice(lengths, clip_lengths, (0, 0))
    vmem, anywhere = pl.BlockSpec(memory_space=pltpu.VMEM), pl.BlockSpec(memory_space=pl.ANY)
    projected, hidden, here, found = pl.pallas_call(
        functools.partial(start_kernel, plan.PLANE, plan.PLACE),
        in_specs=[anywhere] + [vmem] * 5,
        out_specs=[anywhere, vmem, vmem, vmem],
        out_shape=[
            jax.ShapeDtypeStruct((4 * rows, 3 * width), BF16),
            jax.ShapeDtypeStruct((rows, width), BF16),
            jax.ShapeDtypeStruct((rows, width), BF16),
            jax.ShapeDtypeStruct((8, LANES), jnp.int32),
        ],
        scratch_shapes=[
            pltpu.VMEM((4, rows, width), BF16),
            pltpu.VMEM((4 * rows, 3 * width), BF16),
            pltpu.SemaphoreType.DMA((5, 4)),
            pltpu.SemaphoreType.DMA((5, 4)),
            pltpu.SemaphoreType.DMA((4, 4)),
        ],
        compiler_params=pltpu.CompilerParams(
            vmem_limit_bytes=VMEM_BYTES, collective_id=0, has_side_effects=True
        ),
        cost_estimate=pl.CostEstimate(
            flops=24 * rows * width * width, bytes_accessed=32 * rows * width, transcendentals=0
        ),
        name="start_work",
    )(tokens, lengths, gain.reshape(1, -1), shift.reshape(1, -1), weight, bias.reshape(1, -1))
    return projected, hidden, here, found[:1, : clip_lengths.shape[1]]


def added(one, other):
    return (one.astype(F32) + other.astype(F32)).astype(BF16)


class PlanePlan:
    PLANE = (0, 3, 1, 2)
    PLACE = ((1, 3, 2, 0), (2, 0, 1, 3))
    pieces = 4
    ways = (PLANE, PLACE)

    def __init__(self):
        self.there = []
        for place in self.PLACE:
            self.there.append(
                [
                    ((y * 4 + j) * 4 + z, (y * 4 + place[z]) * 4 + self.PLANE[j])
                    for y in range(2)
                    for j in range(4)
                    for z in range(4)
                ]
            )
        self.back = [[(b, a) for a, b in pairs] for pairs in self.there]

    def move(self, rows, pairs):
        half = rows.shape[0] // 2
        return jnp.concatenate(
            [
                lax.ppermute(rows[:half], ("dp", "seq"), pairs[0]),
                lax.ppermute(rows[half:], ("dp", "seq"), pairs[1]),
            ]
        )

    def to_work(self, rows):
        return self.move(rows, self.there)

    def start(self, tokens, clip_lengths, gain, shift, weight, bias):
        projected, hidden, here, lengths = start_work(
            self, tokens, clip_lengths, gain, shift, weight, bias
        )
        return projected, projected, hidden, here, lengths

    def to_home(self, rows):
        return self.move(rows, self.back)

    def gather(self, own):
        core = lax.ppermute(own, "dp", [(i, i ^ 1) for i in range(8)])
        across = lax.ppermute(own, "dp", [(i, i ^ 2) for i in range(8)])
        corner = lax.ppermute(across, "dp", [(i, i ^ 1) for i in range(8)])
        return [own, core, across, corner]

    def positions(self, rows):
        j = lax.axis_index("dp") % 4
        half = rows // 2
        sources = jnp.asarray([[place.index(p) for place in self.PLACE] for p in range(4)], jnp.int32)
        found = []
        for piece in range(4):
            shards = sources[j ^ piece]
            for part in range(2):
                start = shards[part] * rows + part * half
                found.append(start + jnp.arange(half, dtype=jnp.int32))
        return jnp.concatenate(found)

    def own(self, gathered):
        return gathered[: gathered.shape[0] // 4]

    def weight(self, left, right):
        me = lax.axis_index("dp").astype(jnp.int32).reshape(1)
        if left.shape[1] // 8 % LANES == 0:
            return grad_weight_tall(left, right, me, 8)
        tile = 384 if right.shape[1] % 384 == 0 else right.shape[1]
        return grad_weight_wide(left, right, me, 8, tile)

    def swap(self, value, bit):
        return lax.ppermute(value, "dp", [(i, i ^ bit) for i in range(8)])

    def reduce(self, halves):
        keep, send = halves
        total = added(keep, self.swap(send, 1))
        middle = total.shape[2] // 2
        first, second = total[:, :, :middle], total[:, :, middle:]
        first = added(first[0::2], self.swap(first[1::2], 2))
        second = added(second[0:2], self.swap(second[2:4], 4))
        first = added(first[0], self.swap(first[1], 4))
        second = added(second[0], self.swap(second[1], 2))
        total = jnp.concatenate([first, second], 1)
        total = added(total, lax.ppermute(total, "seq", [(0, 1), (3, 2)]))
        total = added(total, lax.ppermute(total, "seq", [(1, 2), (2, 1)]))
        ends = lax.ppermute(total, "seq", [(1, 0), (2, 3)])
        z = lax.axis_index("seq")
        return jnp.where((z == 1) | (z == 2), total, ends).astype(F32)

    def reduce_vectors(self, vectors):
        packed = jnp.concatenate(vectors)
        for bit in (1, 2, 4):
            packed = packed + self.swap(packed, bit)
        for bit in (1, 2):
            packed = packed + lax.ppermute(packed, "seq", [(i, i ^ bit) for i in range(4)])
        results, start = [], 0
        for vector in vectors:
            part = vector.shape[0] // 8
            results.append(
                lax.dynamic_slice(packed, (start + lax.axis_index("dp") * part,), (part,))
            )
            start += vector.shape[0]
        return results


class PlainPlan:
    ways = None

    def __init__(self, pieces):
        self.pieces = pieces

    def to_work(self, rows):
        return rows

    def to_home(self, rows):
        return rows

    def start(self, tokens, clip_lengths, gain, shift, weight, bias):
        hidden = layer_norm(tokens.astype(F32), gain, shift)[0].astype(BF16)
        own = (matmul(hidden, weight) + bias).astype(BF16)
        projected = lax.all_gather(own, "seq", axis=0, tiled=True)
        return projected, own, hidden, tokens, clip_lengths

    def gather(self, own):
        gathered = lax.all_gather(own, "seq", axis=0, tiled=False)
        return [gathered[i] for i in range(self.pieces)]

    def positions(self, rows):
        return jnp.arange(rows * self.pieces, dtype=jnp.int32)

    def own(self, gathered):
        rows = gathered.shape[0] // self.pieces
        return lax.dynamic_slice_in_dim(gathered, lax.axis_index("seq") * rows, rows, 0)

    def weight(self, left, right):
        return inner_rows(left, right)

    def reduce(self, total):
        return lax.psum(lax.psum_scatter(total, "dp", scatter_dimension=0, tiled=True), "seq")

    def reduce_vectors(self, vectors):
        return [self.reduce(vector) for vector in vectors]


def gelu_parts(pre_act):
    inside = 0.5 * (1.0 + lax.erf(pre_act * math.sqrt(0.5)))
    slope = inside + pre_act * jnp.exp(-0.5 * pre_act * pre_act) * (1.0 / math.sqrt(2.0 * math.pi))
    return pre_act * inside, slope


def body(
    plan,
    tokens,
    clip_lengths,
    ln1_gain,
    ln1_shift,
    w_qkv,
    bias_query,
    bias_value,
    w_out,
    bias_out,
    ln2_gain,
    ln2_shift,
    w_up,
    bias_up,
    w_down,
    bias_down,
    cotangent,
):
    rows, width = tokens.shape
    bias = jnp.concatenate([bias_query, jnp.zeros_like(bias_query), bias_value])
    projected, own, hidden1, here, lengths = plan.start(
        tokens, clip_lengths, ln1_gain, ln1_shift, w_qkv, bias
    )

    clip_ends = jnp.cumsum(lengths.reshape(-1))
    position = plan.positions(rows)
    segment = jnp.sum((position[:, None] >= clip_ends[None, :]).astype(jnp.int32), 1)
    lane = jnp.arange(LANES, dtype=jnp.int32)[None, :]
    same = lane == segment[:, None]
    mark_k = same.astype(BF16)
    mark_q = jnp.where(same | (lane >= clip_ends.shape[0]), 0.0, masked_score).astype(BF16)

    attended, chances, log_totals, grad_out = attend(
        plan, own, projected, plan.own(mark_q), mark_k, cotangent
    )
    log_totals = plan.gather(log_totals)

    inputs32 = here.astype(F32)
    middle = inputs32 + matmul(attended, w_out) + bias_out
    normed2_out, normed2, inverse2 = layer_norm(middle, ln2_gain, ln2_shift)
    hidden2 = normed2_out.astype(BF16)
    upper = matmul(hidden2, w_up) + bias_up
    activated, slope = gelu_parts(upper)
    activated = activated.astype(BF16)
    grad_upper = (inner_cols(grad_out, w_down) * slope).astype(BF16)
    grad_hidden2 = inner_cols(grad_upper, w_up)
    grad_norm2, grad_ln2_gain, grad_ln2_shift = norm_back(grad_hidden2, normed2, inverse2, ln2_gain)
    grad_middle = grad_out.astype(F32) + grad_norm2
    grad_branch = grad_middle.astype(BF16)
    grad_attended = inner_cols(grad_branch, w_out).astype(BF16)
    grads = plan.gather(grad_attended)

    block_out = (middle + matmul(activated, w_down) + bias_down).astype(BF16)
    block_out = plan.to_home(block_out)
    grad_w_down = plan.reduce(plan.weight(activated, grad_out))
    grad_w_up = plan.reduce(plan.weight(hidden2, grad_upper))
    grad_w_out = plan.reduce(plan.weight(attended, grad_branch))
    grad_bias_down = jnp.sum(grad_out.astype(F32), 0)
    grad_bias_up = jnp.sum(grad_upper.astype(F32), 0)
    grad_bias_out = jnp.sum(grad_branch.astype(F32), 0)
    grad_bias_down, grad_bias_up, grad_bias_out, grad_ln2_gain, grad_ln2_shift = (
        plan.reduce_vectors(
            [grad_bias_down, grad_bias_up, grad_bias_out, grad_ln2_gain, grad_ln2_shift]
        )
    )

    dq, deltas = grad_query(chances, grad_attended, attended, projected)
    deltas = plan.gather(deltas)
    dk, dv = grad_key_value(
        own, projected, grads, log_totals, deltas, plan.own(mark_k), mark_q
    )
    grad_projected = jnp.concatenate([dq, dk, dv], 1)
    grad_w_qkv = plan.reduce(plan.weight(hidden1, grad_projected))
    grad_bias_query = jnp.sum(dq.astype(F32), 0)
    grad_bias_value = jnp.sum(dv.astype(F32), 0)
    grad_hidden1 = inner_cols(grad_projected, w_qkv)
    _, normed1, inverse1 = layer_norm(inputs32, ln1_gain, ln1_shift)
    grad_norm1, grad_ln1_gain, grad_ln1_shift = norm_back(grad_hidden1, normed1, inverse1, ln1_gain)
    grad_tokens = plan.to_home((grad_middle + grad_norm1).astype(BF16))
    grad_bias_query, grad_bias_value, grad_ln1_gain, grad_ln1_shift = plan.reduce_vectors(
        [grad_bias_query, grad_bias_value, grad_ln1_gain, grad_ln1_shift]
    )
    return (
        block_out,
        grad_tokens,
        grad_ln1_gain,
        grad_ln1_shift,
        grad_w_qkv,
        grad_bias_query,
        grad_bias_value,
        grad_w_out,
        grad_bias_out,
        grad_ln2_gain,
        grad_ln2_shift,
        grad_w_up,
        grad_bias_up,
        grad_w_down,
        grad_bias_down,
    )


def solution(mesh):
    sizes = dict(mesh.shape)
    plan = PlanePlan() if sizes == {"dp": 8, "seq": 4} else PlainPlan(sizes["seq"])
    rows = P(("dp", "seq"), None)
    return jax.shard_map(
        functools.partial(body, plan),
        mesh=mesh,
        in_specs=(rows, P("dp", None)) + (P(),) * 13 + (rows,),
        out_specs=(
            rows,
            rows,
            P("dp"),
            P("dp"),
            P("dp", None),
            P("dp"),
            P("dp"),
            P("dp", None),
            P("dp"),
            P("dp"),
            P("dp"),
            P("dp", None),
            P("dp"),
            P("dp", None),
            P("dp"),
        ),
        check_vma=False,
    )
```

profile of v0, /device:TPU:0, one launch (start us, length us, event | category | flops | bytes accessed | tf_op | source)
XLA Modules:
  0.0 406.1 jit_solution(16203822696203865653)
XLA Ops:
  13.1 48.7 %start_work.1 = (bf16[2048,2304]{1,0:T(8,128)(2,1)}, bf16[512,768]{1,0:T(8,128)(2,1)}, bf16[512,768]{1,0:T(8,128)(2,1)}, s32[8,128]{1,0:T(8,128)}) custom-call(bf16[512,768]{1,0:T(8,128)(2,1)} %tokens_ref.1, s32[8,128]{1,0:T(8,128)} %dynamic_update_slice.3.lengths_ref, f32[1,768]{1,0:T(1,128)} %reshape.179.gain_ref, f32[1,768]{1,0:T(1,128)} %reshape.180.shift_ref, ...), custom_call_target="tpu_custom_call" | custom-call | flops 7247757312 | bytes 12582912 | tf_op jit(solution)/shard_map/start_work/pallas_call | solution.py:544
  65.0 36.2 %attend.1 = (bf16[512,768]{1,0:T(8,128)(2,1)}, bf16[12,512,2048]{2,1,0:T(8,128)(2,1)}, f32[16,512]{1,0:T(8,128)}, bf16[512,768]{1,0:T(8,128)(2,1)}) custom-call(bf16[2048,2304]{1,0:T(8,128)(2,1)} %get-tuple-element.34.q_ref.k_ref.v_ref, bf16[2048,2304]{1,0:T(8,128)(2,1)} %get-tuple-element.34.q_ref.k_ref.v_ref, ...), custom_call_target="tpu_custom_call" | custom-call | flops 19327352832 | bytes 25165824 | tf_op jit(solution)/shard_map/attend/pallas_call | solution.py:272
  101.3 2.0 fusion.37
  104.4 3.7 multiply_convert_fusion
  108.2 4.9 %convert_reduce_fusion = (f32[3072]{0:T(1024)S(1)}, bf16[512,3072]{1,0:T(8,128)(2,1)S(1)}) fusion(f32[512,3072]{1,0:T(8,128)S(1)} %get-tuple-element.90, f32[3072]{0:T(1024)S(1)} %copy-done.28, bf16[512,768]{1,0:T(8,128)(2,1)S(1)} %copy-done.4, bf16[3072,768]{1,0:T(8,128)(2,1)S(1)} %bitcast.86), kind=kOutput, calls=%fused_computation.7 | convolution fusion | flops 2436363264 | bytes 14966784 | tf_op jit(solution)/shard_map/dot_general | solution.py:25
  113.1 3.1 multiply_reduce_fusion
  116.2 1.9 convert_reduce_fusion.3
  120.1 2.6 add_convert_fusion.3
  122.8 2.6 collective-permute-start
  125.5 3.9 grad_weight_wide.4
  130.1 10.0 %grad_weight_wide.5 = (bf16[4,96,3072]{2,1,0:T(8,128)(2,1)}, bf16[4,96,3072]{2,1,0:T(8,128)(2,1)}) custom-call(s32[1]{0:T(128)} %bitcast.10.index_ref, bf16[512,768]{1,0:T(8,128)(2,1)} %copy-done.12, bf16[512,3072]{1,0:T(8,128)(2,1)} %copy-done.31), custom_call_target="tpu_custom_call" | custom-call | flops 2415919104 | bytes 4718592 | tf_op jit(solution)/shard_map/grad_weight_wide/pallas_call | solution.py:375
  140.0 20.6 %grad_query.1 = (bf16[512,768]{1,0:T(8,128)(2,1)}, f32[16,512]{1,0:T(8,128)}) custom-call(bf16[12,512,2048]{2,1,0:T(8,128)(2,1)} %get-tuple-element.38.chance_ref, bf16[512,768]{1,0:T(8,128)(2,1)} %convolution_convert_fusion.grad_ref.refs_0_, bf16[512,768]{1,0:T(8,128)(2,1)} %get-tuple-element.36.out_ref.left_ref, ...), custom_call_target="tpu_custom_call" | custom-call | flops 12884901888 | bytes 25165824 | tf_op jit(solution)/shard_map/grad_query/pallas_call | solution.py:308
  162.1 2.8 collective-permute-done.35
  170.4 2.6 collective-permute-done.37
  175.1 4.6 %collective-permute-done.27 = bf16[2,96,384]{2,1,0:T(8,128)(2,1)S(1)} collective-permute-done((bf16[2,96,384]{2,1,0:T(8,128)(2,1)S(1)}, bf16[2,96,384]{2,1,0:T(8,128)(2,1)S(1)}, u32[]{:S(2)}, u32[]{:S(2)}) %collective-permute-start.27) | collective-permute-done | bytes 147488 | tf_op jit(solution)/shard_map/ppermute | solution.py:645
  180.3 3.8 collective-permute-done.30
  185.9 2.5 collective-permute-done.28
  188.5 2.4 collective-permute-start.31
  190.9 5.0 %grad_weight_tall.3 = bf16[4,384,768]{2,1,0:T(8,128)(2,1)} custom-call(s32[1]{0:T(128)} %bitcast.10.index_ref, bf16[512,3072]{1,0:T(8,128)(2,1)} %copy-done.2, bf16[512,768]{1,0:T(8,128)(2,1)} %get-tuple-element.37.right_ref), custom_call_target="tpu_custom_call" | custom-call | flops 1207959552 | bytes 2359296 | tf_op jit(solution)/shard_map/grad_weight_tall/pallas_call | solution.py:406
  196.7 5.0 %grad_weight_tall.2 = bf16[4,384,768]{2,1,0:T(8,128)(2,1)} custom-call(s32[1]{0:T(128)} %bitcast.10.index_ref, bf16[512,3072]{1,0:T(8,128)(2,1)} %copy-done.2, bf16[512,768]{1,0:T(8,128)(2,1)} %get-tuple-element.37.right_ref), custom_call_target="tpu_custom_call" | custom-call | flops 1207959552 | bytes 2359296 | tf_op jit(solution)/shard_map/grad_weight_tall/pallas_call | solution.py:406
  203.2 3.6 collective-permute-start.6
  206.9 1.9 collective-permute-done.6.refs_6_
  210.8 2.0 collective-permute-start.9
  217.7 33.9 %grad_key_value.1 = (bf16[512,768]{1,0:T(8,128)(2,1)}, bf16[512,768]{1,0:T(8,128)(2,1)}) custom-call(bf16[2048,2304]{1,0:T(8,128)(2,1)} %get-tuple-element.34.q_ref.k_ref.v_ref, bf16[2048,2304]{1,0:T(8,128)(2,1)} %get-tuple-element.34.q_ref.k_ref.v_ref, bf16[2048,2304]{1,0:T(8,128)(2,1)} %get-tuple-element.34.q_ref.k_ref.v_ref, ...), custom_call_target="tpu_custom_call" | custom-call | flops 25769803776 | bytes 12582912 | tf_op jit(solution)/shard_map/grad_key_value/pallas_call | solution.py:332
  253.0 5.2 %fusion.16 = (f32[768]{0:T(1024)S(1)}, f32[512]{0:T(512)S(1)}, f32[512]{0:T(512)S(1)}, f32[768]{0:T(1024)S(1)}, f32[512,768]{1,0:T(8,128)S(1)}) fusion(bf16[512,768]{1,0:T(8,128)(2,1)S(1)} %copy-done.5, f32[512]{0:T(512)S(1)} %add_rsqrt_fusion, f32[512]{0:T(512)S(1)} %broadcast_multiply_fusion.2, f32[768]{0:T(1024)S(1)} %copy-done.18, ...), kind=kOutput, calls=%fused_computation.28 | convolution fusion | flops 1815868928 | bytes 8274944 | tf_op jit(solution)/shard_map/dot_general | solution.py:25
  259.7 2.0 collective-permute-start.14
  267.2 2.9 collective-permute-start.12
  270.0 1.9 collective-permute-start.16
  272.7 6.9 %collective-permute-done.16 = f32[3072]{0:T(1024)S(1)} collective-permute-done((f32[3072]{0:T(1024)S(1)}, f32[3072]{0:T(1024)S(1)}, u32[]{:S(2)}, u32[]{:S(2)}) %collective-permute-start.16) | collective-permute-done | bytes 12320 | tf_op jit(solution)/shard_map/ppermute | solution.py:668
  279.6 2.0 collective-permute-start.17
  281.6 8.1 %grad_weight_wide.3 = (bf16[4,96,2304]{2,1,0:T(8,128)(2,1)}, bf16[4,96,2304]{2,1,0:T(8,128)(2,1)}) custom-call(s32[1]{0:T(128)} %bitcast.10.index_ref, bf16[512,768]{1,0:T(8,128)(2,1)} %get-tuple-element.44.left_ref, bf16[512,2304]{1,0:T(8,128)(2,1)} %copy-done.16), custom_call_target="tpu_custom_call" | custom-call | flops 1811939328 | bytes 3538944 | tf_op jit(solution)/shard_map/grad_weight_wide/pallas_call | solution.py:375
  291.6 2.2 add_convert_fusion
  294.7 2.9 collective-permute-start.48
  300.2 10.1 %collective-permute-done.50 = bf16[2,384,384]{2,1,0:T(8,128)(2,1)S(1)} collective-permute-done((bf16[2,384,384]{2,1,0:T(8,128)(2,1)S(1)}, bf16[2,384,384]{2,1,0:T(8,128)(2,1)S(1)}, u32[]{:S(2)}, u32[]{:S(2)}) %collective-permute-start.50) | collective-permute-done | bytes 589856 | tf_op jit(solution)/shard_map/ppermute | solution.py:645
  310.4 2.6 collective-permute-start.51
  314.1 8.8 %collective-permute-done.42 = bf16[2,96,1536]{2,1,0:T(8,128)(2,1)S(1)} collective-permute-done((bf16[2,96,1536]{2,1,0:T(8,128)(2,1)S(1)}, bf16[2,96,1536]{2,1,0:T(8,128)(2,1)S(1)}, u32[]{:S(2)}, u32[]{:S(2)}) %collective-permute-start.42) | collective-permute-done | bytes 589856 | tf_op jit(solution)/shard_map/ppermute | solution.py:645
  323.1 2.6 collective-permute-start.43
  326.7 3.9 collective-permute-done.51
  330.9 2.2 collective-permute-start.52
  333.2 3.4 collective-permute-done.43
  338.5 2.0 collective-permute-start.44
  342.4 6.6 %collective-permute-done.21 = bf16[2,96,1152]{2,1,0:T(8,128)(2,1)S(1)} collective-permute-done((bf16[2,96,1152]{2,1,0:T(8,128)(2,1)S(1)}, bf16[2,96,1152]{2,1,0:T(8,128)(2,1)S(1)}, u32[]{:S(2)}, u32[]{:S(2)}) %collective-permute-start.21) | collective-permute-done | bytes 442400 | tf_op jit(solution)/shard_map/ppermute | solution.py:645
  354.0 2.3 collective-permute-done.22
  356.3 2.2 collective-permute-done.20
  358.6 2.5 collective-permute-start.23
  363.5 4.2 %collective-permute-done.23 = bf16[96,2304]{1,0:T(8,128)(2,1)S(1)} collective-permute-done((bf16[96,2304]{1,0:T(8,128)(2,1)S(1)}, bf16[96,2304]{1,0:T(8,128)(2,1)S(1)}, u32[]{:S(2)}, u32[]{:S(2)}) %collective-permute-start.23) | collective-permute-done | bytes 442400 | tf_op jit(solution)/shard_map/ppermute | solution.py:657
  371.4 28.2 %collective-permute-done.46 = bf16[96,3072]{1,0:T(8,128)(2,1)S(1)} collective-permute-done((bf16[96,3072]{1,0:T(8,128)(2,1)S(1)}, bf16[96,3072]{1,0:T(8,128)(2,1)S(1)}, u32[]{:S(2)}, u32[]{:S(2)}) %collective-permute-start.46) | collective-permute-done | bytes 589856 | tf_op jit(solution)/shard_map/ppermute | solution.py:659
  401.8 2.9 collective-permute-done.25
  (277 shorter events, 69.8 us)
Async XLA Ops:
  119.8 76.4 %collective-permute-start.3 = (bf16[512,768]{1,0:T(8,128)(2,1)}, bf16[512,768]{1,0:T(8,128)(2,1)}, u32[]{:S(2)}, u32[]{:S(2)}) collective-permute-start(bf16[512,768]{1,0:T(8,128)(2,1)} %convolution_convert_fusion.grad_ref.refs_0_), channel_id=1, source_target_pairs={{0,8},{4,12},{8,0},{12,4},{16,24},{20,28},{24,16},{28,20},{1,9},{5... | collective-permute-start | bytes 2359304 | tf_op jit(solution)/shard_map/ppermute | solution.py:618
  119.8 97.8 %collective-permute-start.2 = (bf16[512,768]{1,0:T(8,128)(2,1)}, bf16[512,768]{1,0:T(8,128)(2,1)}, u32[]{:S(2)}, u32[]{:S(2)}) collective-permute-start(bf16[512,768]{1,0:T(8,128)(2,1)} %convolution_convert_fusion.grad_ref.refs_0_), channel_id=1, source_target_pairs={{0,4},{4,0},{8,12},{12,8},{16,20},{20,16},{24,28},{28,24},{1,5},{5... | collective-permute-start | bytes 2359304 | tf_op jit(solution)/shard_map/ppermute | solution.py:617
  122.8 88.0 %collective-permute-start = (bf16[256,768]{1,0:T(8,128)(2,1)S(1)}, bf16[256,768]{1,0:T(8,128)(2,1)S(1)}, u32[]{:S(2)}, u32[]{:S(2)}) collective-permute-start(bf16[256,768]{1,0:T(8,128)(2,1)S(1)} %get-tuple-element.65), channel_id=1, source_target_pairs={{4,0},{12,1},{8,2},{0,3},{7,4},{15,5},{11,6},{3,7},{5,8},{13,9},{9... | collective-permute-start | bytes 1179656 | tf_op jit(solution)/shard_map/ppermute | solution.py:599
  125.5 35.6 %collective-permute-start.34 = (f32[6144]{0:T(1024)S(1)}, f32[6144]{0:T(1024)S(1)}, u32[]{:S(2)}, u32[]{:S(2)}) collective-permute-start(f32[6144]{0:T(1024)S(1)} %constant_dynamic-update-slice_fusion.13), channel_id=1, source_target_pairs={{0,4},{4,0},{8,12},{12,8},{16,20},{20,16},{24,28},{28,24},{1,5},{5... | collective-permute-start | bytes 73736 | tf_op jit(solution)/shard_map/ppermute | solution.py:645
  129.4 37.0 %collective-permute-start.26 = (bf16[4,96,768]{2,1,0:T(8,128)(2,1)}, bf16[4,96,768]{2,1,0:T(8,128)(2,1)S(1)}, u32[]{:S(2)}, u32[]{:S(2)}) collective-permute-start(bf16[4,96,768]{2,1,0:T(8,128)(2,1)} %get-tuple-element.48), channel_id=1, source_target_pairs={{0,4},{4,0},{8,12},{12,8},{16,20},{20,16},{24,28},{28,24},{1,5},{5... | collective-permute-start | bytes 1769480 | tf_op jit(solution)/shard_map/ppermute | solution.py:645
  161.0 3.9 collective-permute-start.35
  164.9 4.0 collective-permute-start.36
  166.6 7.6 %collective-permute-start.29 = (bf16[2,96,384]{2,1,0:T(8,128)(2,1)S(1)}, bf16[2,96,384]{2,1,0:T(8,128)(2,1)S(1)}, u32[]{:S(2)}, u32[]{:S(2)}) collective-permute-start(bf16[2,96,384]{2,1,0:T(8,128)(2,1)S(1)} %slice.241), channel_id=1, source_target_pairs={{0,16},{4,20},{8,24},{12,28},{16,0},{20,4},{24,8},{28,12},{1,17},{... | collective-permute-start | bytes 442376 | tf_op jit(solution)/shard_map/ppermute | solution.py:645
  169.0 4.1 %collective-permute-start.37 = (f32[6144]{0:T(1024)S(1)}, f32[6144]{0:T(1024)S(1)}, u32[]{:S(2)}, u32[]{:S(2)}) collective-permute-start(f32[6144]{0:T(1024)S(1)} %add.392), channel_id=1, source_target_pairs={{0,1},{1,0},{2,3},{3,2},{4,5},{5,4},{6,7},{7,6},{8,9},{9,8},{10,11... | collective-permute-start | bytes 73736 | tf_op jit(solution)/shard_map/ppermute | solution.py:668
  173.1 22.8 %collective-permute-start.38 = (f32[6144]{0:T(1024)S(1)}, f32[6144]{0:T(1024)S(1)}, u32[]{:S(2)}, u32[]{:S(2)}) collective-permute-start(f32[6144]{0:T(1024)S(1)} %add.393), channel_id=1, source_target_pairs={{0,2},{1,3},{2,0},{3,1},{4,6},{5,7},{6,4},{7,5},{8,10},{9,11},{10,... | collective-permute-start | bytes 73736 | tf_op jit(solution)/shard_map/ppermute | solution.py:668
  174.2 5.5 %collective-permute-start.27 = (bf16[2,96,384]{2,1,0:T(8,128)(2,1)S(1)}, bf16[2,96,384]{2,1,0:T(8,128)(2,1)S(1)}, u32[]{:S(2)}, u32[]{:S(2)}) collective-permute-start(bf16[2,96,384]{2,1,0:T(8,128)(2,1)S(1)} %slice.199), channel_id=1, source_target_pairs={{0,8},{4,12},{8,0},{12,4},{16,24},{20,28},{24,16},{28,20},{1,9},{5... | collective-permute-start | bytes 442376 | tf_op jit(solution)/shard_map/ppermute | solution.py:645
  179.7 4.4 %collective-permute-start.30 = (bf16[96,384]{1,0:T(8,128)(2,1)S(1)}, bf16[96,384]{1,0:T(8,128)(2,1)S(1)}, u32[]{:S(2)}, u32[]{:S(2)}) collective-permute-start(bf16[96,384]{1,0:T(8,128)(2,1)S(1)} %slice_bitcast_fusion.12), channel_id=1, source_target_pairs={{0,8},{4,12},{8,0},{12,4},{16,24},{20,28},{24,16},{28,20},{1,9},{5... | collective-permute-start | bytes 221192 | tf_op jit(solution)/shard_map/ppermute | solution.py:645
  184.1 4.4 %collective-permute-start.28 = (bf16[96,384]{1,0:T(8,128)(2,1)S(1)}, bf16[96,384]{1,0:T(8,128)(2,1)S(1)}, u32[]{:S(2)}, u32[]{:S(2)}) collective-permute-start(bf16[96,384]{1,0:T(8,128)(2,1)S(1)} %slice_bitcast_fusion.14), channel_id=1, source_target_pairs={{0,16},{4,20},{8,24},{12,28},{16,0},{20,4},{24,8},{28,12},{1,17},{... | collective-permute-start | bytes 221192 | tf_op jit(solution)/shard_map/ppermute | solution.py:645
  188.5 14.8 %collective-permute-start.31 = (bf16[96,768]{1,0:T(8,128)(2,1)S(1)}, bf16[96,768]{1,0:T(8,128)(2,1)S(1)}, u32[]{:S(2)}, u32[]{:S(2)}) collective-permute-start(bf16[96,768]{1,0:T(8,128)(2,1)S(1)} %pad_maximum_fusion.5), channel_id=1, source_target_pairs={{0,1},{3,2},{4,5},{7,6},{8,9},{11,10},{12,13},{15,14},{16,17},{19,... | collective-permute-start | bytes 442376 | tf_op jit(solution)/shard_map/ppermute | solution.py:657
  195.9 14.9 %collective-permute-start.1 = (bf16[256,768]{1,0:T(8,128)(2,1)S(1)}, bf16[256,768]{1,0:T(8,128)(2,1)S(1)}, u32[]{:S(2)}, u32[]{:S(2)}) collective-permute-start(bf16[256,768]{1,0:T(8,128)(2,1)S(1)} %get-tuple-element.66), channel_id=1, source_target_pairs={{8,0},{0,1},{4,2},{12,3},{11,4},{3,5},{7,6},{15,7},{9,8},{1,9},{5,... | collective-permute-start | bytes 1179656 | tf_op jit(solution)/shard_map/ppermute | solution.py:600
  196.2 21.4 %collective-permute-start.4 = (bf16[512,768]{1,0:T(8,128)(2,1)}, bf16[512,768]{1,0:T(8,128)(2,1)}, u32[]{:S(2)}, u32[]{:S(2)}) collective-permute-start(bf16[512,768]{1,0:T(8,128)(2,1)} %collective-permute-done.3.refs_2_), channel_id=1, source_target_pairs={{0,4},{4,0},{8,12},{12,8},{16,20},{20,16},{24,28},{28,24},{1,5},{5... | collective-permute-start | bytes 2359304 | tf_op jit(solution)/shard_map/ppermute | solution.py:619
  203.2 5.6 %collective-permute-start.6 = (f32[16,512]{1,0:T(8,128)S(1)}, f32[16,512]{1,0:T(8,128)S(1)}, u32[]{:S(2)}, u32[]{:S(2)}) collective-permute-start(f32[16,512]{1,0:T(8,128)S(1)} %copy-done.20), channel_id=1, source_target_pairs={{0,8},{4,12},{8,0},{12,4},{16,24},{20,28},{24,16},{28,20},{1,9},{5... | collective-permute-start | bytes 98312 | tf_op jit(solution)/shard_map/ppermute | solution.py:618
  208.8 5.9 %collective-permute-start.32 = (bf16[96,768]{1,0:T(8,128)(2,1)S(1)}, bf16[96,768]{1,0:T(8,128)(2,1)S(1)}, u32[]{:S(2)}, u32[]{:S(2)}) collective-permute-start(bf16[96,768]{1,0:T(8,128)(2,1)S(1)} %add_convert_fusion.19), channel_id=1, source_target_pairs={{1,2},{2,1},{5,6},{6,5},{9,10},{10,9},{13,14},{14,13},{17,18},{18,... | collective-permute-start | bytes 442376 | tf_op jit(solution)/shard_map/ppermute | solution.py:658
  210.8 4.0 collective-permute-start.9
  215.3 76.2 %collective-permute-start.47 = (bf16[4,384,768]{2,1,0:T(8,128)(2,1)}, bf16[4,384,768]{2,1,0:T(8,128)(2,1)}, u32[]{:S(2)}, u32[]{:S(2)}) collective-permute-start(bf16[4,384,768]{2,1,0:T(8,128)(2,1)} %grad_weight_tall.3), channel_id=1, source_target_pairs={{0,4},{4,0},{8,12},{12,8},{16,20},{20,16},{24,28},{28,24},{1,5},{5... | collective-permute-start | bytes 7077896 | tf_op jit(solution)/shard_map/ppermute | solution.py:645
  216.0 81.6 %collective-permute-start.39 = (bf16[4,96,3072]{2,1,0:T(8,128)(2,1)}, bf16[4,96,3072]{2,1,0:T(8,128)(2,1)S(1)}, u32[]{:S(2)}, u32[]{:S(2)}) collective-permute-start(bf16[4,96,3072]{2,1,0:T(8,128)(2,1)} %get-tuple-element.50), channel_id=1, source_target_pairs={{0,4},{4,0},{8,12},{12,8},{16,20},{20,16},{24,28},{28,24},{1,5},{5... | collective-permute-start | bytes 7077896 | tf_op jit(solution)/shard_map/ppermute | solution.py:645
  216.2 53.9 %collective-permute-start.33 = (bf16[96,768]{1,0:T(8,128)(2,1)S(1)}, bf16[96,768]{1,0:T(8,128)(2,1)S(1)}, u32[]{:S(2)}, u32[]{:S(2)}) collective-permute-start(bf16[96,768]{1,0:T(8,128)(2,1)S(1)} %add_convert_fusion.18), channel_id=1, source_target_pairs={{1,0},{2,3},{5,4},{6,7},{9,8},{10,11},{13,12},{14,15},{17,16},{18,... | collective-permute-start | bytes 442376 | tf_op jit(solution)/shard_map/ppermute | solution.py:659
  259.7 3.8 collective-permute-start.14
  265.0 25.6 %collective-permute-start.11 = (bf16[256,768]{1,0:T(8,128)(2,1)S(1)}, bf16[256,768]{1,0:T(8,128)(2,1)S(1)}, u32[]{:S(2)}, u32[]{:S(2)}) collective-permute-start(bf16[256,768]{1,0:T(8,128)(2,1)S(1)} %get-tuple-element.63), channel_id=1, source_target_pairs={{4,0},{12,1},{8,2},{0,3},{7,4},{15,5},{11,6},{3,7},{5,8},{13,9},{9... | collective-permute-start | bytes 1179656 | tf_op jit(solution)/shard_map/ppermute | solution.py:599
  267.2 23.5 %collective-permute-start.12 = (bf16[256,768]{1,0:T(8,128)(2,1)S(1)}, bf16[256,768]{1,0:T(8,128)(2,1)S(1)}, u32[]{:S(2)}, u32[]{:S(2)}) collective-permute-start(bf16[256,768]{1,0:T(8,128)(2,1)S(1)} %get-tuple-element.64), channel_id=1, source_target_pairs={{8,0},{0,1},{4,2},{12,3},{11,4},{3,5},{7,6},{15,7},{9,8},{1,9},{5,... | collective-permute-start | bytes 1179656 | tf_op jit(solution)/shard_map/ppermute | solution.py:600
  270.0 9.6 %collective-permute-start.16 = (f32[3072]{0:T(1024)S(1)}, f32[3072]{0:T(1024)S(1)}, u32[]{:S(2)}, u32[]{:S(2)}) collective-permute-start(f32[3072]{0:T(1024)S(1)} %add.368), channel_id=1, source_target_pairs={{0,1},{1,0},{2,3},{3,2},{4,5},{5,4},{6,7},{7,6},{8,9},{9,8},{10,11... | collective-permute-start | bytes 36872 | tf_op jit(solution)/shard_map/ppermute | solution.py:668
  279.6 10.1 %collective-permute-start.17 = (f32[3072]{0:T(1024)S(1)}, f32[3072]{0:T(1024)S(1)}, u32[]{:S(2)}, u32[]{:S(2)}) collective-permute-start(f32[3072]{0:T(1024)S(1)} %add.369), channel_id=1, source_target_pairs={{0,2},{1,3},{2,0},{3,1},{4,6},{5,7},{6,4},{7,5},{8,10},{9,11},{10,... | collective-permute-start | bytes 36872 | tf_op jit(solution)/shard_map/ppermute | solution.py:668
  289.7 46.9 %collective-permute-start.18 = (bf16[4,96,2304]{2,1,0:T(8,128)(2,1)}, bf16[4,96,2304]{2,1,0:T(8,128)(2,1)S(1)}, u32[]{:S(2)}, u32[]{:S(2)}) collective-permute-start(bf16[4,96,2304]{2,1,0:T(8,128)(2,1)} %get-tuple-element.46), channel_id=1, source_target_pairs={{0,4},{4,0},{8,12},{12,8},{16,20},{20,16},{24,28},{28,24},{1,5},{5... | collective-permute-start | bytes 5308424 | tf_op jit(solution)/shard_map/ppermute | solution.py:645
  294.0 16.2 %collective-permute-start.50 = (bf16[2,384,384]{2,1,0:T(8,128)(2,1)S(1)}, bf16[2,384,384]{2,1,0:T(8,128)(2,1)S(1)}, u32[]{:S(2)}, u32[]{:S(2)}) collective-permute-start(bf16[2,384,384]{2,1,0:T(8,128)(2,1)S(1)} %slice.255), channel_id=1, source_target_pairs={{0,16},{4,20},{8,24},{12,28},{16,0},{20,4},{24,8},{28,12},{1,17},{... | collective-permute-start | bytes 1769480 | tf_op jit(solution)/shard_map/ppermute | solution.py:645
  294.7 18.3 %collective-permute-start.48 = (bf16[2,384,384]{2,1,0:T(8,128)(2,1)S(1)}, bf16[2,384,384]{2,1,0:T(8,128)(2,1)S(1)}, u32[]{:S(2)}, u32[]{:S(2)}) collective-permute-start(bf16[2,384,384]{2,1,0:T(8,128)(2,1)S(1)} %slice.217), channel_id=1, source_target_pairs={{0,8},{4,12},{8,0},{12,4},{16,24},{20,28},{24,16},{28,20},{1,9},{5... | collective-permute-start | bytes 1769480 | tf_op jit(solution)/shard_map/ppermute | solution.py:645
  298.7 24.2 %collective-permute-start.42 = (bf16[2,96,1536]{2,1,0:T(8,128)(2,1)S(1)}, bf16[2,96,1536]{2,1,0:T(8,128)(2,1)S(1)}, u32[]{:S(2)}, u32[]{:S(2)}) collective-permute-start(bf16[2,96,1536]{2,1,0:T(8,128)(2,1)S(1)} %slice.248), channel_id=1, source_target_pairs={{0,16},{4,20},{8,24},{12,28},{16,0},{20,4},{24,8},{28,12},{1,17},{... | collective-permute-start | bytes 1769480 | tf_op jit(solution)/shard_map/ppermute | solution.py:645
  299.9 25.7 %collective-permute-start.40 = (bf16[2,96,1536]{2,1,0:T(8,128)(2,1)S(1)}, bf16[2,96,1536]{2,1,0:T(8,128)(2,1)S(1)}, u32[]{:S(2)}, u32[]{:S(2)}) collective-permute-start(bf16[2,96,1536]{2,1,0:T(8,128)(2,1)S(1)} %slice.208), channel_id=1, source_target_pairs={{0,8},{4,12},{8,0},{12,4},{16,24},{20,28},{24,16},{28,20},{1,9},{5... | collective-permute-start | bytes 1769480 | tf_op jit(solution)/shard_map/ppermute | solution.py:645
  310.4 20.2 %collective-permute-start.51 = (bf16[384,384]{1,0:T(8,128)(2,1)S(1)}, bf16[384,384]{1,0:T(8,128)(2,1)S(1)}, u32[]{:S(2)}, u32[]{:S(2)}) collective-permute-start(bf16[384,384]{1,0:T(8,128)(2,1)S(1)} %slice_bitcast_fusion), channel_id=1, source_target_pairs={{0,8},{4,12},{8,0},{12,4},{16,24},{20,28},{24,16},{28,20},{1,9},{5... | collective-permute-start | bytes 884744 | tf_op jit(solution)/shard_map/ppermute | solution.py:645
  313.2 17.6 %collective-permute-start.49 = (bf16[384,384]{1,0:T(8,128)(2,1)S(1)}, bf16[384,384]{1,0:T(8,128)(2,1)S(1)}, u32[]{:S(2)}, u32[]{:S(2)}) collective-permute-start(bf16[384,384]{1,0:T(8,128)(2,1)S(1)} %slice_bitcast_fusion.2), channel_id=1, source_target_pairs={{0,16},{4,20},{8,24},{12,28},{16,0},{20,4},{24,8},{28,12},{1,17},{... | collective-permute-start | bytes 884744 | tf_op jit(solution)/shard_map/ppermute | solution.py:645
  323.1 13.5 %collective-permute-start.43 = (bf16[96,1536]{1,0:T(8,128)(2,1)S(1)}, bf16[96,1536]{1,0:T(8,128)(2,1)S(1)}, u32[]{:S(2)}, u32[]{:S(2)}) collective-permute-start(bf16[96,1536]{1,0:T(8,128)(2,1)S(1)} %slice_bitcast_fusion.4), channel_id=1, source_target_pairs={{0,8},{4,12},{8,0},{12,4},{16,24},{20,28},{24,16},{28,20},{1,9},{5... | collective-permute-start | bytes 884744 | tf_op jit(solution)/shard_map/ppermute | solution.py:645
  325.8 12.6 %collective-permute-start.41 = (bf16[96,1536]{1,0:T(8,128)(2,1)S(1)}, bf16[96,1536]{1,0:T(8,128)(2,1)S(1)}, u32[]{:S(2)}, u32[]{:S(2)}) collective-permute-start(bf16[96,1536]{1,0:T(8,128)(2,1)S(1)} %slice_bitcast_fusion.6), channel_id=1, source_target_pairs={{0,16},{4,20},{8,24},{12,28},{16,0},{20,4},{24,8},{28,12},{1,17},{... | collective-permute-start | bytes 884744 | tf_op jit(solution)/shard_map/ppermute | solution.py:645
  330.9 22.2 %collective-permute-start.52 = (bf16[384,768]{1,0:T(8,128)(2,1)S(1)}, bf16[384,768]{1,0:T(8,128)(2,1)S(1)}, u32[]{:S(2)}, u32[]{:S(2)}) collective-permute-start(bf16[384,768]{1,0:T(8,128)(2,1)S(1)} %pad_maximum_fusion.3), channel_id=1, source_target_pairs={{0,1},{3,2},{4,5},{7,6},{8,9},{11,10},{12,13},{15,14},{16,17},{19,... | collective-permute-start | bytes 1769480 | tf_op jit(solution)/shard_map/ppermute | solution.py:657
  337.1 11.8 %collective-permute-start.21 = (bf16[2,96,1152]{2,1,0:T(8,128)(2,1)S(1)}, bf16[2,96,1152]{2,1,0:T(8,128)(2,1)S(1)}, u32[]{:S(2)}, u32[]{:S(2)}) collective-permute-start(bf16[2,96,1152]{2,1,0:T(8,128)(2,1)S(1)} %slice.234), channel_id=1, source_target_pairs={{0,16},{4,20},{8,24},{12,28},{16,0},{20,4},{24,8},{28,12},{1,17},{... | collective-permute-start | bytes 1327112 | tf_op jit(solution)/shard_map/ppermute | solution.py:645
  338.5 22.6 %collective-permute-start.44 = (bf16[96,3072]{1,0:T(8,128)(2,1)S(1)}, bf16[96,3072]{1,0:T(8,128)(2,1)S(1)}, u32[]{:S(2)}, u32[]{:S(2)}) collective-permute-start(bf16[96,3072]{1,0:T(8,128)(2,1)S(1)} %pad_maximum_fusion.2), channel_id=1, source_target_pairs={{0,1},{3,2},{4,5},{7,6},{8,9},{11,10},{12,13},{15,14},{16,17},{19,... | collective-permute-start | bytes 1769480 | tf_op jit(solution)/shard_map/ppermute | solution.py:657
  340.6 11.8 %collective-permute-start.19 = (bf16[2,96,1152]{2,1,0:T(8,128)(2,1)S(1)}, bf16[2,96,1152]{2,1,0:T(8,128)(2,1)S(1)}, u32[]{:S(2)}, u32[]{:S(2)}) collective-permute-start(bf16[2,96,1152]{2,1,0:T(8,128)(2,1)S(1)} %slice.190), channel_id=1, source_target_pairs={{0,8},{4,12},{8,0},{12,4},{16,24},{20,28},{24,16},{28,20},{1,9},{5... | collective-permute-start | bytes 1327112 | tf_op jit(solution)/shard_map/ppermute | solution.py:645
  349.1 7.1 %collective-permute-start.22 = (bf16[96,1152]{1,0:T(8,128)(2,1)S(1)}, bf16[96,1152]{1,0:T(8,128)(2,1)S(1)}, u32[]{:S(2)}, u32[]{:S(2)}) collective-permute-start(bf16[96,1152]{1,0:T(8,128)(2,1)S(1)} %slice_bitcast_fusion.8), channel_id=1, source_target_pairs={{0,8},{4,12},{8,0},{12,4},{16,24},{20,28},{24,16},{28,20},{1,9},{5... | collective-permute-start | bytes 663560 | tf_op jit(solution)/shard_map/ppermute | solution.py:645
  352.5 6.0 %collective-permute-start.20 = (bf16[96,1152]{1,0:T(8,128)(2,1)S(1)}, bf16[96,1152]{1,0:T(8,128)(2,1)S(1)}, u32[]{:S(2)}, u32[]{:S(2)}) collective-permute-start(bf16[96,1152]{1,0:T(8,128)(2,1)S(1)} %slice_bitcast_fusion.10), channel_id=1, source_target_pairs={{0,16},{4,20},{8,24},{12,28},{16,0},{20,4},{24,8},{28,12},{1,17},{... | collective-permute-start | bytes 663560 | tf_op jit(solution)/shard_map/ppermute | solution.py:645
  353.3 8.7 %collective-permute-start.53 = (bf16[384,768]{1,0:T(8,128)(2,1)S(1)}, bf16[384,768]{1,0:T(8,128)(2,1)S(1)}, u32[]{:S(2)}, u32[]{:S(2)}) collective-permute-start(bf16[384,768]{1,0:T(8,128)(2,1)S(1)} %add_convert_fusion.6), channel_id=1, source_target_pairs={{1,2},{2,1},{5,6},{6,5},{9,10},{10,9},{13,14},{14,13},{17,18},{18,... | collective-permute-start | bytes 1769480 | tf_op jit(solution)/shard_map/ppermute | solution.py:658
  358.6 9.1 %collective-permute-start.23 = (bf16[96,2304]{1,0:T(8,128)(2,1)S(1)}, bf16[96,2304]{1,0:T(8,128)(2,1)S(1)}, u32[]{:S(2)}, u32[]{:S(2)}) collective-permute-start(bf16[96,2304]{1,0:T(8,128)(2,1)S(1)} %pad_maximum_fusion.4), channel_id=1, source_target_pairs={{0,1},{3,2},{4,5},{7,6},{8,9},{11,10},{12,13},{15,14},{16,17},{19,... | collective-permute-start | bytes 1327112 | tf_op jit(solution)/shard_map/ppermute | solution.py:657
  361.3 7.2 %collective-permute-start.45 = (bf16[96,3072]{1,0:T(8,128)(2,1)S(1)}, bf16[96,3072]{1,0:T(8,128)(2,1)S(1)}, u32[]{:S(2)}, u32[]{:S(2)}) collective-permute-start(bf16[96,3072]{1,0:T(8,128)(2,1)S(1)} %add_convert_fusion.10), channel_id=1, source_target_pairs={{1,2},{2,1},{5,6},{6,5},{9,10},{10,9},{13,14},{14,13},{17,18},{18,... | collective-permute-start | bytes 1769480 | tf_op jit(solution)/shard_map/ppermute | solution.py:658
  362.2 38.5 %collective-permute-start.54 = (bf16[384,768]{1,0:T(8,128)(2,1)S(1)}, bf16[384,768]{1,0:T(8,128)(2,1)S(1)}, u32[]{:S(2)}, u32[]{:S(2)}) collective-permute-start(bf16[384,768]{1,0:T(8,128)(2,1)S(1)} %add_convert_fusion.5), channel_id=1, source_target_pairs={{1,0},{2,3},{5,4},{6,7},{9,8},{10,11},{13,12},{14,15},{17,16},{18,... | collective-permute-start | bytes 1769480 | tf_op jit(solution)/shard_map/ppermute | solution.py:659
  368.7 30.9 %collective-permute-start.46 = (bf16[96,3072]{1,0:T(8,128)(2,1)S(1)}, bf16[96,3072]{1,0:T(8,128)(2,1)S(1)}, u32[]{:S(2)}, u32[]{:S(2)}) collective-permute-start(bf16[96,3072]{1,0:T(8,128)(2,1)S(1)} %add_convert_fusion.9), channel_id=1, source_target_pairs={{1,0},{2,3},{5,4},{6,7},{9,8},{10,11},{13,12},{14,15},{17,16},{18,... | collective-permute-start | bytes 1769480 | tf_op jit(solution)/shard_map/ppermute | solution.py:659
  370.1 34.6 %collective-permute-start.25 = (bf16[96,2304]{1,0:T(8,128)(2,1)S(1)}, bf16[96,2304]{1,0:T(8,128)(2,1)S(1)}, u32[]{:S(2)}, u32[]{:S(2)}) collective-permute-start(bf16[96,2304]{1,0:T(8,128)(2,1)S(1)} %add_convert_fusion.14), channel_id=1, source_target_pairs={{1,0},{2,3},{5,4},{6,7},{9,8},{10,11},{13,12},{14,15},{17,16},{18,... | collective-permute-start | bytes 1327112 | tf_op jit(solution)/shard_map/ppermute | solution.py:659
  (43 other events, 495.5 us)
where the time goes:
time: 414 us; the launch traced here: 406 us
  Pallas kernels  171 us (41%)
  waiting for transfers between devices  106 us (26%)
  starting transfers between devices  64.5 us (16%)
  matrix products  23.2 us (6%)
  other arithmetic  18.3 us (4%)
  local copies, waits for them, and re-layouts  15 us (4%)
  between operations  7.49 us (2%)
    ppermute x26, waiting for transfers between devices, swap(): return lax.ppermute(value, 'dp', [(i, i ^ bit) for i in range(8)])  58.1 us
    pallas_call x1, Pallas kernels, start_work(): pl.pallas_call(functools.partial(start_kernel, plan.PLANE, plan.PLACE), i...  48.7 us
    pallas_call x1, Pallas kernels, attend(): kernel_call(functools.partial(attend_kernel, sub, ways), 'attend', (pairs...  36.2 us
    pallas_call x1, Pallas kernels, grad_key_value(): kernel_call(functools.partial(grad_key_kernel, sub, pieces), 'grad_key_va...  33.9 us
    ppermute x4, waiting for transfers between devices, reduce(): ends = lax.ppermute(total, 'seq', [(1, 0), (2, 3)])  31.1 us
    ppermute x26, starting transfers between devices, swap(): return lax.ppermute(value, 'dp', [(i, i ^ bit) for i in range(8)])  28.5 us
    dot_general x7, matrix products, dot_as(): return lax.dot_general(left, right, dims, preferred_element_type=F32)  23.2 us
    pallas_call x3, Pallas kernels, grad_weight_wide(): pl.pallas_call(functools.partial(grad_weight_kernel, parts), grid_spec=pl...  21.9 us
  transfers between devices with their start and end apart: 55, of which 24 were waited for; matrix products, arithmetic and copies ran while one was open for 7% of the time, Pallas kernels for 21%

commit v1 on v0

--- a/solution.py
+++ b/solution.py
@@ -54,16 +54,16 @@
     return (grad_in, jnp.sum(grad_out * normed, 0), jnp.sum(grad_out, 0))
 
 
-def pick(table, index):
-    found = jnp.int32(table[0])
-    for i, value in enumerate(table[1:], 1):
-        found = jnp.where(index == i, jnp.int32(value), found)
-    return found
-
-
-def place_of_device():
+def neighbours():
     dp, z = lax.axis_index("dp"), lax.axis_index("seq")
-    return lax.div(dp, jnp.int32(4)), lax.rem(dp, jnp.int32(4)), z
+    other = dp + 1 - 2 * lax.rem(dp, jnp.int32(2))
+    pair = z + 1 - 2 * lax.rem(z, jnp.int32(2))
+    return (other, z), (dp, pair), (other, lax.rem(z + 2, jnp.int32(4)))
+
+
+def stays():
+    dp, z = lax.axis_index("dp"), lax.axis_index("seq")
+    return lax.rem(dp, jnp.int32(2)) == lax.div(z, jnp.int32(2))
 
 
 def greet(devices):
@@ -84,31 +84,36 @@
     )
 
 
-def routes(plane, place):
-    y, j, z = place_of_device()
-    targets = [(y * 4 + pick(place[h], z), pick(plane, j)) for h in range(2)]
-    sources = [
-        (
-            y * 4 + pick([plane.index(p) for p in range(4)], z),
-            pick([place[h].index(p) for p in range(4)], j),
-        )
-        for h in range(2)
-    ]
-    return targets, sources
-
-
-def moves(source, target, sent, landed, devices):
-    half = source.shape[0] // 2
-    return [
-        remote(
-            source.at[pl.ds(h * half, half)],
-            target.at[pl.ds(h * half, half)],
-            sent.at[h],
-            landed.at[h],
-            devices[h],
-        )
-        for h in range(2)
-    ]
+def move_start(source, target, sent, landed):
+    swap = neighbours()[2]
+
+    @pl.when(stays())
+    def _():
+        pltpu.make_async_copy(source, target, landed).start()
+
+    @pl.when(jnp.logical_not(stays()))
+    def _():
+        remote(source, target, sent, landed, swap).start()
+
+
+def move_landed(source, target, sent, landed):
+    swap = neighbours()[2]
+
+    @pl.when(stays())
+    def _():
+        pltpu.make_async_copy(source, target, landed).wait()
+
+    @pl.when(jnp.logical_not(stays()))
+    def _():
+        remote(source, target, sent, landed, swap).wait_recv()
+
+
+def move_sent(source, target, sent, landed):
+    swap = neighbours()[2]
+
+    @pl.when(jnp.logical_not(stays()))
+    def _():
+        remote(source, target, sent, landed, swap).wait_send()
 
 
 def head_lanes(rows, head):
@@ -130,13 +135,12 @@
         out_ref, chance_ref, lse_ref, stat = refs
     else:
         home_ref, out_ref, chance_ref, lse_ref, here_ref, stat, sent, landed = refs
-        targets, sources = routes(*ways)
+        move = (home_ref, here_ref, sent, landed)
 
         @pl.when(pair == 0)
         def _():
-            greet(targets + sources)
-            for copy in moves(home_ref, here_ref, sent, landed, targets):
-                copy.start()
+            greet([neighbours()[2]])
+            move_start(*move)
 
     keys = jnp.concatenate([k_ref[...], mark_k[...]], 1)
     values = v_ref[...]
@@ -165,8 +169,8 @@
     def _():
         lse_ref[...] = jnp.transpose(stat[...])[:STATS]
         if ways is not None:
-            for copy in moves(home_ref, here_ref, sent, landed, targets):
-                copy.wait()
+            move_landed(*move)
+            move_sent(*move)
 
 
 def grad_query_kernel(
@@ -293,7 +297,7 @@
             stats,
         ]
         + [jax.ShapeDtypeStruct(array.shape, array.dtype) for array in moving],
-        [pltpu.VMEM((rows, LANES), F32)] + [pltpu.SemaphoreType.DMA((2,))] * (2 * len(moving)),
+        [pltpu.VMEM((rows, LANES), F32)] + [pltpu.SemaphoreType.DMA] * (2 * len(moving)),
         24 * rows * length * width,
         4 * pairs * rows * length,
         **params,
@@ -343,6 +347,456 @@
         32 * rows * length * width,
         8 * length * width,
     )(own, own, projected, *grads, *log_totals, *deltas, mark_k, mark_q)
+
+
+class Chunk:
+    def __init__(self, index, source, rows, columns, y_first):
+        self.index, self.source, self.rows, self.columns = index, source, rows, columns
+        self.shape = (rows[1], columns[1])
+        self.blocks = ((2, 3), 1) if y_first else ((1, 3), 2)
+        self.y_first = y_first
+
+    def scratch(self):
+        rows, columns = self.shape
+        return [
+            pltpu.VMEM((4, rows, columns), BF16),
+            pltpu.VMEM((4, rows, columns), BF16),
+            pltpu.VMEM((2, rows, columns), BF16),
+            pltpu.VMEM((rows, columns), BF16),
+            pltpu.VMEM((rows, columns), BF16),
+            pltpu.VMEM((rows, columns), BF16),
+            pltpu.VMEM((rows, columns), BF16),
+            pltpu.SemaphoreType.DMA((8,)),
+            pltpu.SemaphoreType.DMA((8,)),
+        ]
+
+    def bind(self, keep_refs, send_refs, out_refs, scratch, devices):
+        at = (pl.ds(*self.rows), pl.ds(*self.columns))
+        whole = (pl.ds(0, 4),) + at
+        keep_hbm = keep_refs[self.source].at[whole]
+        send_hbm = send_refs[self.source].at[whole]
+        self.out = out_refs[self.source].at[at]
+        (self.keep, core, first, second, self.z1, self.z2, self.z3, sent, landed) = scratch
+        near, far = (devices["y"], devices["x"]) if self.y_first else (devices["x"], devices["y"])
+        self.core, self.first, self.second = core, first, second
+        sends, last = self.blocks
+        self.load = pltpu.make_async_copy(keep_hbm, self.keep, landed.at[7])
+        self.to_core = remote(send_hbm, core, sent.at[0], landed.at[0], devices["core"])
+        self.to_near = [
+            remote(self.keep.at[b], first.at[i], sent.at[1 + i], landed.at[1 + i], near)
+            for i, b in enumerate(sends)
+        ]
+        self.to_far = remote(self.keep.at[last], second, sent.at[3], landed.at[3], far)
+        self.inward = remote(self.keep.at[0], self.z1, sent.at[4], landed.at[4], devices["pair"])
+        self.middle = remote(self.keep.at[0], self.z2, sent.at[5], landed.at[5], devices["mirror"])
+        self.outward = remote(self.z1, self.z3, sent.at[6], landed.at[6], devices["pair"])
+
+    def add(self, target, source):
+        def step(i, carry):
+            at = pl.ds(pl.multiple_of(i * 16, 16), 16)
+            target[at, :] = added(target[at, :], source[at, :])
+            return carry
+
+        lax.fori_loop(0, self.shape[0] // 16, step, 0)
+
+    def start(self):
+        self.to_core.start()
+        self.load.start()
+
+    def near(self):
+        self.load.wait()
+        self.to_core.wait_recv()
+        for block in range(4):
+            self.add(self.keep.at[block], self.core.at[block])
+        for copy in self.to_near:
+            copy.start()
+
+    def far(self):
+        stay = [b for b in range(4) if b not in self.blocks[0]]
+        for i, copy in enumerate(self.to_near):
+            copy.wait_recv()
+            self.add(self.keep.at[stay[i]], self.first.at[i])
+        self.to_far.start()
+
+    def along(self):
+        self.to_far.wait_recv()
+        self.add(self.keep.at[0], self.second)
+
+        @pl.when(jnp.logical_not(inner()))
+        def _():
+            self.inward.start()
+
+    def meet(self):
+        @pl.when(inner())
+        def _():
+            self.inward.wait_recv()
+            self.add(self.keep.at[0], self.z1)
+            self.middle.start()
+
+    def spread(self):
+        @pl.when(inner())
+        def _():
+            self.middle.wait_recv()
+
+            def step(i, carry):
+                at = pl.ds(pl.multiple_of(i * 16, 16), 16)
+                total = added(self.keep[0, at, :], self.z2[at, :])
+                self.z1[at, :] = total
+                self.out[at, :] = total.astype(F32)
+                return carry
+
+            lax.fori_loop(0, self.shape[0] // 16, step, 0)
+            self.outward.start()
+
+    def finish(self):
+        @pl.when(jnp.logical_not(inner()))
+        def _():
+            self.outward.wait_recv()
+
+            def step(i, carry):
+                at = pl.ds(pl.multiple_of(i * 16, 16), 16)
+                self.out[at, :] = self.z3[at, :].astype(F32)
+                return carry
+
+            lax.fori_loop(0, self.shape[0] // 16, step, 0)
+            self.inward.wait_send()
+
+        @pl.when(inner())
+        def _():
+            self.middle.wait_send()
+            self.outward.wait_send()
+
+        self.to_core.wait_send()
+        for copy in self.to_near:
+            copy.wait_send()
+        self.to_far.wait_send()
+
+
+def inner():
+    z = lax.axis_index("seq")
+    return jnp.logical_and(z > 0, z < 3)
+
+
+def ring_devices():
+    dp, z = lax.axis_index("dp"), lax.axis_index("seq")
+    core, pair, swap = neighbours()
+    x = dp + 2 - 4 * lax.rem(lax.div(dp, jnp.int32(2)), jnp.int32(2))
+    y = dp + 4 - 8 * lax.div(dp, jnp.int32(4))
+    return {
+        "core": core,
+        "pair": pair,
+        "swap": swap,
+        "x": (x, z),
+        "y": (y, z),
+        "mirror": (dp, 3 - z),
+    }
+
+
+def backward_chunks(shapes):
+    found = []
+    for source, y_first, count in ((0, True, 3), (1, False, 3), (2, True, 1)):
+        _, rows, columns = shapes[source]
+        for part in range(count):
+            if source == 0:
+                size = rows // count
+                found.append((part, source, (part * size, size), (0, columns), y_first))
+            else:
+                size = columns // count
+                found.append((part, source, (0, rows), (part * size, size), y_first))
+    found.sort(key=lambda chunk: (chunk[0] if chunk[1] < 2 else 3, chunk[1]))
+    return [Chunk(i, *chunk[1:]) for i, chunk in enumerate(found)]
+
+
+def backward_kernel(
+    shapes,
+    pairs,
+    chance_ref,
+    grad_ref,
+    attended_ref,
+    k_ref,
+    v_ref,
+    q_ref,
+    mark_k,
+    mark_q,
+    lse_ref,
+    keep_down,
+    send_down,
+    keep_up,
+    send_up,
+    keep_out,
+    send_out,
+    block_ref,
+    dq_ref,
+    dk_ref,
+    dv_ref,
+    down_ref,
+    up_ref,
+    out_ref,
+    home_ref,
+    grads,
+    stats,
+    own_stats,
+    sent,
+    landed,
+    *scratch,
+):
+    step = pl.program_id(0)
+    rows, width = grad_ref.shape
+    half = rows // 2
+    devices = ring_devices()
+    chunks = backward_chunks(shapes)
+    per = len(scratch) // len(chunks)
+    for chunk in chunks:
+        chunk.bind(
+            (keep_down, keep_up, keep_out),
+            (send_down, send_up, send_out),
+            (down_ref, up_ref, out_ref),
+            scratch[chunk.index * per : (chunk.index + 1) * per],
+            devices,
+        )
+    move = (block_ref, home_ref, sent.at[12], landed.at[12])
+
+    def grad_copy(i, part, source, device):
+        at = pl.ds(part * half, half)
+        n = 2 * i + part
+        return remote(source.at[at], grads.at[i, at], sent.at[n], landed.at[n], device)
+
+    def to_core(part):
+        return grad_copy(1, part, grad_ref, devices["core"])
+
+    def to_pair(part):
+        return grad_copy(2, part, grad_ref, devices["pair"])
+
+    def to_corner(part):
+        return grad_copy(3, part, grads.at[2], devices["core"])
+
+    def stat_copy(i, source, device):
+        return remote(source, stats.at[i], sent.at[8 + i], landed.at[8 + i], device)
+
+    stat_core = stat_copy(1, own_stats, devices["core"])
+    stat_pair = stat_copy(2, own_stats, devices["pair"])
+    stat_corner = stat_copy(3, stats.at[2], devices["core"])
+
+    def begin():
+        greet(list(devices.values()))
+        for part in range(2):
+            to_pair(part).start()
+        for part in range(2):
+            to_core(part).start()
+        product = grad_ref[...].astype(F32) * attended_ref[...].astype(F32)
+        high = product.astype(BF16)
+        low = (product - high.astype(F32)).astype(BF16)
+        head = lax.broadcasted_iota(jnp.int32, (STATS, width), 0)
+        column = lax.broadcasted_iota(jnp.int32, (STATS, width), 1)
+        mine = jnp.where(
+            jnp.logical_and(column >= head * HDIM, column < (head + 1) * HDIM), 1.0, 0.0
+        ).astype(BF16)
+        own_stats[0:STATS, :] = lse_ref[...]
+        own_stats[STATS:, :] = dot_as(mine, high, NT) + dot_as(mine, low, NT)
+        stats[0] = own_stats[...]
+        grads[0] = grad_ref[...]
+        stat_pair.start()
+        stat_core.start()
+
+    def corner_stats():
+        stat_pair.wait_recv()
+        stat_corner.start()
+
+    def corner(part):
+        def run():
+            to_pair(part).wait_recv()
+            to_corner(part).start()
+
+        return run
+
+    def all_grads():
+        stat_core.wait_recv()
+        stat_corner.wait_recv()
+        for part in range(2):
+            to_core(part).wait_recv()
+            to_corner(part).wait_recv()
+
+    events = {0: [begin], 2: [corner_stats], 4: [corner(0)], pairs: [corner(1), all_grads]}
+
+    def plan(at, *methods):
+        events.setdefault(at, []).extend(methods)
+
+    plan(0, *[chunk.start for chunk in chunks])
+    plan(pairs, lambda: move_start(*move))
+    when = {
+        0: (1, 5, 7, 9, 11, 13),
+        1: (1, 5, 7, 9, 11, 13),
+        2: (3, 8, 10, 12, 14, 16),
+        3: (3, 8, 10, 12, 14, 16),
+        4: (6, 12, 14, 16, 17, 18),
+        5: (6, 12, 14, 16, 17, 18),
+        6: (8, 13, 15, 17, 18, 18),
+    }
+    for number, stage in enumerate(("near", "far", "along", "meet", "spread", "finish")):
+        for chunk in chunks:
+            plan(when[chunk.index][number], getattr(chunk, stage))
+
+    def end():
+        move_landed(*move)
+        move_sent(*move)
+        stat_core.wait_send()
+        stat_pair.wait_send()
+        stat_corner.wait_send()
+        for part in range(2):
+            to_core(part).wait_send()
+            to_pair(part).wait_send()
+            to_corner(part).wait_send()
+
+    steps = 3 * pairs
+    plan(steps, end)
+    for at in range(steps):
+        if at in events:
+
+            @pl.when(step == at)
+            def _():
+                for event in events[at]:
+                    event()
+
+    @pl.when(step < pairs)
+    def _():
+        query_grads(chance_ref, grad_ref, attended_ref, k_ref, v_ref, dq_ref, step)
+
+    @pl.when(step >= pairs)
+    def _():
+        pair = lax.rem(step, jnp.int32(pairs))
+        first = (lax.div(step, jnp.int32(pairs)) - 1) * half
+        at = pl.ds(pl.multiple_of(first, half), half)
+        tile = pl.ds(pl.multiple_of(pair * LANES, LANES), LANES)
+
+        def stat(row):
+            return jnp.concatenate([stats[i, pl.ds(row, 1), :] for i in range(4)], 1)
+
+        dk, dv = key_grads(
+            k_ref[at, :],
+            v_ref[at, :],
+            mark_k[at, :],
+            q_ref[...],
+            jnp.concatenate([grads[i, :, tile] for i in range(4)], 0),
+            mark_q[...],
+            [stat(2 * pair + head) for head in range(2)],
+            [stat(STATS + 2 * pair + head) for head in range(2)],
+        )
+        dk_ref[...] = dk
+        dv_ref[...] = dv
+
+    @pl.when(step == steps - 1)
+    def _():
+        for event in events[steps]:
+            event()
+
+
+def query_grads(chance_ref, grad_ref, out_ref, k_ref, v_ref, dq_ref, pair, sub=256):
+    keys, values = k_ref[...], v_ref[...]
+    tile = pl.ds(pl.multiple_of(pair * LANES, LANES), LANES)
+
+    def step(i, carry):
+        rows = pl.ds(pl.multiple_of(i * sub, sub), sub)
+        grad = grad_ref[rows, tile]
+        product = grad.astype(F32) * out_ref[rows, tile].astype(F32)
+        outs = []
+        for head in range(2):
+            own = head_lanes(sub, head)
+            delta = jnp.sum(jnp.where(own, product, 0.0), -1, keepdims=True)
+            grad_chances = dot_as(jnp.where(own, grad, jnp.zeros_like(grad)), values, NT)
+            scores = (chance_ref[head, rows, :].astype(F32) * (grad_chances - delta)).astype(BF16)
+            outs.append(dot_as(scores, keys, NN))
+        both = jnp.where(head_lanes(sub, 0), outs[0], outs[1])
+        dq_ref[rows, :] = (both * (1.0 / math.sqrt(HDIM))).astype(BF16)
+        return carry
+
+    lax.fori_loop(0, dq_ref.shape[0] // sub, step, 0)
+
+
+def key_grads(key, value, mark_k, queries, grads, mark_q, log_totals, deltas):
+    scaled = jnp.concatenate([queries * jnp.asarray(1.0 / math.sqrt(HDIM), BF16), mark_q], 1)
+    dks, dvs = [], []
+    for head in range(2):
+        own = head_lanes(key.shape[0], head)
+        key_own = jnp.where(own, key, jnp.zeros_like(key))
+        value_own = jnp.where(own, value, jnp.zeros_like(value))
+        scores = dot_as(jnp.concatenate([key_own, mark_k], 1), scaled, NT)
+        chances = jnp.exp(scores - log_totals[head])
+        grad_chances = dot_as(value_own, grads, NT)
+        grad_scores = (chances * (grad_chances - deltas[head])).astype(BF16)
+        dvs.append(dot_as(chances.astype(BF16), grads, NN))
+        dks.append(dot_as(grad_scores, queries, NN))
+    first = head_lanes(key.shape[0], 0)
+    dk = jnp.where(first, dks[0], dks[1]) * (1.0 / math.sqrt(HDIM))
+    return dk.astype(BF16), jnp.where(first, dvs[0], dvs[1]).astype(BF16)
+
+
+def backward(chances, grad, attended, projected, mark_k, mark_q, log_totals, halves, block_out):
+    rows, width = grad.shape
+    length, pairs = projected.shape[0], width // LANES
+    shapes = [keep.shape for keep, _ in halves]
+    anywhere = pl.BlockSpec(memory_space=pl.ANY)
+    result = jax.ShapeDtypeStruct((rows, width), BF16)
+    reduced = [jax.ShapeDtypeStruct(shape[1:], F32) for shape in shapes]
+
+    def once(array):
+        return pl.BlockSpec(
+            array.shape, lambda t: (0,) * array.ndim, pipeline_mode=pl.Buffered(1)
+        )
+
+    def tile(first):
+        return pl.BlockSpec((length, LANES), lambda t: (0, first + lax.rem(t, pairs)))
+
+    late = pl.BlockSpec(
+        (rows // 2, LANES),
+        lambda t: (jnp.maximum(lax.div(t, pairs) - 1, 0), jnp.maximum(t - pairs, 0) % pairs),
+    )
+    chunks = backward_chunks(shapes)
+    stats = (2 * STATS, rows)
+    return kernel_call(
+        functools.partial(backward_kernel, shapes, pairs),
+        "backward",
+        (3 * pairs,),
+        [
+            pl.BlockSpec((2, rows, length), lambda t: (jnp.minimum(t, pairs - 1), 0, 0)),
+            once(grad),
+            once(attended),
+            tile(pairs),
+            tile(2 * pairs),
+            pl.BlockSpec((length, LANES), lambda t: (0, jnp.maximum(t - pairs, 0) % pairs)),
+            once(mark_k),
+            once(mark_q),
+            once(log_totals),
+        ]
+        + [anywhere] * (2 * len(halves) + 1),
+        [pl.BlockSpec((rows, LANES), lambda t: (0, jnp.minimum(t, pairs - 1))), late, late]
+        + [once(shape) for shape in reduced]
+        + [anywhere],
+        [result] * 3 + reduced + [result],
+        [
+            pltpu.VMEM((4, rows, width), BF16),
+            pltpu.VMEM((4,) + stats, F32),
+            pltpu.VMEM(stats, F32),
+            pltpu.SemaphoreType.DMA((13,)),
+            pltpu.SemaphoreType.DMA((13,)),
+        ]
+        + [entry for chunk in chunks for entry in chunk.scratch()],
+        48 * rows * length * width,
+        4 * pairs * rows * length,
+        collective_id=2,
+        has_side_effects=True,
+    )(
+        chances,
+        grad,
+        attended,
+        projected,
+        projected,
+        projected,
+        mark_k,
+        mark_q,
+        log_totals,
+        *[array for pair in halves for array in pair],
+        block_out,
+    )
 
 
 def grad_weight_kernel(parts, index_ref, left_ref, right_ref, keep_ref, send_ref, turned):
@@ -426,8 +880,6 @@
 
 
 def start_kernel(
-    plane,
-    place,
     tokens_ref,
     lengths_ref,
     gain_ref,
@@ -444,66 +896,59 @@
     landed,
     out_sem,
 ):
-    y, j, z = place_of_device()
-    dp = lax.axis_index("dp")
-    half = tokens_ref.shape[0] // 2
-    part = half // 2
-    targets, sources = routes(plane, place)
-    core, across = (dp + 1 - 2 * lax.rem(dp, jnp.int32(2)), z), (
-        y * 4 + lax.rem(j + 2, jnp.int32(4)),
-        z,
-    )
-    greet(targets + sources + [core, across])
+    core, across, swap = neighbours()
+    parts = sent.shape[1]
+    height = tokens_ref.shape[0]
+    part = height // parts
+    greet([core, across, swap])
 
     def span(i):
-        return pl.ds(pl.multiple_of(lax.rem(i, 2) * half + lax.div(i, 2) * part, part), part)
-
-    def moved(i, h):
-        at = pl.ds(h * half + (i // 2) * part, part)
+        return pl.ds(pl.multiple_of(i * part, part), part)
+
+    def moved(i):
+        return (tokens_ref.at[span(i)], rows.at[0, span(i)], sent.at[0, i], landed.at[0, i])
+
+    def lengths():
+        return remote(lengths_ref, found_ref, sent.at[4, 0], landed.at[4, 0], core)
+
+    def forward(i, origin, piece, device):
         return remote(
-            tokens_ref.at[at], rows.at[0, at], sent.at[0, i], landed.at[0, i], targets[h]
+            rows.at[origin, span(i)],
+            rows.at[piece, span(i)],
+            sent.at[piece, i],
+            landed.at[piece, i],
+            device,
         )
 
-    def lengths():
-        return remote(lengths_ref, found_ref, sent.at[4, 0], landed.at[4, 0], targets[0])
-
-    def forward(i, origin, piece, device):
-        at = span(i)
-        return remote(
-            rows.at[origin, at], rows.at[piece, at], sent.at[piece, i], landed.at[piece, i], device
-        )
+    def out_span(piece, i):
+        return pl.ds(pl.multiple_of(piece * height + i * part, part), part)
 
     def to_hbm(piece, i):
-        at = pl.ds(pl.multiple_of(piece * 2 * half + span(i).start, part), part)
-        return pltpu.make_async_copy(
-            staged.at[at], projected_ref.at[at], out_sem.at[piece, i]
-        )
+        at = out_span(piece, i)
+        return pltpu.make_async_copy(staged.at[at], projected_ref.at[at], out_sem.at[piece, i])
 
     def project(piece, i):
-        at = span(i)
-        values = rows[piece, at, :].astype(F32)
+        values = rows[piece, span(i), :].astype(F32)
         hidden = layer_norm(values, gain_ref[...], shift_ref[...])[0].astype(BF16)
-        out = pl.ds(pl.multiple_of(piece * 2 * half + at.start, part), part)
-        staged[out, :] = (dot_as(hidden, w_ref[...], NN) + bias_ref[...]).astype(BF16)
+        staged[out_span(piece, i), :] = (
+            dot_as(hidden, w_ref[...], NN) + bias_ref[...]
+        ).astype(BF16)
         to_hbm(piece, i).start()
         return hidden
 
-    for i in range(4):
-        moved(i, i % 2).start()
+    for i in range(parts):
+        move_start(*moved(i))
     lengths().start()
 
     def first(i, carry):
-        at = span(i)
-        remote(
-            rows.at[0, at], rows.at[0, at], sent.at[0, i], landed.at[0, i], core
-        ).wait_recv()
+        move_landed(*moved(i))
         forward(i, 0, 2, across).start()
         forward(i, 0, 1, core).start()
-        hidden_ref[at, :] = project(0, i)
-        here_ref[at, :] = rows[0, at, :]
+        hidden_ref[span(i), :] = project(0, i)
+        here_ref[span(i), :] = rows[0, span(i), :]
         return carry
 
-    lax.fori_loop(0, 4, first, 0)
+    lax.fori_loop(0, parts, first, 0)
 
     def second(i, carry):
         forward(i, 0, 1, core).wait_recv()
@@ -513,19 +958,18 @@
         project(2, i)
         return carry
 
-    lax.fori_loop(0, 4, second, 0)
+    lax.fori_loop(0, parts, second, 0)
 
     def third(i, carry):
         forward(i, 2, 3, core).wait_recv()
         project(3, i)
         return carry
 
-    lax.fori_loop(0, 4, third, 0)
+    lax.fori_loop(0, parts, third, 0)
     lengths().wait()
-    for i in range(4):
-        moved(i, i % 2).wait_send()
 
     def last(i, carry):
+        move_sent(*moved(i))
         forward(i, 0, 2, across).wait_send()
         forward(i, 0, 1, core).wait_send()
         forward(i, 2, 3, core).wait_send()
@@ -533,23 +977,21 @@
             to_hbm(piece, i).wait()
         return carry
 
-    lax.fori_loop(0, 4, last, 0)
-
-
-def start_work(plan, tokens, clip_lengths, gain, shift, weight, bias):
+    lax.fori_loop(0, parts, last, 0)
+
+
+def start_work(tokens, clip_lengths, gain, shift, weight, bias):
     rows, width = tokens.shape
-    lengths = jnp.zeros((8, LANES), jnp.int32)
-    lengths = lax.dynamic_update_slice(lengths, clip_lengths, (0, 0))
     vmem, anywhere = pl.BlockSpec(memory_space=pltpu.VMEM), pl.BlockSpec(memory_space=pl.ANY)
     projected, hidden, here, found = pl.pallas_call(
-        functools.partial(start_kernel, plan.PLANE, plan.PLACE),
+        start_kernel,
         in_specs=[anywhere] + [vmem] * 5,
         out_specs=[anywhere, vmem, vmem, vmem],
         out_shape=[
             jax.ShapeDtypeStruct((4 * rows, 3 * width), BF16),
             jax.ShapeDtypeStruct((rows, width), BF16),
             jax.ShapeDtypeStruct((rows, width), BF16),
-            jax.ShapeDtypeStruct((8, LANES), jnp.int32),
+            jax.ShapeDtypeStruct(clip_lengths.shape, jnp.int32),
         ],
         scratch_shapes=[
             pltpu.VMEM((4, rows, width), BF16),
@@ -565,74 +1007,64 @@
             flops=24 * rows * width * width, bytes_accessed=32 * rows * width, transcendentals=0
         ),
         name="start_work",
-    )(tokens, lengths, gain.reshape(1, -1), shift.reshape(1, -1), weight, bias.reshape(1, -1))
-    return projected, hidden, here, found[:1, : clip_lengths.shape[1]]
+    )(tokens, clip_lengths, gain.reshape(1, -1), shift.reshape(1, -1), weight, bias.reshape(1, -1))
+    return projected, hidden, here, jnp.where(stays(), clip_lengths, found)
 
 
 def added(one, other):
     return (one.astype(F32) + other.astype(F32)).astype(BF16)
 
 
-class PlanePlan:
-    PLANE = (0, 3, 1, 2)
-    PLACE = ((1, 3, 2, 0), (2, 0, 1, 3))
-    pieces = 4
-    ways = (PLANE, PLACE)
-
-    def __init__(self):
-        self.there = []
-        for place in self.PLACE:
-            self.there.append(
-                [
-                    ((y * 4 + j) * 4 + z, (y * 4 + place[z]) * 4 + self.PLANE[j])
-                    for y in range(2)
-                    for j in range(4)
-                    for z in range(4)
-                ]
-            )
-        self.back = [[(b, a) for a, b in pairs] for pairs in self.there]
-
-    def move(self, rows, pairs):
-        half = rows.shape[0] // 2
-        return jnp.concatenate(
-            [
-                lax.ppermute(rows[:half], ("dp", "seq"), pairs[0]),
-                lax.ppermute(rows[half:], ("dp", "seq"), pairs[1]),
-            ]
-        )
-
-    def to_work(self, rows):
-        return self.move(rows, self.there)
+class PairPlan:
+    ways = True
 
     def start(self, tokens, clip_lengths, gain, shift, weight, bias):
         projected, hidden, here, lengths = start_work(
-            self, tokens, clip_lengths, gain, shift, weight, bias
+            tokens, clip_lengths, gain, shift, weight, bias
         )
         return projected, projected, hidden, here, lengths
 
     def to_home(self, rows):
-        return self.move(rows, self.back)
+        pairs = [
+            (dp * 4 + z, (dp ^ 1) * 4 + (z ^ 2))
+            for dp in range(8)
+            for z in range(4)
+            if dp % 2 != z // 2
+        ]
+        return jnp.where(stays(), rows, lax.ppermute(rows, ("dp", "seq"), pairs))
 
     def gather(self, own):
-        core = lax.ppermute(own, "dp", [(i, i ^ 1) for i in range(8)])
-        across = lax.ppermute(own, "dp", [(i, i ^ 2) for i in range(8)])
-        corner = lax.ppermute(across, "dp", [(i, i ^ 1) for i in range(8)])
-        return [own, core, across, corner]
+        core = self.swap(own, 1)
+        across = lax.ppermute(own, "seq", [(i, i ^ 1) for i in range(4)])
+        return [own, core, across, self.swap(across, 1)]
 
     def positions(self, rows):
-        j = lax.axis_index("dp") % 4
-        half = rows // 2
-        sources = jnp.asarray([[place.index(p) for place in self.PLACE] for p in range(4)], jnp.int32)
+        core, z = lax.axis_index("dp") % 2, lax.axis_index("seq")
         found = []
         for piece in range(4):
-            shards = sources[j ^ piece]
-            for part in range(2):
-                start = shards[part] * rows + part * half
-                found.append(start + jnp.arange(half, dtype=jnp.int32))
+            c, plane = core ^ (piece % 2), z ^ (piece // 2)
+            shard = jnp.where(c == plane // 2, plane, plane ^ 2)
+            found.append(shard * rows + jnp.arange(rows, dtype=jnp.int32))
         return jnp.concatenate(found)
 
     def own(self, gathered):
         return gathered[: gathered.shape[0] // 4]
+
+    def backward(
+        self, chances, grad, attended, projected, own, mark_k, mark_q, log_totals, halves, block_out
+    ):
+        dq, dk, dv, down, up, out, home = backward(
+            chances,
+            grad,
+            attended,
+            projected,
+            self.own(mark_k),
+            mark_q,
+            log_totals,
+            halves,
+            block_out,
+        )
+        return dq, dk, dv, (down, up, out), home
 
     def weight(self, left, right):
         me = lax.axis_index("dp").astype(jnp.int32).reshape(1)
@@ -682,9 +1114,6 @@
     def __init__(self, pieces):
         self.pieces = pieces
 
-    def to_work(self, rows):
-        return rows
-
     def to_home(self, rows):
         return rows
 
@@ -704,6 +1133,21 @@
     def own(self, gathered):
         rows = gathered.shape[0] // self.pieces
         return lax.dynamic_slice_in_dim(gathered, lax.axis_index("seq") * rows, rows, 0)
+
+    def backward(
+        self, chances, grad, attended, projected, own, mark_k, mark_q, log_totals, halves, block_out
+    ):
+        dq, deltas = grad_query(chances, grad, attended, projected)
+        dk, dv = grad_key_value(
+            own,
+            projected,
+            self.gather(grad),
+            self.gather(log_totals),
+            self.gather(deltas),
+            self.own(mark_k),
+            mark_q,
+        )
+        return dq, dk, dv, [self.reduce(total) for total in halves], block_out
 
     def weight(self, left, right):
         return inner_rows(left, right)
@@ -757,7 +1201,6 @@
     attended, chances, log_totals, grad_out = attend(
         plan, own, projected, plan.own(mark_q), mark_k, cotangent
     )
-    log_totals = plan.gather(log_totals)
 
     inputs32 = here.astype(F32)
     middle = inputs32 + matmul(attended, w_out) + bias_out
@@ -772,13 +1215,13 @@
     grad_middle = grad_out.astype(F32) + grad_norm2
     grad_branch = grad_middle.astype(BF16)
     grad_attended = inner_cols(grad_branch, w_out).astype(BF16)
-    grads = plan.gather(grad_attended)
 
     block_out = (middle + matmul(activated, w_down) + bias_down).astype(BF16)
-    block_out = plan.to_home(block_out)
-    grad_w_down = plan.reduce(plan.weight(activated, grad_out))
-    grad_w_up = plan.reduce(plan.weight(hidden2, grad_upper))
-    grad_w_out = plan.reduce(plan.weight(attended, grad_branch))
+    halves = [
+        plan.weight(activated, grad_out),
+        plan.weight(hidden2, grad_upper),
+        plan.weight(attended, grad_branch),
+    ]
     grad_bias_down = jnp.sum(grad_out.astype(F32), 0)
     grad_bias_up = jnp.sum(grad_upper.astype(F32), 0)
     grad_bias_out = jnp.sum(grad_branch.astype(F32), 0)
@@ -788,10 +1231,17 @@
         )
     )
 
-    dq, deltas = grad_query(chances, grad_attended, attended, projected)
-    deltas = plan.gather(deltas)
-    dk, dv = grad_key_value(
-        own, projected, grads, log_totals, deltas, plan.own(mark_k), mark_q
+    dq, dk, dv, (grad_w_down, grad_w_up, grad_w_out), block_out = plan.backward(
+        chances,
+        grad_attended,
+        attended,
+        projected,
+        own,
+        mark_k,
+        mark_q,
+        log_totals,
+        halves,
+        block_out,
     )
     grad_projected = jnp.concatenate([dq, dk, dv], 1)
     grad_w_qkv = plan.reduce(plan.weight(hidden1, grad_projected))
@@ -825,7 +1275,7 @@
 
 def solution(mesh):
     sizes = dict(mesh.shape)
-    plan = PlanePlan() if sizes == {"dp": 8, "seq": 4} else PlainPlan(sizes["seq"])
+    plan = PairPlan() if sizes == {"dp": 8, "seq": 4} else PlainPlan(sizes["seq"])
     rows = P(("dp", "seq"), None)
     return jax.shard_map(
         functools.partial(body, plan),

time: 414 us -> 342 us (0.83); the launches traced: 406 us -> 341 us
  waiting for transfers between devices: 106 us -> 45 us
  Pallas kernels: 171 us -> 215 us
  starting transfers between devices: 64.5 us -> 23.2 us
  between operations: 7.49 us -> 1.3 us
  other arithmetic: 18.3 us -> 13.3 us
  matrix products: 23.2 us -> 28 us
    pallas_call x3 -> x2, Pallas kernels: 103 us -> 149 us  [the longest x1 111 us: backward(): kernel_call(functools.partial(backward_kernel, shapes, pairs), 'backward'...]
    ppermute x26 -> x11, waiting for transfers between devices: 58.1 us -> 21.3 us  [swap(): return lax.ppermute(value, 'dp', [(i, i ^ bit) for i in range(8)])]
    ppermute x4 -> x1, waiting for transfers between devices: 31.1 us -> 2.48 us  [reduce(): ends = lax.ppermute(total, 'seq', [(1, 0), (2, 3)])]
    ppermute x26 -> x11, starting transfers between devices: 28.5 us -> 14.1 us  [swap(): return lax.ppermute(value, 'dp', [(i, i ^ bit) for i in range(8)])]
    ppermute x13 -> x1, starting transfers between devices: 13.4 us -> 0.71 us  [to_home(): return jnp.where(stays(), rows, lax.ppermute(rows, ('dp', 'seq'), pairs))]
    ppermute x4, waiting for transfers between devices: 9.55 us -> 21.2 us  [reduce_vectors(): lax.ppermute(packed, 'seq', [(i, i ^ bit) for i in range(4)])]
    ppermute x4 -> x1, starting transfers between devices: 9.13 us -> 1.44 us  [reduce(): total = added(total, lax.ppermute(total, 'seq', [(0, 1), (3, 2)]))]
    dot_general x7, matrix products: 23.2 us -> 28 us  [dot_as(): return lax.dot_general(left, right, dims, preferred_element_type=F32)]
  transfers between devices with their start and end apart: 55 -> 19, of which waited for: 24 -> 10; matrix products, arithmetic and copies ran while one was open for 7% -> 4% of each run, Pallas kernels for 21% -> 0%
where the time goes in v1:
time: 342 us; the launch traced here: 341 us
  Pallas kernels  215 us (63%)
  waiting for transfers between devices  45 us (13%)
  matrix products  28 us (8%)
  starting transfers between devices  23.2 us (7%)
  local copies, waits for them, and re-layouts  14.8 us (4%)
  other arithmetic  13.3 us (4%)
    pallas_call x1, Pallas kernels, backward(): kernel_call(functools.partial(backward_kernel, shapes, pairs), 'backward'...  111 us
    pallas_call x1, Pallas kernels, start_work(): pl.pallas_call(start_kernel, in_specs=[anywhere] + [vmem] * 5, out_specs=...  38.8 us
    pallas_call x1, Pallas kernels, attend(): kernel_call(functools.partial(attend_kernel, sub, ways), 'attend', (pairs...  34.2 us
    dot_general x7, matrix products, dot_as(): return lax.dot_general(left, right, dims, preferred_element_type=F32)  28 us
    pallas_call x3, Pallas kernels, grad_weight_wide(): pl.pallas_call(functools.partial(grad_weight_kernel, parts), grid_spec=pl...  21.8 us
    ppermute x11, waiting for transfers between devices, swap(): return lax.ppermute(value, 'dp', [(i, i ^ bit) for i in range(8)])  21.3 us
    ppermute x4, waiting for transfers between devices, reduce_vectors(): lax.ppermute(packed, 'seq', [(i, i ^ bit) for i in range(4)])  21.2 us
    ppermute x11, starting transfers between devices, swap(): return lax.ppermute(value, 'dp', [(i, i ^ bit) for i in range(8)])  14.1 us
  transfers between devices with their start and end apart: 19, of which 10 were waited for; matrix products, arithmetic and copies ran while one was open for 4% of the time, Pallas kernels for 0%

profile of v1, /device:TPU:0, one launch (start us, length us, event | category | flops | bytes accessed | tf_op | source)
XLA Modules:
  0.0 340.9 jit_solution(11733556022319344503)
XLA Ops:
  2.2 1.3 reshape.127.gain_ref
  3.4 1.3 reshape.128.shift_ref
  4.7 38.8 %start_work.1 = (bf16[2048,2304]{1,0:T(8,128)(2,1)}, bf16[512,768]{1,0:T(8,128)(2,1)}, bf16[512,768]{1,0:T(8,128)(2,1)}, s32[1,4]{1,0:T(1,128)}) custom-call(bf16[512,768]{1,0:T(8,128)(2,1)} %tokens_ref.1, s32[1,4]{1,0:T(1,128)} %lengths_ref.1, f32[1,768]{1,0:T(1,128)} %reshape.127.gain_ref, f32[1,768]{1,0:T(1,128)} %reshape.128.shift_ref, ...), custom_call_target="tpu_custom_call" | custom-call | flops 7247757312 | bytes 12582912 | tf_op jit(solution)/shard_map/start_work/pallas_call | solution.py:986
  43.8 1.1 fusion.19.mark_k
  46.2 34.2 %attend.1 = (bf16[512,768]{1,0:T(8,128)(2,1)}, bf16[12,512,2048]{2,1,0:T(8,128)(2,1)}, f32[16,512]{1,0:T(8,128)}, bf16[512,768]{1,0:T(8,128)(2,1)}) custom-call(bf16[2048,2304]{1,0:T(8,128)(2,1)} %get-tuple-element.36.q_ref.k_ref.v_ref, bf16[2048,2304]{1,0:T(8,128)(2,1)} %get-tuple-element.36.q_ref.k_ref.v_ref, ...), custom_call_target="tpu_custom_call" | custom-call | flops 19327352832 | bytes 25165824 | tf_op jit(solution)/shard_map/attend/pallas_call | solution.py:276
  80.4 2.0 fusion.26
  83.5 6.6 %multiply_convert_fusion = (bf16[512,3072]{1,0:T(8,128)(2,1)}, f32[512,3072]{1,0:T(8,128)S(1)}) fusion(f32[3072]{0:T(1024)S(1)} %copy-done.23, bf16[512,768]{1,0:T(8,128)(2,1)S(1)} %add_convert_fusion.2.left_ref, bf16[768,3072]{1,0:T(8,128)(2,1)} %param.27), kind=kOutput, calls=%fused_computation.8 | convolution fusion | flops 2425356288 | bytes 14954496 | tf_op jit(solution)/shard_map/dot_general | solution.py:25
  90.1 5.3 %convert_reduce_fusion = (f32[3072]{0:T(1024)}, bf16[512,3072]{1,0:T(8,128)(2,1)S(1)}) fusion(f32[512,3072]{1,0:T(8,128)S(1)} %get-tuple-element.81, f32[3072]{0:T(1024)S(1)} %copy-done.23, bf16[512,768]{1,0:T(8,128)(2,1)S(1)} %copy-done.3, bf16[3072,768]{1,0:T(8,128)(2,1)S(1)} %bitcast.36), kind=kOutput, calls=%fused_computation.7 | convolution fusion | flops 2436363264 | bytes 14966784 | tf_op jit(solution)/shard_map/dot_general | solution.py:25
  95.4 3.0 multiply_reduce_fusion
  98.5 10.0 %grad_weight_wide.3 = (bf16[4,96,3072]{2,1,0:T(8,128)(2,1)}, bf16[4,96,3072]{2,1,0:T(8,128)(2,1)}) custom-call(s32[1]{0:T(128)} %bitcast.2.index_ref, bf16[512,768]{1,0:T(8,128)(2,1)} %copy-done.13, bf16[512,3072]{1,0:T(8,128)(2,1)} %copy-done.26), custom_call_target="tpu_custom_call" | custom-call | flops 2415919104 | bytes 4718592 | tf_op jit(solution)/shard_map/grad_weight_wide/pallas_call | solution.py:829
  108.5 5.0 %grad_weight_tall.3.send_down = bf16[4,384,768]{2,1,0:T(8,128)(2,1)} custom-call(s32[1]{0:T(128)} %bitcast.2.index_ref, bf16[512,3072]{1,0:T(8,128)(2,1)} %get-tuple-element.80.left_ref, bf16[512,768]{1,0:T(8,128)(2,1)} %get-tuple-element.39.right_ref), custom_call_target="tpu_custom_call" | custom-call | flops 1207959552 | bytes 2359296 | tf_op jit(solution)/shard_map/grad_weight_tall/pallas_call | solution.py:860
  113.4 5.0 %grad_weight_tall.2.keep_down = bf16[4,384,768]{2,1,0:T(8,128)(2,1)} custom-call(s32[1]{0:T(128)} %bitcast.2.index_ref, bf16[512,3072]{1,0:T(8,128)(2,1)} %get-tuple-element.80.left_ref, bf16[512,768]{1,0:T(8,128)(2,1)} %get-tuple-element.39.right_ref), custom_call_target="tpu_custom_call" | custom-call | flops 1207959552 | bytes 2359296 | tf_op jit(solution)/shard_map/grad_weight_tall/pallas_call | solution.py:860
  118.5 1.6 convert_reduce_fusion.3
  120.1 3.9 %grad_weight_wide.4 = (bf16[4,96,768]{2,1,0:T(8,128)(2,1)}, bf16[4,96,768]{2,1,0:T(8,128)(2,1)}) custom-call(s32[1]{0:T(128)} %bitcast.2.index_ref, bf16[512,768]{1,0:T(8,128)(2,1)} %get-tuple-element.41.left_ref.attended_ref, bf16[512,768]{1,0:T(8,128)(2,1)} %get-tuple-element.66.right_ref), custom_call_target="tpu_custom_call" | custom-call | flops 603979776 | bytes 1179648 | tf_op jit(solution)/shard_map/grad_weight_wide/pallas_call | solution.py:829
  123.9 3.0 convolution_convert_fusion.grad_ref
  126.9 1.6 slice.48.mark_k
  128.5 5.8 %add_convert_fusion.1.block_ref = bf16[512,768]{1,0:T(8,128)(2,1)} fusion(f32[512,768]{1,0:T(8,128)S(1)} %get-tuple-element.78, bf16[512,3072]{1,0:T(8,128)(2,1)S(1)} %copy-done.2, bf16[3072,768]{1,0:T(8,128)(2,1)} %param.29, f32[768]{0:T(1024)S(1)} %copy-done.25), kind=kOutput, calls=%fused_computation.33 | convolution fusion | flops 2417098752 | bytes 10226688 | tf_op jit(solution)/shard_map/dot_general | solution.py:25
  134.3 110.5 %backward.1 = (bf16[512,768]{1,0:T(8,128)(2,1)}, bf16[512,768]{1,0:T(8,128)(2,1)}, bf16[512,768]{1,0:T(8,128)(2,1)}, f32[384,768]{1,0:T(8,128)}, f32[96,3072]{1,...) custom-call(bf16[12,512,2048]{2,1,0:T(8,128)(2,1)} %get-tuple-element.38.chance_ref, ...), custom_call_target="tpu_custom_call" | custom-call | flops 38654705664 | bytes 25165824 | tf_op jit(solution)/shard_map/backward/pallas_call | solution.py:755
  244.9 1.3 constant_dynamic-update-slice_fusion.2
  246.5 1.4 copy-done.15
  247.9 8.0 %grad_weight_wide.5 = (bf16[4,96,2304]{2,1,0:T(8,128)(2,1)}, bf16[4,96,2304]{2,1,0:T(8,128)(2,1)}) custom-call(s32[1]{0:T(128)} %bitcast.2.index_ref, bf16[512,768]{1,0:T(8,128)(2,1)} %get-tuple-element.51.left_ref, bf16[512,2304]{1,0:T(8,128)(2,1)} %copy-done.15), custom_call_target="tpu_custom_call" | custom-call | flops 1811939328 | bytes 3538944 | tf_op jit(solution)/shard_map/grad_weight_wide/pallas_call | solution.py:829
  257.1 2.9 collective-permute-done.6
  260.0 2.6 add_convert_fusion
  262.7 3.5 %collective-permute-start.7 = (bf16[2,96,1152]{2,1,0:T(8,128)(2,1)S(1)}, bf16[2,96,1152]{2,1,0:T(8,128)(2,1)S(1)}, u32[]{:S(2)}, u32[]{:S(2)}) collective-permute-start(bf16[2,96,1152]{2,1,0:T(8,128)(2,1)S(1)} %slice.40), channel_id=1, source_target_pairs={{0,8},{4,12},{8,0},{12,4},{16,24},{20,28},{24,16},{28,20},{1,9},{5... | collective-permute-start | bytes 1327112 | tf_op jit(solution)/shard_map/ppermute | solution.py:1077
  266.2 2.4 fusion.16
  269.0 1.7 collective-permute-start.9
  270.7 6.0 %collective-permute-done.7 = bf16[2,96,1152]{2,1,0:T(8,128)(2,1)S(1)} collective-permute-done((bf16[2,96,1152]{2,1,0:T(8,128)(2,1)S(1)}, bf16[2,96,1152]{2,1,0:T(8,128)(2,1)S(1)}, u32[]{:S(2)}, u32[]{:S(2)}) %collective-permute-start.7) | collective-permute-done | bytes 442400 | tf_op jit(solution)/shard_map/ppermute | solution.py:1077
  276.8 1.7 collective-permute-start.8
  278.5 3.5 %collective-permute-done.9 = bf16[2,96,1152]{2,1,0:T(8,128)(2,1)S(1)} collective-permute-done((bf16[2,96,1152]{2,1,0:T(8,128)(2,1)S(1)}, bf16[2,96,1152]{2,1,0:T(8,128)(2,1)S(1)}, u32[]{:S(2)}, u32[]{:S(2)}) %collective-permute-start.9) | collective-permute-done | bytes 442400 | tf_op jit(solution)/shard_map/ppermute | solution.py:1077
  282.2 1.8 collective-permute-start.10
  284.0 2.4 collective-permute-done.8
  286.4 2.4 collective-permute-done.10
  289.0 1.4 collective-permute-start.11
  290.5 1.5 collective-permute-start.2
  292.6 1.6 collective-permute-done.2
  294.2 1.3 collective-permute-start.3
  295.5 2.4 collective-permute-done.3
  297.9 1.4 collective-permute-start.16
  300.2 1.4 collective-permute-start.12
  301.6 4.0 %collective-permute-start.5 = (f32[3072]{0:T(1024)S(1)}, f32[3072]{0:T(1024)S(1)}, u32[]{:S(2)}, u32[]{:S(2)}) collective-permute-start(f32[3072]{0:T(1024)S(1)} %add.226), channel_id=1, source_target_pairs={{0,2},{1,3},{2,0},{3,1},{4,6},{5,7},{6,4},{7,5},{8,10},{9,11},{10,... | collective-permute-start | bytes 36872 | tf_op jit(solution)/shard_map/ppermute | solution.py:1100
  307.1 15.5 %collective-permute-done.5 = f32[3072]{0:T(1024)S(1)} collective-permute-done((f32[3072]{0:T(1024)S(1)}, f32[3072]{0:T(1024)S(1)}, u32[]{:S(2)}, u32[]{:S(2)}) %collective-permute-start.5) | collective-permute-done | bytes 12320 | tf_op jit(solution)/shard_map/ppermute | solution.py:1100
  322.7 1.3 add_convert_fusion.3
  323.9 1.3 collective-permute-start.13
  325.9 5.7 %collective-permute-done.18 = f32[6144]{0:T(1024)S(1)} collective-permute-done((f32[6144]{0:T(1024)S(1)}, f32[6144]{0:T(1024)S(1)}, u32[]{:S(2)}, u32[]{:S(2)}) %collective-permute-start.18) | collective-permute-done | bytes 24608 | tf_op jit(solution)/shard_map/ppermute | solution.py:1100
  332.8 1.0 broadcast_select_fusion
  333.8 2.5 collective-permute-done.13
  338.9 1.0 copy.44
  339.9 1.0 copy.45
  (143 shorter events, 13.9 us)
Async XLA Ops:
  0.6 79.8 %copy-start = (bf16[768,768]{1,0:T(8,128)(2,1)S(1)}, bf16[768,768]{1,0:T(8,128)(2,1)}, u32[]{:S(2)}) copy-start(bf16[768,768]{1,0:T(8,128)(2,1)} %param.23) | copy-start | bytes 3538948
  4.7 38.8 %copy-start.21 = (s32[1,4]{1,0:T(1,128)S(1)}, s32[1,4]{1,0:T(1,128)}, u32[]{:S(2)}) copy-start(s32[1,4]{1,0:T(1,128)} %lengths_ref.1) | copy-start | bytes 52
  45.3 0.8 copy-start.10
  46.2 34.3 %copy-start.5 = (bf16[512,768]{1,0:T(8,128)(2,1)S(1)}, bf16[512,768]{1,0:T(8,128)(2,1)}, u32[]{:S(2)}) copy-start(bf16[512,768]{1,0:T(8,128)(2,1)} %get-tuple-element.40) | copy-start | bytes 2359300
  46.2 34.3 %copy-start.24 = (f32[768]{0:T(1024)S(1)}, f32[768]{0:T(1024)}, u32[]{:S(2)}) copy-start(f32[768]{0:T(1024)} %param.24) | copy-start | bytes 9220
  82.8 0.7 copy-start.23
  83.1 6.9 %slice-start.2 = ((s8[4718592]{0:T(1024)(128)(4,1)}), s8[4194304]{0:T(1024)(128)(4,1)S(1)}, s32[]{:S(2)}) async-start(s8[4718592]{0:T(1024)(128)(4,1)} %bitcast.35), calls=%async_computation.2 | async-start | bytes 8388608
  83.5 6.6 %copy-start.13 = (bf16[512,768]{1,0:T(8,128)(2,1)}, bf16[512,768]{1,0:T(8,128)(2,1)S(1)}, u32[]{:S(2)}) copy-start(bf16[512,768]{1,0:T(8,128)(2,1)S(1)} %add_convert_fusion.2.left_ref) | copy-start | bytes 2359300
  83.5 6.6 %copy-start.3 = (bf16[512,768]{1,0:T(8,128)(2,1)S(1)}, bf16[512,768]{1,0:T(8,128)(2,1)}, u32[]{:S(2)}) copy-start(bf16[512,768]{1,0:T(8,128)(2,1)} %get-tuple-element.39.right_ref) | copy-start | bytes 2359300
  83.5 6.6 %slice-start.3 = ((s8[4718592]{0:T(1024)(128)(4,1)}), s8[524288]{0:T(1024)(128)(4,1)S(1)}, s32[]{:S(2)}) async-start(s8[4718592]{0:T(1024)(128)(4,1)} %bitcast.35), calls=%async_computation.3 | async-start | bytes 1048576
  83.5 11.9 %slice-start = ((s8[4718592]{0:T(1024)(128)(4,1)}), s8[4194304]{0:T(1024)(128)(4,1)S(1)}, s32[]{:S(2)}) async-start(s8[4718592]{0:T(1024)(128)(4,1)} %bitcast.33), calls=%async_computation | async-start | bytes 8388608
  90.1 5.3 %slice-start.1 = ((s8[4718592]{0:T(1024)(128)(4,1)}), s8[524288]{0:T(1024)(128)(4,1)S(1)}, s32[]{:S(2)}) async-start(s8[4718592]{0:T(1024)(128)(4,1)} %bitcast.33), calls=%async_computation.1 | async-start | bytes 1048576
  95.4 3.0 copy-start.26
  113.4 5.0 %copy-start.4 = (bf16[512,768]{1,0:T(8,128)(2,1)S(1)}, bf16[512,768]{1,0:T(8,128)(2,1)}, u32[]{:S(2)}) copy-start(bf16[512,768]{1,0:T(8,128)(2,1)} %get-tuple-element.39.right_ref) | copy-start | bytes 2359300
  123.9 4.5 %copy-start.2 = (bf16[512,3072]{1,0:T(8,128)(2,1)S(1)}, bf16[512,3072]{1,0:T(8,128)(2,1)}, u32[]{:S(2)}) copy-start(bf16[512,3072]{1,0:T(8,128)(2,1)} %get-tuple-element.80.left_ref) | copy-start | bytes 9437188
  123.9 4.5 %copy-start.25 = (f32[768]{0:T(1024)S(1)}, f32[768]{0:T(1024)}, u32[]{:S(2)}) copy-start(f32[768]{0:T(1024)} %param.30) | copy-start | bytes 9220
  244.9 1.4 copy-start.12
  244.9 1.6 copy-start.7
  246.5 1.4 copy-start.15
  247.9 8.0 %copy-start.19 = (f32[3072]{0:T(1024)S(1)}, f32[3072]{0:T(1024)}, u32[]{:S(2)}) copy-start(f32[3072]{0:T(1024)} %get-tuple-element.83) | copy-start | bytes 36868
  255.9 4.1 %collective-permute-start.6 = (bf16[4,96,2304]{2,1,0:T(8,128)(2,1)}, bf16[4,96,2304]{2,1,0:T(8,128)(2,1)}, u32[]{:S(2)}, u32[]{:S(2)}) collective-permute-start(bf16[4,96,2304]{2,1,0:T(8,128)(2,1)} %get-tuple-element.53), channel_id=1, source_target_pairs={{0,4},{4,0},{8,12},{12,8},{16,20},{20,16},{24,28},{28,24},{1,5},{5... | collective-permute-start | bytes 5308424 | tf_op jit(solution)/shard_map/ppermute | solution.py:1077
  256.0 36.0 %collective-permute-start.14 = (f32[6144]{0:T(1024)S(1)}, f32[6144]{0:T(1024)S(1)}, u32[]{:S(2)}, u32[]{:S(2)}) collective-permute-start(f32[6144]{0:T(1024)S(1)} %constant_dynamic-update-slice_fusion.5), channel_id=1, source_target_pairs={{0,4},{4,0},{8,12},{12,8},{16,20},{20,16},{24,28},{28,24},{1,5},{5... | collective-permute-start | bytes 73736 | tf_op jit(solution)/shard_map/ppermute | solution.py:1077
  260.0 6.2 %copy-start.22 = (bf16[768,2304]{1,0:T(8,128)(2,1)S(1)}, bf16[768,2304]{1,0:T(8,128)(2,1)}, u32[]{:S(2)}) copy-start(bf16[768,2304]{1,0:T(8,128)(2,1)} %w_ref.1) | copy-start | bytes 10616836
  262.5 3.7 %copy-start.16 = (bf16[512,2304]{1,0:T(8,128)(2,1)S(1)}, bf16[512,2304]{1,0:T(8,128)(2,1)}, u32[]{:S(2)}) copy-start(bf16[512,2304]{1,0:T(8,128)(2,1)} %copy-done.15) | copy-start | bytes 7077892
  262.5 3.7 %copy-start.18 = (f32[768]{0:T(1024)S(1)}, f32[768]{0:T(1024)}, u32[]{:S(2)}) copy-start(f32[768]{0:T(1024)} %param.18) | copy-start | bytes 9220
  262.7 6.0 %copy-start.6 = (bf16[512,768]{1,0:T(8,128)(2,1)S(1)}, bf16[512,768]{1,0:T(8,128)(2,1)}, u32[]{:S(2)}) copy-start(bf16[512,768]{1,0:T(8,128)(2,1)} %get-tuple-element.48) | copy-start | bytes 2359300
  262.7 14.0 %collective-permute-start.7 = (bf16[2,96,1152]{2,1,0:T(8,128)(2,1)S(1)}, bf16[2,96,1152]{2,1,0:T(8,128)(2,1)S(1)}, u32[]{:S(2)}, u32[]{:S(2)}) collective-permute-start(bf16[2,96,1152]{2,1,0:T(8,128)(2,1)S(1)} %slice.40), channel_id=1, source_target_pairs={{0,8},{4,12},{8,0},{12,4},{16,24},{20,28},{24,16},{28,20},{1,9},{5... | collective-permute-start | bytes 1327112 | tf_op jit(solution)/shard_map/ppermute | solution.py:1077
  268.9 21.5 %collective-permute-start.1 = (f32[3072]{0:T(1024)S(1)}, f32[3072]{0:T(1024)S(1)}, u32[]{:S(2)}, u32[]{:S(2)}) collective-permute-start(f32[3072]{0:T(1024)S(1)} %pad_maximum_fusion.2), channel_id=1, source_target_pairs={{0,4},{4,0},{8,12},{12,8},{16,20},{20,16},{24,28},{28,24},{1,5},{5... | collective-permute-start | bytes 36872 | tf_op jit(solution)/shard_map/ppermute | solution.py:1077
  269.0 13.0 %collective-permute-start.9 = (bf16[2,96,1152]{2,1,0:T(8,128)(2,1)S(1)}, bf16[2,96,1152]{2,1,0:T(8,128)(2,1)S(1)}, u32[]{:S(2)}, u32[]{:S(2)}) collective-permute-start(bf16[2,96,1152]{2,1,0:T(8,128)(2,1)S(1)} %slice.53), channel_id=1, source_target_pairs={{0,16},{4,20},{8,24},{12,28},{16,0},{20,4},{24,8},{28,12},{1,17},{... | collective-permute-start | bytes 1327112 | tf_op jit(solution)/shard_map/ppermute | solution.py:1077
  276.8 9.6 %collective-permute-start.8 = (bf16[96,1152]{1,0:T(8,128)(2,1)S(1)}, bf16[96,1152]{1,0:T(8,128)(2,1)S(1)}, u32[]{:S(2)}, u32[]{:S(2)}) collective-permute-start(bf16[96,1152]{1,0:T(8,128)(2,1)S(1)} %slice_bitcast_fusion.2), channel_id=1, source_target_pairs={{0,16},{4,20},{8,24},{12,28},{16,0},{20,4},{24,8},{28,12},{1,17},{... | collective-permute-start | bytes 663560 | tf_op jit(solution)/shard_map/ppermute | solution.py:1077
  282.2 6.7 %collective-permute-start.10 = (bf16[96,1152]{1,0:T(8,128)(2,1)S(1)}, bf16[96,1152]{1,0:T(8,128)(2,1)S(1)}, u32[]{:S(2)}, u32[]{:S(2)}) collective-permute-start(bf16[96,1152]{1,0:T(8,128)(2,1)S(1)} %slice_bitcast_fusion), channel_id=1, source_target_pairs={{0,8},{4,12},{8,0},{12,4},{16,24},{20,28},{24,16},{28,20},{1,9},{5... | collective-permute-start | bytes 663560 | tf_op jit(solution)/shard_map/ppermute | solution.py:1077
  289.0 10.3 %collective-permute-start.11 = (bf16[96,2304]{1,0:T(8,128)(2,1)S(1)}, bf16[96,2304]{1,0:T(8,128)(2,1)S(1)}, u32[]{:S(2)}, u32[]{:S(2)}) collective-permute-start(bf16[96,2304]{1,0:T(8,128)(2,1)S(1)} %pad_maximum_fusion), channel_id=1, source_target_pairs={{0,1},{3,2},{4,5},{7,6},{8,9},{11,10},{12,13},{15,14},{16,17},{19,... | collective-permute-start | bytes 1327112 | tf_op jit(solution)/shard_map/ppermute | solution.py:1089
  290.5 3.8 %collective-permute-start.2 = (f32[3072]{0:T(1024)S(1)}, f32[3072]{0:T(1024)S(1)}, u32[]{:S(2)}, u32[]{:S(2)}) collective-permute-start(f32[3072]{0:T(1024)S(1)} %fusion.41), channel_id=1, source_target_pairs={{0,8},{4,12},{8,0},{12,4},{16,24},{20,28},{24,16},{28,20},{1,9},{5... | collective-permute-start | bytes 36872 | tf_op jit(solution)/shard_map/ppermute | solution.py:1077
  291.9 6.0 %collective-permute-start.15 = (f32[6144]{0:T(1024)S(1)}, f32[6144]{0:T(1024)S(1)}, u32[]{:S(2)}, u32[]{:S(2)}) collective-permute-start(f32[6144]{0:T(1024)S(1)} %add.240), channel_id=1, source_target_pairs={{0,8},{4,12},{8,0},{12,4},{16,24},{20,28},{24,16},{28,20},{1,9},{5... | collective-permute-start | bytes 73736 | tf_op jit(solution)/shard_map/ppermute | solution.py:1077
  294.2 3.7 %collective-permute-start.3 = (f32[3072]{0:T(1024)S(1)}, f32[3072]{0:T(1024)S(1)}, u32[]{:S(2)}, u32[]{:S(2)}) collective-permute-start(f32[3072]{0:T(1024)S(1)} %add.224), channel_id=1, source_target_pairs={{0,16},{4,20},{8,24},{12,28},{16,0},{20,4},{24,8},{28,12},{1,17},{... | collective-permute-start | bytes 36872 | tf_op jit(solution)/shard_map/ppermute | solution.py:1077
  297.9 3.7 %collective-permute-start.4 = (f32[3072]{0:T(1024)S(1)}, f32[3072]{0:T(1024)S(1)}, u32[]{:S(2)}, u32[]{:S(2)}) collective-permute-start(f32[3072]{0:T(1024)S(1)} %add.225), channel_id=1, source_target_pairs={{0,1},{1,0},{2,3},{3,2},{4,5},{5,4},{6,7},{7,6},{8,9},{9,8},{10,11... | collective-permute-start | bytes 36872 | tf_op jit(solution)/shard_map/ppermute | solution.py:1100
  297.9 7.7 %collective-permute-start.16 = (f32[6144]{0:T(1024)S(1)}, f32[6144]{0:T(1024)S(1)}, u32[]{:S(2)}, u32[]{:S(2)}) collective-permute-start(f32[6144]{0:T(1024)S(1)} %add.241), channel_id=1, source_target_pairs={{0,16},{4,20},{8,24},{12,28},{16,0},{20,4},{24,8},{28,12},{1,17},{... | collective-permute-start | bytes 73736 | tf_op jit(solution)/shard_map/ppermute | solution.py:1077
  300.2 22.5 %collective-permute-start.12 = (bf16[96,2304]{1,0:T(8,128)(2,1)}, bf16[96,2304]{1,0:T(8,128)(2,1)}, u32[]{:S(2)}, u32[]{:S(2)}) collective-permute-start(bf16[96,2304]{1,0:T(8,128)(2,1)} %add_convert_fusion.4), channel_id=1, source_target_pairs={{1,2},{2,1},{5,6},{6,5},{9,10},{10,9},{13,14},{14,13},{17,18},{18,... | collective-permute-start | bytes 1327112 | tf_op jit(solution)/shard_map/ppermute | solution.py:1090
  301.6 20.9 %collective-permute-start.5 = (f32[3072]{0:T(1024)S(1)}, f32[3072]{0:T(1024)S(1)}, u32[]{:S(2)}, u32[]{:S(2)}) collective-permute-start(f32[3072]{0:T(1024)S(1)} %add.226), channel_id=1, source_target_pairs={{0,2},{1,3},{2,0},{3,1},{4,6},{5,7},{6,4},{7,5},{8,10},{9,11},{10,... | collective-permute-start | bytes 36872 | tf_op jit(solution)/shard_map/ppermute | solution.py:1100
  305.7 16.9 %collective-permute-start.17 = (f32[6144]{0:T(1024)S(1)}, f32[6144]{0:T(1024)S(1)}, u32[]{:S(2)}, u32[]{:S(2)}) collective-permute-start(f32[6144]{0:T(1024)S(1)} %add.242), channel_id=1, source_target_pairs={{0,1},{1,0},{2,3},{3,2},{4,5},{5,4},{6,7},{7,6},{8,9},{9,8},{10,11... | collective-permute-start | bytes 73736 | tf_op jit(solution)/shard_map/ppermute | solution.py:1100
  306.4 26.5 %collective-permute-start = (bf16[512,768]{1,0:T(8,128)(2,1)S(1)}, bf16[512,768]{1,0:T(8,128)(2,1)S(1)}, u32[]{:S(2)}, u32[]{:S(2)}) collective-permute-start(bf16[512,768]{1,0:T(8,128)(2,1)S(1)} %fusion.15), channel_id=1, source_target_pairs={{2,4},{3,5},{4,2},{5,3},{10,12},{11,13},{12,10},{13,11},{18,20},{1... | collective-permute-start | bytes 2359304 | tf_op jit(solution)/shard_map/ppermute | solution.py:1034
  322.6 8.9 %collective-permute-start.18 = (f32[6144]{0:T(1024)S(1)}, f32[6144]{0:T(1024)S(1)}, u32[]{:S(2)}, u32[]{:S(2)}) collective-permute-start(f32[6144]{0:T(1024)S(1)} %add.243), channel_id=1, source_target_pairs={{0,2},{1,3},{2,0},{3,1},{4,6},{5,7},{6,4},{7,5},{8,10},{9,11},{10,... | collective-permute-start | bytes 73736 | tf_op jit(solution)/shard_map/ppermute | solution.py:1100
  323.9 12.3 %collective-permute-start.13 = (bf16[96,2304]{1,0:T(8,128)(2,1)S(1)}, bf16[96,2304]{1,0:T(8,128)(2,1)S(1)}, u32[]{:S(2)}, u32[]{:S(2)}) collective-permute-start(bf16[96,2304]{1,0:T(8,128)(2,1)S(1)} %add_convert_fusion.3), channel_id=1, source_target_pairs={{1,0},{2,3},{5,4},{6,7},{9,8},{10,11},{13,12},{14,15},{17,16},{18,... | collective-permute-start | bytes 1327112 | tf_op jit(solution)/shard_map/ppermute | solution.py:1091
  332.8 4.5 %copy-start.11 = (bf16[512,768]{1,0:T(8,128)(2,1)S(1)}, bf16[512,768]{1,0:T(8,128)(2,1)}, u32[]{:S(2)}) copy-start(bf16[512,768]{1,0:T(8,128)(2,1)} %get-tuple-element.104) | copy-start | bytes 2359300
  333.8 4.3 %copy-start.14 = (f32[96,768]{1,0:T(8,128)S(1)}, f32[96,768]{1,0:T(8,128)}, u32[]{:S(2)}) copy-start(f32[96,768]{1,0:T(8,128)} %get-tuple-element.111) | copy-start | bytes 884740
  333.8 5.1 %copy-start.9 = (f32[96,3072]{1,0:T(8,128)S(1)}, f32[96,3072]{1,0:T(8,128)}, u32[]{:S(2)}) copy-start(f32[96,3072]{1,0:T(8,128)} %get-tuple-element.115) | copy-start | bytes 3538948
  338.1 1.7 copy-start.8
  338.9 2.0 copy-start.1
  (2 other events, 1.4 us)

commit v2 on v1

--- a/solution.py
+++ b/solution.py
@@ -370,11 +370,10 @@
             pltpu.SemaphoreType.DMA((8,)),
         ]
 
-    def bind(self, keep_refs, send_refs, out_refs, scratch, devices):
+    def bind(self, refs, out_refs, scratch, devices):
         at = (pl.ds(*self.rows), pl.ds(*self.columns))
-        whole = (pl.ds(0, 4),) + at
-        keep_hbm = keep_refs[self.source].at[whole]
-        send_hbm = send_refs[self.source].at[whole]
+        keep_hbm = refs[self.source].at[(pl.ds(0, 4),) + at]
+        send_hbm = refs[self.source].at[(pl.ds(4, 4),) + at]
         self.out = out_refs[self.source].at[at]
         (self.keep, core, first, second, self.z1, self.z2, self.z3, sent, landed) = scratch
         near, far = (devices["y"], devices["x"]) if self.y_first else (devices["x"], devices["y"])
@@ -519,12 +518,9 @@
     mark_k,
     mark_q,
     lse_ref,
-    keep_down,
-    send_down,
-    keep_up,
-    send_up,
-    keep_out,
-    send_out,
+    grad_down,
+    grad_up,
+    grad_out,
     block_ref,
     dq_ref,
     dk_ref,
@@ -548,8 +544,7 @@
     per = len(scratch) // len(chunks)
     for chunk in chunks:
         chunk.bind(
-            (keep_down, keep_up, keep_out),
-            (send_down, send_up, send_out),
+            (grad_down, grad_up, grad_out),
             (down_ref, up_ref, out_ref),
             scratch[chunk.index * per : (chunk.index + 1) * per],
             devices,
@@ -730,10 +725,10 @@
     return dk.astype(BF16), jnp.where(first, dvs[0], dvs[1]).astype(BF16)
 
 
-def backward(chances, grad, attended, projected, mark_k, mark_q, log_totals, halves, block_out):
+def backward(chances, grad, attended, projected, mark_k, mark_q, log_totals, totals, block_out):
     rows, width = grad.shape
     length, pairs = projected.shape[0], width // LANES
-    shapes = [keep.shape for keep, _ in halves]
+    shapes = [total.shape for total in totals]
     anywhere = pl.BlockSpec(memory_space=pl.ANY)
     result = jax.ShapeDtypeStruct((rows, width), BF16)
     reduced = [jax.ShapeDtypeStruct(shape[1:], F32) for shape in shapes]
@@ -767,7 +762,7 @@
             once(mark_q),
             once(log_totals),
         ]
-        + [anywhere] * (2 * len(halves) + 1),
+        + [anywhere] * (len(totals) + 1),
         [pl.BlockSpec((rows, LANES), lambda t: (0, jnp.minimum(t, pairs - 1))), late, late]
         + [once(shape) for shape in reduced]
         + [anywhere],
@@ -794,8 +789,225 @@
         mark_k,
         mark_q,
         log_totals,
-        *[array for pair in halves for array in pair],
+        *totals,
         block_out,
+    )
+
+
+def gelu_parts(pre_act):
+    inside = 0.5 * (1.0 + lax.erf(pre_act * math.sqrt(0.5)))
+    slope = inside + pre_act * jnp.exp(-0.5 * pre_act * pre_act) * (1.0 / math.sqrt(2.0 * math.pi))
+    return pre_act * inside, slope
+
+
+def relative(block, me):
+    turned = block ^ me
+    return (turned % 2) * 4 + turned // 2
+
+
+def feed_kernel(
+    sub,
+    index_ref,
+    here_ref,
+    attended_ref,
+    grad_ref,
+    w_out_ref,
+    bias_out_ref,
+    gain_ref,
+    shift_ref,
+    w_up_ref,
+    bias_up_ref,
+    w_down_ref,
+    bias_down_ref,
+    block_ref,
+    grad_attended_ref,
+    grad_middle_ref,
+    down_ref,
+    up_ref,
+    out_ref,
+    sum_up_ref,
+    sums_ref,
+    middle,
+    normed,
+    inverse,
+    hidden,
+    turned,
+    total,
+    grad_hidden,
+    activated,
+    grad_upper,
+):
+    step, last = pl.program_id(0), pl.num_programs(0) - 1
+    me = index_ref[0]
+    rows, width = here_ref.shape
+    blocks = rows // sub
+
+    def span(i):
+        return pl.ds(pl.multiple_of(i * sub, sub), sub)
+
+    @pl.when(step == 0)
+    def _():
+        def norm(i, carry):
+            at = span(i)
+            values = (
+                here_ref[at, :].astype(F32)
+                + dot_as(attended_ref[at, :], w_out_ref[...], NN)
+                + bias_out_ref[...]
+            )
+            out, unit, root = layer_norm(values, gain_ref[...], shift_ref[...])
+            middle[at, :] = values
+            normed[at, :] = unit
+            inverse[at, :] = jnp.broadcast_to(root, (sub, LANES))
+            hidden[at, :] = out.astype(BF16)
+            total[at, :] = values + bias_down_ref[...]
+            grad_hidden[at, :] = jnp.zeros((sub, width), F32)
+            return carry
+
+        lax.fori_loop(0, blocks, norm, 0)
+        turned[...] = jnp.transpose(hidden[...])
+
+    def tile(i, carry):
+        at = span(i)
+        upper = dot_as(hidden[at, :], w_up_ref[...], NN) + bias_up_ref[...]
+        grad_activated = dot_as(grad_ref[at, :], w_down_ref[...], NT)
+        active, slope = gelu_parts(upper)
+        active = active.astype(BF16)
+        grad_in = (grad_activated * slope).astype(BF16)
+        activated[at, :] = active
+        grad_upper[at, :] = grad_in
+        total[at, :] += dot_as(active, w_down_ref[...], NN)
+        grad_hidden[at, :] += dot_as(grad_in, w_up_ref[...], NT)
+        return carry + jnp.sum(grad_in.astype(F32), 0, keepdims=True)
+
+    sum_up_ref[...] = lax.fori_loop(0, blocks, tile, jnp.zeros(sum_up_ref.shape, F32))
+
+    grad_up = dot_as(turned[...], grad_upper[...], NN)
+    part = width // 8
+    for block in range(8):
+        up_ref[relative(block, me)] = grad_up[block * part : (block + 1) * part].astype(BF16)
+    grad_down = inner_rows(activated[...], grad_ref[...])
+    part = down_ref.shape[2]
+    for i in range(2):
+        down_ref[(i ^ me) % 2, 0] = grad_down[i * part : (i + 1) * part].astype(BF16)
+
+    @pl.when(step == last)
+    def _():
+        def norm(i, carry):
+            at = span(i)
+            block_ref[at, :] = total[at, :].astype(BF16)
+            grad, unit = grad_hidden[at, :], normed[at, :]
+            scaled = grad * gain_ref[...]
+            grad_in = inverse[at, 0:1] * (
+                scaled
+                - jnp.mean(scaled, -1, keepdims=True)
+                - unit * jnp.mean(scaled * unit, -1, keepdims=True)
+            )
+            before = grad_ref[at, :].astype(F32)
+            grad_in = before + grad_in
+            branch = grad_in.astype(BF16)
+            grad_middle_ref[at, :] = grad_in
+            hidden[at, :] = branch
+            grad_attended_ref[at, :] = dot_as(branch, w_out_ref[...], NT).astype(BF16)
+            sums = [grad * unit, grad, branch.astype(F32), before]
+            return tuple(
+                old + jnp.sum(value, 0, keepdims=True) for old, value in zip(carry, sums)
+            )
+
+        zero = jnp.zeros((1, width), F32)
+        sums = lax.fori_loop(0, blocks, norm, (zero,) * 4)
+        sums_ref[...] = jnp.concatenate(list(sums) + [zero] * 4, 0)
+        grad_out = inner_rows(attended_ref[...], hidden[...])
+        part = width // 8
+        for block in range(8):
+            out_ref[relative(block, me)] = grad_out[block * part : (block + 1) * part].astype(BF16)
+
+
+def feed(
+    here, attended, grad, w_out, bias_out, gain, shift, w_up, bias_up, w_down, bias_down, me, sub=256
+):
+    rows, width = here.shape
+    wide = w_up.shape[1]
+    steps = 4
+    tile = wide // steps
+    part = width // 8
+
+    def row(vector):
+        return vector.reshape(1, -1)
+
+    def once(*shape):
+        return pl.BlockSpec(shape, lambda f, at: (0,) * len(shape), pipeline_mode=pl.Buffered(1))
+
+    act = once(rows, width)
+    line = once(1, width)
+    outs = [
+        jax.ShapeDtypeStruct((rows, width), BF16),
+        jax.ShapeDtypeStruct((rows, width), BF16),
+        jax.ShapeDtypeStruct((rows, width), F32),
+        jax.ShapeDtypeStruct((2, 4, wide // 8, width), BF16),
+        jax.ShapeDtypeStruct((8, part, wide), BF16),
+        jax.ShapeDtypeStruct((8, part, width), BF16),
+        jax.ShapeDtypeStruct((1, wide), F32),
+        jax.ShapeDtypeStruct((8, width), F32),
+    ]
+    return pl.pallas_call(
+        functools.partial(feed_kernel, sub),
+        grid_spec=pltpu.PrefetchScalarGridSpec(
+            num_scalar_prefetch=1,
+            grid=(steps,),
+            in_specs=[
+                act,
+                act,
+                act,
+                once(width, width),
+                line,
+                line,
+                line,
+                pl.BlockSpec((width, tile), lambda f, at: (0, f)),
+                pl.BlockSpec((1, tile), lambda f, at: (0, f)),
+                pl.BlockSpec((tile, width), lambda f, at: (f, 0)),
+                line,
+            ],
+            out_specs=[
+                act,
+                act,
+                act,
+                pl.BlockSpec((2, 1, wide // 8, width), lambda f, at: (0, f ^ (at[0] // 2), 0, 0)),
+                pl.BlockSpec((8, part, tile), lambda f, at: (0, 0, f)),
+                once(8, part, width),
+                pl.BlockSpec((1, tile), lambda f, at: (0, f)),
+                once(8, width),
+            ],
+            scratch_shapes=[
+                pltpu.VMEM((rows, width), F32),
+                pltpu.VMEM((rows, width), F32),
+                pltpu.VMEM((rows, LANES), F32),
+                pltpu.VMEM((rows, width), BF16),
+                pltpu.VMEM((width, rows), BF16),
+                pltpu.VMEM((rows, width), F32),
+                pltpu.VMEM((rows, width), F32),
+                pltpu.VMEM((rows, tile), BF16),
+                pltpu.VMEM((rows, tile), BF16),
+            ],
+        ),
+        out_shape=outs,
+        compiler_params=pltpu.CompilerParams(vmem_limit_bytes=VMEM_BYTES),
+        cost_estimate=pl.CostEstimate(
+            flops=12 * rows * width * wide, bytes_accessed=8 * width * wide, transcendentals=0
+        ),
+        name="feed",
+    )(
+        me,
+        here,
+        attended,
+        grad,
+        w_out,
+        row(bias_out),
+        row(gain),
+        row(shift),
+        w_up,
+        row(bias_up),
+        w_down,
+        row(bias_down),
     )
 
 
@@ -1050,8 +1262,14 @@
     def own(self, gathered):
         return gathered[: gathered.shape[0] // 4]
 
+    def feed(self, *args):
+        me = lax.axis_index("dp").astype(jnp.int32).reshape(1)
+        block_out, grad_attended, grad_middle, down, up, out, sum_up, sums = feed(*args, me)
+        totals = [down.reshape((8,) + down.shape[2:]), up, out]
+        return block_out, grad_attended, grad_middle, totals, [*sums[:4], sum_up[0]]
+
     def backward(
-        self, chances, grad, attended, projected, own, mark_k, mark_q, log_totals, halves, block_out
+        self, chances, grad, attended, projected, own, mark_k, mark_q, log_totals, totals, block_out
     ):
         dq, dk, dv, down, up, out, home = backward(
             chances,
@@ -1061,7 +1279,7 @@
             self.own(mark_k),
             mark_q,
             log_totals,
-            halves,
+            totals,
             block_out,
         )
         return dq, dk, dv, (down, up, out), home
@@ -1135,7 +1353,7 @@
         return lax.dynamic_slice_in_dim(gathered, lax.axis_index("seq") * rows, rows, 0)
 
     def backward(
-        self, chances, grad, attended, projected, own, mark_k, mark_q, log_totals, halves, block_out
+        self, chances, grad, attended, projected, own, mark_k, mark_q, log_totals, totals, block_out
     ):
         dq, deltas = grad_query(chances, grad, attended, projected)
         dk, dv = grad_key_value(
@@ -1147,7 +1365,43 @@
             self.own(mark_k),
             mark_q,
         )
-        return dq, dk, dv, [self.reduce(total) for total in halves], block_out
+        return dq, dk, dv, [self.reduce(total) for total in totals], block_out
+
+    def feed(
+        self,
+        here,
+        attended,
+        grad_out,
+        w_out,
+        bias_out,
+        gain,
+        shift,
+        w_up,
+        bias_up,
+        w_down,
+        bias_down,
+    ):
+        middle = here.astype(F32) + matmul(attended, w_out) + bias_out
+        normed_out, normed, inverse = layer_norm(middle, gain, shift)
+        hidden = normed_out.astype(BF16)
+        activated, slope = gelu_parts(matmul(hidden, w_up) + bias_up)
+        activated = activated.astype(BF16)
+        grad_upper = (inner_cols(grad_out, w_down) * slope).astype(BF16)
+        grad_hidden = inner_cols(grad_upper, w_up)
+        grad_norm, grad_gain, grad_shift = norm_back(grad_hidden, normed, inverse, gain)
+        grad_middle = grad_out.astype(F32) + grad_norm
+        grad_branch = grad_middle.astype(BF16)
+        grad_attended = inner_cols(grad_branch, w_out).astype(BF16)
+        block_out = (middle + matmul(activated, w_down) + bias_down).astype(BF16)
+        totals = [
+            inner_rows(activated, grad_out),
+            inner_rows(hidden, grad_upper),
+            inner_rows(attended, grad_branch),
+        ]
+        vectors = [grad_gain, grad_shift] + [
+            jnp.sum(value.astype(F32), 0) for value in (grad_branch, grad_out, grad_upper)
+        ]
+        return block_out, grad_attended, grad_middle, totals, vectors
 
     def weight(self, left, right):
         return inner_rows(left, right)
@@ -1157,12 +1411,6 @@
 
     def reduce_vectors(self, vectors):
         return [self.reduce(vector) for vector in vectors]
-
-
-def gelu_parts(pre_act):
-    inside = 0.5 * (1.0 + lax.erf(pre_act * math.sqrt(0.5)))
-    slope = inside + pre_act * jnp.exp(-0.5 * pre_act * pre_act) * (1.0 / math.sqrt(2.0 * math.pi))
-    return pre_act * inside, slope
 
 
 def body(
@@ -1202,33 +1450,21 @@
         plan, own, projected, plan.own(mark_q), mark_k, cotangent
     )
 
-    inputs32 = here.astype(F32)
-    middle = inputs32 + matmul(attended, w_out) + bias_out
-    normed2_out, normed2, inverse2 = layer_norm(middle, ln2_gain, ln2_shift)
-    hidden2 = normed2_out.astype(BF16)
-    upper = matmul(hidden2, w_up) + bias_up
-    activated, slope = gelu_parts(upper)
-    activated = activated.astype(BF16)
-    grad_upper = (inner_cols(grad_out, w_down) * slope).astype(BF16)
-    grad_hidden2 = inner_cols(grad_upper, w_up)
-    grad_norm2, grad_ln2_gain, grad_ln2_shift = norm_back(grad_hidden2, normed2, inverse2, ln2_gain)
-    grad_middle = grad_out.astype(F32) + grad_norm2
-    grad_branch = grad_middle.astype(BF16)
-    grad_attended = inner_cols(grad_branch, w_out).astype(BF16)
-
-    block_out = (middle + matmul(activated, w_down) + bias_down).astype(BF16)
-    halves = [
-        plan.weight(activated, grad_out),
-        plan.weight(hidden2, grad_upper),
-        plan.weight(attended, grad_branch),
-    ]
-    grad_bias_down = jnp.sum(grad_out.astype(F32), 0)
-    grad_bias_up = jnp.sum(grad_upper.astype(F32), 0)
-    grad_bias_out = jnp.sum(grad_branch.astype(F32), 0)
-    grad_bias_down, grad_bias_up, grad_bias_out, grad_ln2_gain, grad_ln2_shift = (
-        plan.reduce_vectors(
-            [grad_bias_down, grad_bias_up, grad_bias_out, grad_ln2_gain, grad_ln2_shift]
-        )
+    block_out, grad_attended, grad_middle, totals, vectors = plan.feed(
+        here,
+        attended,
+        grad_out,
+        w_out,
+        bias_out,
+        ln2_gain,
+        ln2_shift,
+        w_up,
+        bias_up,
+        w_down,
+        bias_down,
+    )
+    grad_ln2_gain, grad_ln2_shift, grad_bias_out, grad_bias_down, grad_bias_up = (
+        plan.reduce_vectors(vectors)
     )
 
     dq, dk, dv, (grad_w_down, grad_w_up, grad_w_out), block_out = plan.backward(
@@ -1240,7 +1476,7 @@
         mark_k,
         mark_q,
         log_totals,
-        halves,
+        totals,
         block_out,
     )
     grad_projected = jnp.concatenate([dq, dk, dv], 1)
@@ -1248,7 +1484,7 @@
     grad_bias_query = jnp.sum(dq.astype(F32), 0)
     grad_bias_value = jnp.sum(dv.astype(F32), 0)
     grad_hidden1 = inner_cols(grad_projected, w_qkv)
-    _, normed1, inverse1 = layer_norm(inputs32, ln1_gain, ln1_shift)
+    _, normed1, inverse1 = layer_norm(here.astype(F32), ln1_gain, ln1_shift)
     grad_norm1, grad_ln1_gain, grad_ln1_shift = norm_back(grad_hidden1, normed1, inverse1, ln1_gain)
     grad_tokens = plan.to_home((grad_middle + grad_norm1).astype(BF16))
     grad_bias_query, grad_bias_value, grad_ln1_gain, grad_ln1_shift = plan.reduce_vectors(

time: 342 us -> 316 us (0.924)
  matrix products: 28 us -> 2.35 us
  other arithmetic: 13.3 us -> 7.77 us
  Pallas kernels: 215 us -> 219 us
    dot_general x7 -> x1, matrix products: 28 us -> 2.35 us  [dot_as(): return lax.dot_general(left, right, dims, preferred_element_type=F32)]
    pallas_call x2 -> x1, Pallas kernels: 9.99 us -> 27.6 us  [feed(): pl.pallas_call(functools.partial(feed_kernel, sub), grid_spec=pltpu.Prefe...]
    pallas_call x3 -> x1, Pallas kernels: 21.8 us -> 8.03 us  [grad_weight_wide(): pl.pallas_call(functools.partial(grad_weight_kernel, parts), grid_spec=pl...]
    unnamed x72 -> x54, local copies, waits for them, and re-layouts: 7.24 us -> 6.71 us
  transfers between devices with their start and end apart: 19 -> 19, of which waited for: 10 -> 11; matrix products, arithmetic and copies ran while one was open for 4% -> 3% of each run, Pallas kernels for 0% -> 0%
where the time goes in v2:
time: 316 us; the launch traced here: 315 us
  Pallas kernels  219 us (69%)
  waiting for transfers between devices  47.5 us (15%)
  starting transfers between devices  21.7 us (7%)
  local copies, waits for them, and re-layouts  15.7 us (5%)
  other arithmetic  7.77 us (2%)
    pallas_call x1, Pallas kernels, backward(): kernel_call(functools.partial(backward_kernel, shapes, pairs), 'backward'...  110 us
    pallas_call x1, Pallas kernels, start_work(): pl.pallas_call(start_kernel, in_specs=[anywhere] + [vmem] * 5, out_specs=...  38.8 us
    pallas_call x1, Pallas kernels, attend(): kernel_call(functools.partial(attend_kernel, sub, ways), 'attend', (pairs...  34.1 us
    pallas_call x1, Pallas kernels, feed(): pl.pallas_call(functools.partial(feed_kernel, sub), grid_spec=pltpu.Prefe...  27.6 us
    ppermute x4, waiting for transfers between devices, reduce_vectors(): lax.ppermute(packed, 'seq', [(i, i ^ bit) for i in range(4)])  23.8 us
    ppermute x11, waiting for transfers between devices, swap(): return lax.ppermute(value, 'dp', [(i, i ^ bit) for i in range(8)])  21.3 us
    ppermute x11, starting transfers between devices, swap(): return lax.ppermute(value, 'dp', [(i, i ^ bit) for i in range(8)])  14.2 us
    pallas_call x1, Pallas kernels, grad_weight_wide(): pl.pallas_call(functools.partial(grad_weight_kernel, parts), grid_spec=pl...  8.03 us
  transfers between devices with their start and end apart: 19, of which 11 were waited for; matrix products, arithmetic and copies ran while one was open for 3% of the time, Pallas kernels for 0%

profile of v2, /device:TPU:0, one launch (start us, length us, event | category | flops | bytes accessed | tf_op | source)
XLA Modules:
  0.0 315.2 jit_solution(7561647776302541446)
XLA Ops:
  0.7 0.7 pad_maximum_fusion.1
  1.5 0.6 reshape.120.bias_ref
  2.1 1.3 reshape.118.gain_ref
  3.3 1.3 reshape.119.shift_ref
  4.6 38.8 %start_work.1 = (bf16[2048,2304]{1,0:T(8,128)(2,1)}, bf16[512,768]{1,0:T(8,128)(2,1)}, bf16[512,768]{1,0:T(8,128)(2,1)}, s32[1,4]{1,0:T(1,128)}) custom-call(bf16[512,768]{1,0:T(8,128)(2,1)} %tokens_ref.1, s32[1,4]{1,0:T(1,128)} %lengths_ref.1, f32[1,768]{1,0:T(1,128)} %reshape.118.gain_ref, f32[1,768]{1,0:T(1,128)} %reshape.119.shift_ref, ...), custom_call_target="tpu_custom_call" | custom-call | flops 7247757312 | bytes 12582912 | tf_op jit(solution)/shard_map/start_work/pallas_call | solution.py:1198
  44.5 0.7 slice.52.mark_q
  47.6 0.7 slice.53.mark_k
  48.3 34.1 %attend.1 = (bf16[512,768]{1,0:T(8,128)(2,1)}, bf16[12,512,2048]{2,1,0:T(8,128)(2,1)}, f32[16,512]{1,0:T(8,128)}, bf16[512,768]{1,0:T(8,128)(2,1)}) custom-call(bf16[2048,2304]{1,0:T(8,128)(2,1)} %get-tuple-element.40.q_ref.k_ref.v_ref, bf16[2048,2304]{1,0:T(8,128)(2,1)} %get-tuple-element.40.q_ref.k_ref.v_ref, ...), custom_call_target="tpu_custom_call" | custom-call | flops 19327352832 | bytes 25165824 | tf_op jit(solution)/shard_map/attend/pallas_call | solution.py:276
  82.4 27.6 %feed.1 = (bf16[512,768]{1,0:T(8,128)(2,1)}, bf16[512,768]{1,0:T(8,128)(2,1)}, f32[512,768]{1,0:T(8,128)}, bf16[2,4,384,768]{3,2,1,0:T(8,128)(2,1)}, bf16[8,96,3...) custom-call(s32[1]{0:T(128)} %bitcast.2.index_ref, ...), custom_call_target="tpu_custom_call" | custom-call | flops 14495514624 | bytes 18874368 | tf_op jit(solution)/shard_map/feed/pallas_call | solution.py:952
  110.0 110.3 %backward.1 = (bf16[512,768]{1,0:T(8,128)(2,1)}, bf16[512,768]{1,0:T(8,128)(2,1)}, bf16[512,768]{1,0:T(8,128)(2,1)}, f32[384,768]{1,0:T(8,128)}, f32[96,3072]{1,...) custom-call(bf16[12,512,2048]{2,1,0:T(8,128)(2,1)} %get-tuple-element.42.chance_ref, ...), custom_call_target="tpu_custom_call" | custom-call | flops 38654705664 | bytes 25165824 | tf_op jit(solution)/shard_map/backward/pallas_call | solution.py:750
  220.4 1.3 constant_dynamic-update-slice_fusion.2
  222.0 1.4 copy-done.11
  223.4 8.0 %grad_weight_wide.1 = (bf16[4,96,2304]{2,1,0:T(8,128)(2,1)}, bf16[4,96,2304]{2,1,0:T(8,128)(2,1)}) custom-call(s32[1]{0:T(128)} %bitcast.2.index_ref, bf16[512,768]{1,0:T(8,128)(2,1)} %get-tuple-element.57.left_ref, bf16[512,2304]{1,0:T(8,128)(2,1)} %copy-done.11), custom_call_target="tpu_custom_call" | custom-call | flops 1811939328 | bytes 3538944 | tf_op jit(solution)/shard_map/grad_weight_wide/pallas_call | solution.py:1041
  232.7 2.7 collective-permute-done.6
  235.4 2.0 add_convert_fusion
  237.6 3.9 %collective-permute-start.7 = (bf16[2,96,1152]{2,1,0:T(8,128)(2,1)S(1)}, bf16[2,96,1152]{2,1,0:T(8,128)(2,1)S(1)}, u32[]{:S(2)}, u32[]{:S(2)}) collective-permute-start(bf16[2,96,1152]{2,1,0:T(8,128)(2,1)S(1)} %slice.45), channel_id=1, source_target_pairs={{0,8},{4,12},{8,0},{12,4},{16,24},{20,28},{24,16},{28,20},{1,9},{5... | collective-permute-start | bytes 1327112 | tf_op jit(solution)/shard_map/ppermute | solution.py:1295
  241.5 2.4 fusion.10
  244.3 1.6 collective-permute-start.9
  245.9 6.1 %collective-permute-done.7 = bf16[2,96,1152]{2,1,0:T(8,128)(2,1)S(1)} collective-permute-done((bf16[2,96,1152]{2,1,0:T(8,128)(2,1)S(1)}, bf16[2,96,1152]{2,1,0:T(8,128)(2,1)S(1)}, u32[]{:S(2)}, u32[]{:S(2)}) %collective-permute-start.7) | collective-permute-done | bytes 442400 | tf_op jit(solution)/shard_map/ppermute | solution.py:1295
  252.1 1.6 collective-permute-start.8
  253.7 3.6 %collective-permute-done.9 = bf16[2,96,1152]{2,1,0:T(8,128)(2,1)S(1)} collective-permute-done((bf16[2,96,1152]{2,1,0:T(8,128)(2,1)S(1)}, bf16[2,96,1152]{2,1,0:T(8,128)(2,1)S(1)}, u32[]{:S(2)}, u32[]{:S(2)}) %collective-permute-start.9) | collective-permute-done | bytes 442400 | tf_op jit(solution)/shard_map/ppermute | solution.py:1295
  257.5 1.8 collective-permute-start.10
  259.2 2.4 collective-permute-done.8
  261.7 2.4 collective-permute-done.10
  264.3 1.4 collective-permute-start.11
  265.7 1.5 collective-permute-start.2
  267.2 0.7 collective-permute-start.15
  267.9 1.6 collective-permute-done.2
  269.5 1.2 collective-permute-start.3
  270.7 2.5 collective-permute-done.3
  273.2 1.3 collective-permute-start.16
  274.6 0.7 collective-permute-start.12
  275.3 1.6 collective-permute-done.4
  276.9 3.2 %collective-permute-start.5 = (f32[3072]{0:T(1024)S(1)}, f32[3072]{0:T(1024)S(1)}, u32[]{:S(2)}, u32[]{:S(2)}) collective-permute-start(f32[3072]{0:T(1024)S(1)} %add.166), channel_id=1, source_target_pairs={{0,2},{1,3},{2,0},{3,1},{4,6},{5,7},{6,4},{7,5},{8,10},{9,11},{10,... | collective-permute-start | bytes 36872 | tf_op jit(solution)/shard_map/ppermute | solution.py:1318
  280.2 0.6 fusion.9
  280.8 0.7 collective-permute-start
  281.6 15.3 %collective-permute-done.5 = f32[3072]{0:T(1024)S(1)} collective-permute-done((f32[3072]{0:T(1024)S(1)}, f32[3072]{0:T(1024)S(1)}, u32[]{:S(2)}, u32[]{:S(2)}) %collective-permute-start.5) | collective-permute-done | bytes 12320 | tf_op jit(solution)/shard_map/ppermute | solution.py:1318
  297.1 1.3 collective-permute-start.13
  298.4 0.6 fusion.18
  299.0 6.9 %collective-permute-done.18 = f32[6144]{0:T(1024)S(1)} collective-permute-done((f32[6144]{0:T(1024)S(1)}, f32[6144]{0:T(1024)S(1)}, u32[]{:S(2)}, u32[]{:S(2)}) %collective-permute-start.18) | collective-permute-done | bytes 24608 | tf_op jit(solution)/shard_map/ppermute | solution.py:1318
  306.0 0.7 dynamic_slice.34
  307.2 1.0 broadcast_select_fusion
  308.2 2.4 collective-permute-done.13
  310.6 1.0 select_convert_fusion.1
  311.6 0.9 copy.42
  312.5 0.7 copy.43
  313.2 1.0 copy.44
  314.2 1.0 copy.45
  (112 shorter events, 6.9 us)
Async XLA Ops:
  4.6 38.9 %copy-start.20 = (s32[1,4]{1,0:T(1,128)S(1)}, s32[1,4]{1,0:T(1,128)}, u32[]{:S(2)}) copy-start(s32[1,4]{1,0:T(1,128)} %lengths_ref.1) | copy-start | bytes 52
  4.6 40.7 %copy-start.16 = (f32[768]{0:T(1024)S(1)}, f32[768]{0:T(1024)}, u32[]{:S(2)}) copy-start(f32[768]{0:T(1024)} %param.24) | copy-start | bytes 9220
  4.6 41.2 %copy-start.17 = (f32[768]{0:T(1024)S(1)}, f32[768]{0:T(1024)}, u32[]{:S(2)}) copy-start(f32[768]{0:T(1024)} %param.25) | copy-start | bytes 9220
  4.6 41.8 %copy-start.18 = (f32[768]{0:T(1024)S(1)}, f32[768]{0:T(1024)}, u32[]{:S(2)}) copy-start(f32[768]{0:T(1024)} %param.26) | copy-start | bytes 9220
  4.6 42.4 %copy-start.19 = (f32[768]{0:T(1024)S(1)}, f32[768]{0:T(1024)}, u32[]{:S(2)}) copy-start(f32[768]{0:T(1024)} %param.30) | copy-start | bytes 9220
  44.2 4.1 %copy-start.7 = (bf16[2048,128]{1,0:T(8,128)(2,1)}, bf16[2048,128]{1,0:T(8,128)(2,1)S(1)}, u32[]{:S(2)}) copy-start(bf16[2048,128]{1,0:T(8,128)(2,1)S(1)} %fusion.12.mark_k) | copy-start | bytes 1572868
  44.5 37.9 %copy-start.6 = (bf16[2048,128]{1,0:T(8,128)(2,1)}, bf16[2048,128]{1,0:T(8,128)(2,1)S(1)}, u32[]{:S(2)}) copy-start(bf16[2048,128]{1,0:T(8,128)(2,1)S(1)} %select_convert_fusion.mark_q) | copy-start | bytes 1572868
  220.3 1.4 copy-start.9
  220.4 1.6 copy-start.2
  222.0 1.4 copy-start.11
  223.4 8.0 %copy-start.15 = (f32[8,768]{1,0:T(8,128)S(1)}, f32[8,768]{1,0:T(8,128)}, u32[]{:S(2)}) copy-start(f32[8,768]{1,0:T(8,128)} %get-tuple-element.61) | copy-start | bytes 73732
  223.4 8.1 %copy-start.14 = (f32[1,3072]{1,0:T(1,128)S(1)}, f32[1,3072]{1,0:T(1,128)}, u32[]{:S(2)}) copy-start(f32[1,3072]{1,0:T(1,128)} %get-tuple-element.62) | copy-start | bytes 36868
  223.4 8.7 %copy-start = (bf16[512,768]{1,0:T(8,128)(2,1)S(1)}, bf16[512,768]{1,0:T(8,128)(2,1)}, u32[]{:S(2)}) copy-start(bf16[512,768]{1,0:T(8,128)(2,1)} %get-tuple-element.43.here_ref) | copy-start | bytes 2359300
  231.5 3.9 %collective-permute-start.6 = (bf16[4,96,2304]{2,1,0:T(8,128)(2,1)}, bf16[4,96,2304]{2,1,0:T(8,128)(2,1)S(1)}, u32[]{:S(2)}, u32[]{:S(2)}) collective-permute-start(bf16[4,96,2304]{2,1,0:T(8,128)(2,1)} %get-tuple-element.59), channel_id=1, source_target_pairs={{0,4},{4,0},{8,12},{12,8},{16,20},{20,16},{24,28},{28,24},{1,5},{5... | collective-permute-start | bytes 5308424 | tf_op jit(solution)/shard_map/ppermute | solution.py:1295
  231.6 35.6 %collective-permute-start.14 = (f32[6144]{0:T(1024)S(1)}, f32[6144]{0:T(1024)S(1)}, u32[]{:S(2)}, u32[]{:S(2)}) collective-permute-start(f32[6144]{0:T(1024)S(1)} %constant_dynamic-update-slice_fusion.6), channel_id=1, source_target_pairs={{0,4},{4,0},{8,12},{12,8},{16,20},{20,16},{24,28},{28,24},{1,5},{5... | collective-permute-start | bytes 73736 | tf_op jit(solution)/shard_map/ppermute | solution.py:1295
  235.4 6.1 %copy-start.21 = (bf16[768,2304]{1,0:T(8,128)(2,1)S(1)}, bf16[768,2304]{1,0:T(8,128)(2,1)}, u32[]{:S(2)}) copy-start(bf16[768,2304]{1,0:T(8,128)(2,1)} %w_ref.1) | copy-start | bytes 10616836
  237.4 4.0 %copy-start.12 = (bf16[512,2304]{1,0:T(8,128)(2,1)S(1)}, bf16[512,2304]{1,0:T(8,128)(2,1)}, u32[]{:S(2)}) copy-start(bf16[512,2304]{1,0:T(8,128)(2,1)} %copy-done.11) | copy-start | bytes 7077892
  237.4 4.0 %copy-start.13 = (f32[768]{0:T(1024)S(1)}, f32[768]{0:T(1024)}, u32[]{:S(2)}) copy-start(f32[768]{0:T(1024)} %param.18) | copy-start | bytes 9220
  237.6 6.4 %copy-start.1 = (bf16[512,768]{1,0:T(8,128)(2,1)S(1)}, bf16[512,768]{1,0:T(8,128)(2,1)}, u32[]{:S(2)}) copy-start(bf16[512,768]{1,0:T(8,128)(2,1)} %get-tuple-element.54) | copy-start | bytes 2359300
  237.6 14.4 %collective-permute-start.7 = (bf16[2,96,1152]{2,1,0:T(8,128)(2,1)S(1)}, bf16[2,96,1152]{2,1,0:T(8,128)(2,1)S(1)}, u32[]{:S(2)}, u32[]{:S(2)}) collective-permute-start(bf16[2,96,1152]{2,1,0:T(8,128)(2,1)S(1)} %slice.45), channel_id=1, source_target_pairs={{0,8},{4,12},{8,0},{12,4},{16,24},{20,28},{24,16},{28,20},{1,9},{5... | collective-permute-start | bytes 1327112 | tf_op jit(solution)/shard_map/ppermute | solution.py:1295
  244.2 21.6 %collective-permute-start.1 = (f32[3072]{0:T(1024)S(1)}, f32[3072]{0:T(1024)S(1)}, u32[]{:S(2)}, u32[]{:S(2)}) collective-permute-start(f32[3072]{0:T(1024)S(1)} %pad_maximum_fusion.2), channel_id=1, source_target_pairs={{0,4},{4,0},{8,12},{12,8},{16,20},{20,16},{24,28},{28,24},{1,5},{5... | collective-permute-start | bytes 36872 | tf_op jit(solution)/shard_map/ppermute | solution.py:1295
  244.3 13.0 %collective-permute-start.9 = (bf16[2,96,1152]{2,1,0:T(8,128)(2,1)S(1)}, bf16[2,96,1152]{2,1,0:T(8,128)(2,1)S(1)}, u32[]{:S(2)}, u32[]{:S(2)}) collective-permute-start(bf16[2,96,1152]{2,1,0:T(8,128)(2,1)S(1)} %slice.58), channel_id=1, source_target_pairs={{0,16},{4,20},{8,24},{12,28},{16,0},{20,4},{24,8},{28,12},{1,17},{... | collective-permute-start | bytes 1327112 | tf_op jit(solution)/shard_map/ppermute | solution.py:1295
  252.1 9.6 %collective-permute-start.8 = (bf16[96,1152]{1,0:T(8,128)(2,1)S(1)}, bf16[96,1152]{1,0:T(8,128)(2,1)S(1)}, u32[]{:S(2)}, u32[]{:S(2)}) collective-permute-start(bf16[96,1152]{1,0:T(8,128)(2,1)S(1)} %slice_bitcast_fusion.2), channel_id=1, source_target_pairs={{0,16},{4,20},{8,24},{12,28},{16,0},{20,4},{24,8},{28,12},{1,17},{... | collective-permute-start | bytes 663560 | tf_op jit(solution)/shard_map/ppermute | solution.py:1295
  257.5 6.7 %collective-permute-start.10 = (bf16[96,1152]{1,0:T(8,128)(2,1)S(1)}, bf16[96,1152]{1,0:T(8,128)(2,1)S(1)}, u32[]{:S(2)}, u32[]{:S(2)}) collective-permute-start(bf16[96,1152]{1,0:T(8,128)(2,1)S(1)} %slice_bitcast_fusion), channel_id=1, source_target_pairs={{0,8},{4,12},{8,0},{12,4},{16,24},{20,28},{24,16},{28,20},{1,9},{5... | collective-permute-start | bytes 663560 | tf_op jit(solution)/shard_map/ppermute | solution.py:1295
  261.7 18.5 %copy-start.3 = (f32[512,768]{1,0:T(8,128)S(1)}, f32[512,768]{1,0:T(8,128)}, u32[]{:S(2)}) copy-start(f32[512,768]{1,0:T(8,128)} %get-tuple-element.53) | copy-start | bytes 4718596
  264.3 10.2 %collective-permute-start.11 = (bf16[96,2304]{1,0:T(8,128)(2,1)S(1)}, bf16[96,2304]{1,0:T(8,128)(2,1)S(1)}, u32[]{:S(2)}, u32[]{:S(2)}) collective-permute-start(bf16[96,2304]{1,0:T(8,128)(2,1)S(1)} %pad_maximum_fusion), channel_id=1, source_target_pairs={{0,1},{3,2},{4,5},{7,6},{8,9},{11,10},{12,13},{15,14},{16,17},{19,... | collective-permute-start | bytes 1327112 | tf_op jit(solution)/shard_map/ppermute | solution.py:1307
  265.7 3.8 %collective-permute-start.2 = (f32[3072]{0:T(1024)S(1)}, f32[3072]{0:T(1024)S(1)}, u32[]{:S(2)}, u32[]{:S(2)}) collective-permute-start(f32[3072]{0:T(1024)S(1)} %fusion.21), channel_id=1, source_target_pairs={{0,8},{4,12},{8,0},{12,4},{16,24},{20,28},{24,16},{28,20},{1,9},{5... | collective-permute-start | bytes 36872 | tf_op jit(solution)/shard_map/ppermute | solution.py:1295
  267.2 6.0 %collective-permute-start.15 = (f32[6144]{0:T(1024)S(1)}, f32[6144]{0:T(1024)S(1)}, u32[]{:S(2)}, u32[]{:S(2)}) collective-permute-start(f32[6144]{0:T(1024)S(1)} %add.182), channel_id=1, source_target_pairs={{0,8},{4,12},{8,0},{12,4},{16,24},{20,28},{24,16},{28,20},{1,9},{5... | collective-permute-start | bytes 73736 | tf_op jit(solution)/shard_map/ppermute | solution.py:1295
  269.5 3.7 %collective-permute-start.3 = (f32[3072]{0:T(1024)S(1)}, f32[3072]{0:T(1024)S(1)}, u32[]{:S(2)}, u32[]{:S(2)}) collective-permute-start(f32[3072]{0:T(1024)S(1)} %add.164), channel_id=1, source_target_pairs={{0,16},{4,20},{8,24},{12,28},{16,0},{20,4},{24,8},{28,12},{1,17},{... | collective-permute-start | bytes 36872 | tf_op jit(solution)/shard_map/ppermute | solution.py:1295
  273.2 3.7 %collective-permute-start.4 = (f32[3072]{0:T(1024)S(1)}, f32[3072]{0:T(1024)S(1)}, u32[]{:S(2)}, u32[]{:S(2)}) collective-permute-start(f32[3072]{0:T(1024)S(1)} %add.165), channel_id=1, source_target_pairs={{0,1},{1,0},{2,3},{3,2},{4,5},{5,4},{6,7},{7,6},{8,9},{9,8},{10,11... | collective-permute-start | bytes 36872 | tf_op jit(solution)/shard_map/ppermute | solution.py:1318
  273.2 6.9 %collective-permute-start.16 = (f32[6144]{0:T(1024)S(1)}, f32[6144]{0:T(1024)S(1)}, u32[]{:S(2)}, u32[]{:S(2)}) collective-permute-start(f32[6144]{0:T(1024)S(1)} %add.183), channel_id=1, source_target_pairs={{0,16},{4,20},{8,24},{12,28},{16,0},{20,4},{24,8},{28,12},{1,17},{... | collective-permute-start | bytes 73736 | tf_op jit(solution)/shard_map/ppermute | solution.py:1295
  274.6 22.4 %collective-permute-start.12 = (bf16[96,2304]{1,0:T(8,128)(2,1)S(1)}, bf16[96,2304]{1,0:T(8,128)(2,1)S(1)}, u32[]{:S(2)}, u32[]{:S(2)}) collective-permute-start(bf16[96,2304]{1,0:T(8,128)(2,1)S(1)} %add_convert_fusion.2), channel_id=1, source_target_pairs={{1,2},{2,1},{5,6},{6,5},{9,10},{10,9},{13,14},{14,13},{17,18},{18,... | collective-permute-start | bytes 1327112 | tf_op jit(solution)/shard_map/ppermute | solution.py:1308
  276.9 20.0 %collective-permute-start.5 = (f32[3072]{0:T(1024)S(1)}, f32[3072]{0:T(1024)S(1)}, u32[]{:S(2)}, u32[]{:S(2)}) collective-permute-start(f32[3072]{0:T(1024)S(1)} %add.166), channel_id=1, source_target_pairs={{0,2},{1,3},{2,0},{3,1},{4,6},{5,7},{6,4},{7,5},{8,10},{9,11},{10,... | collective-permute-start | bytes 36872 | tf_op jit(solution)/shard_map/ppermute | solution.py:1318
  280.1 16.8 %collective-permute-start.17 = (f32[6144]{0:T(1024)S(1)}, f32[6144]{0:T(1024)S(1)}, u32[]{:S(2)}, u32[]{:S(2)}) collective-permute-start(f32[6144]{0:T(1024)S(1)} %add.184), channel_id=1, source_target_pairs={{0,1},{1,0},{2,3},{3,2},{4,5},{5,4},{6,7},{7,6},{8,9},{9,8},{10,11... | collective-permute-start | bytes 73736 | tf_op jit(solution)/shard_map/ppermute | solution.py:1318
  280.8 26.4 %collective-permute-start = (bf16[512,768]{1,0:T(8,128)(2,1)S(1)}, bf16[512,768]{1,0:T(8,128)(2,1)S(1)}, u32[]{:S(2)}, u32[]{:S(2)}) collective-permute-start(bf16[512,768]{1,0:T(8,128)(2,1)S(1)} %fusion.9), channel_id=1, source_target_pairs={{2,4},{3,5},{4,2},{5,3},{10,12},{11,13},{12,10},{13,11},{18,20},{1... | collective-permute-start | bytes 2359304 | tf_op jit(solution)/shard_map/ppermute | solution.py:1246
  296.9 9.0 %collective-permute-start.18 = (f32[6144]{0:T(1024)S(1)}, f32[6144]{0:T(1024)S(1)}, u32[]{:S(2)}, u32[]{:S(2)}) collective-permute-start(f32[6144]{0:T(1024)S(1)} %add.185), channel_id=1, source_target_pairs={{0,2},{1,3},{2,0},{3,1},{4,6},{5,7},{6,4},{7,5},{8,10},{9,11},{10,... | collective-permute-start | bytes 73736 | tf_op jit(solution)/shard_map/ppermute | solution.py:1318
  297.1 13.5 %collective-permute-start.13 = (bf16[96,2304]{1,0:T(8,128)(2,1)S(1)}, bf16[96,2304]{1,0:T(8,128)(2,1)S(1)}, u32[]{:S(2)}, u32[]{:S(2)}) collective-permute-start(bf16[96,2304]{1,0:T(8,128)(2,1)S(1)} %add_convert_fusion.1), channel_id=1, source_target_pairs={{1,0},{2,3},{5,4},{6,7},{9,8},{10,11},{13,12},{14,15},{17,16},{18,... | collective-permute-start | bytes 1327112 | tf_op jit(solution)/shard_map/ppermute | solution.py:1309
  307.2 4.4 %copy-start.8 = (bf16[512,768]{1,0:T(8,128)(2,1)S(1)}, bf16[512,768]{1,0:T(8,128)(2,1)}, u32[]{:S(2)}) copy-start(bf16[512,768]{1,0:T(8,128)(2,1)} %get-tuple-element.101) | copy-start | bytes 2359300
  308.2 4.3 %copy-start.10 = (f32[96,768]{1,0:T(8,128)S(1)}, f32[96,768]{1,0:T(8,128)}, u32[]{:S(2)}) copy-start(f32[96,768]{1,0:T(8,128)} %get-tuple-element.108) | copy-start | bytes 884740
  308.2 5.0 %copy-start.5 = (f32[96,3072]{1,0:T(8,128)S(1)}, f32[96,3072]{1,0:T(8,128)}, u32[]{:S(2)}) copy-start(f32[96,3072]{1,0:T(8,128)} %get-tuple-element.112) | copy-start | bytes 3538948
  312.5 1.7 copy-start.4

commit v3 on v2

v3 whole, which is shorter than its diff:
```python
import functools
import math

import jax
import jax.numpy as jnp
from jax import lax
from jax.experimental import pallas as pl
from jax.experimental.pallas import tpu as pltpu
from jax.sharding import PartitionSpec as P

HDIM = 64
LANES = 128
STATS = 16
F32 = jnp.float32
BF16 = jnp.bfloat16
VMEM_BYTES = 56 << 20
NT = (((1,), (1,)), ((), ()))
NN = (((1,), (0,)), ((), ()))

epsilon = 1e-06
masked_score = -1e30


def dot_as(left, right, dims):
    return lax.dot_general(left, right, dims, preferred_element_type=F32)


def matmul(left, right):
    return dot_as(left, right, NN)


def inner_rows(left, right):
    return dot_as(left, right, (((0,), (0,)), ((), ())))


def inner_cols(left, right):
    return dot_as(left, right, NT)


def layer_norm(values, gain, shift):
    center = values - jnp.mean(values, -1, keepdims=True)
    inverse = lax.rsqrt(jnp.mean(center * center, -1, keepdims=True) + epsilon)
    normed = center * inverse
    return (normed * gain + shift, normed, inverse)


def row_of(ref):
    return ref[...].reshape(1, -1)


def norm_back(grad_out, normed, inverse, gain):
    scaled = grad_out * gain
    grad_in = inverse * (
        scaled
        - jnp.mean(scaled, -1, keepdims=True)
        - normed * jnp.mean(scaled * normed, -1, keepdims=True)
    )
    return (grad_in, jnp.sum(grad_out * normed, 0), jnp.sum(grad_out, 0))


def neighbours():
    dp, z = lax.axis_index("dp"), lax.axis_index("seq")
    other = dp + 1 - 2 * lax.rem(dp, jnp.int32(2))
    pair = z + 1 - 2 * lax.rem(z, jnp.int32(2))
    return (other, z), (dp, pair), (other, lax.rem(z + 2, jnp.int32(4)))


def stays():
    dp, z = lax.axis_index("dp"), lax.axis_index("seq")
    return lax.rem(dp, jnp.int32(2)) == lax.div(z, jnp.int32(2))


def greet(devices):
    barrier = pltpu.get_barrier_semaphore()
    for device in devices:
        pl.semaphore_signal(barrier, inc=1, device_id=device, device_id_type=pl.DeviceIdType.MESH)
    pl.semaphore_wait(barrier, len(devices))


def remote(source, target, sent, landed, device):
    return pltpu.make_async_remote_copy(
        src_ref=source,
        dst_ref=target,
        send_sem=sent,
        recv_sem=landed,
        device_id=device,
        device_id_type=pl.DeviceIdType.MESH,
    )


def move_start(source, target, sent, landed):
    swap = neighbours()[2]

    @pl.when(stays())
    def _():
        pltpu.make_async_copy(source, target, landed).start()

    @pl.when(jnp.logical_not(stays()))
    def _():
        remote(source, target, sent, landed, swap).start()


def move_landed(source, target, sent, landed):
    swap = neighbours()[2]

    @pl.when(stays())
    def _():
        pltpu.make_async_copy(source, target, landed).wait()

    @pl.when(jnp.logical_not(stays()))
    def _():
        remote(source, target, sent, landed, swap).wait_recv()


def move_sent(source, target, sent, landed):
    swap = neighbours()[2]

    @pl.when(jnp.logical_not(stays()))
    def _():
        remote(source, target, sent, landed, swap).wait_send()


def two_heads(values):
    lane = lax.broadcasted_iota(jnp.int32, values.shape, 1)
    zero = jnp.zeros_like(values)
    return jnp.concatenate(
        [jnp.where(lane < HDIM, values, zero), jnp.where(lane < HDIM, zero, values)], 0
    )


def own_columns(values):
    rows = values.shape[0] // 2
    lane = lax.broadcasted_iota(jnp.int32, (rows, LANES), 1)
    return jnp.where(lane < HDIM, values[:rows], values[rows:])


def own_rows(values):
    count = values.shape[1] // 2
    return jnp.transpose(jnp.concatenate([values[:HDIM, :count], values[HDIM:, count:]], 0))


def scaled_down(values):
    return values * jnp.asarray(1.0 / math.sqrt(HDIM), values.dtype)


def attend_kernel(ways, q_ref, k_ref, v_ref, mark_q, mark_k, *refs):
    pair = pl.program_id(0)
    if ways is None:
        out_ref, chance_ref, lse_ref = refs
    else:
        home_ref, out_ref, chance_ref, lse_ref, here_ref, sent, landed = refs
        move = (home_ref, here_ref, sent, landed)

        @pl.when(pair == 0)
        def _():
            greet([neighbours()[2]])
            move_start(*move)

    rows = q_ref.shape[0]
    marks = mark_q[...]
    queries = jnp.concatenate(
        [two_heads(scaled_down(q_ref[...])), jnp.concatenate([marks, marks], 0)], 1
    )
    scores = dot_as(jnp.concatenate([k_ref[...], mark_k[...]], 1), queries, NT)
    highest = jnp.max(scores, 0, keepdims=True)
    powers = jnp.exp(scores - highest)
    total = jnp.sum(powers, 0, keepdims=True)
    chances = (powers * (1.0 / total)).astype(BF16)
    chance_ref[0] = chances[:, :rows]
    chance_ref[1] = chances[:, rows:]
    out_ref[...] = own_rows(dot_as(jnp.transpose(v_ref[...]), chances, NN)).astype(BF16)
    log_total = highest + jnp.log(total)
    lse_ref[pl.ds(2 * pair, 1), :] = log_total[:, :rows]
    lse_ref[pl.ds(2 * pair + 1, 1), :] = log_total[:, rows:]

    if ways is not None:

        @pl.when(pair == pl.num_programs(0) - 1)
        def _():
            move_landed(*move)
            move_sent(*move)


def query_grads(chance_ref, grad, keys, values, deltas, sub=1024):
    turned, grads = jnp.transpose(keys), two_heads(grad)
    delta = jnp.concatenate(deltas, 1)
    total = jnp.zeros((LANES, grads.shape[0]), F32)
    for first in range(0, keys.shape[0], sub):
        at = slice(first, first + sub)
        grad_chances = dot_as(values[at], grads, NT)
        chances = jnp.concatenate([chance_ref[0, at, :], chance_ref[1, at, :]], 1)
        scores = (chances.astype(F32) * (grad_chances - delta)).astype(BF16)
        total += dot_as(turned[:, at], scores, NN)
    return scaled_down(own_rows(total)).astype(BF16)


def key_grads(key, value, mark_k, parts):
    rows = key.shape[0]
    keys = jnp.concatenate([two_heads(key), jnp.concatenate([mark_k, mark_k], 0)], 1)
    values = two_heads(value)
    dk = dv = jnp.zeros((2 * rows, LANES), F32)
    for queries, grads, marks, log_totals, deltas in parts:
        scores = dot_as(keys, jnp.concatenate([scaled_down(queries), marks], 1), NT)
        grad_chances = dot_as(values, grads, NT)
        chances, grad_scores = [], []
        for head in range(2):
            at = slice(head * rows, (head + 1) * rows)
            powers = jnp.exp(scores[at] - log_totals[head])
            chances.append(powers.astype(BF16))
            grad_scores.append((powers * (grad_chances[at] - deltas[head])).astype(BF16))
        dv += dot_as(jnp.concatenate(chances, 0), grads, NN)
        dk += dot_as(jnp.concatenate(grad_scores, 0), queries, NN)
    return scaled_down(own_columns(dk)).astype(BF16), own_columns(dv).astype(BF16)


def grad_query_kernel(chance_ref, grad_ref, k_ref, v_ref, delta_ref, dq_ref):
    pair = pl.program_id(0)
    deltas = [delta_ref[pl.ds(2 * pair + head, 1), :] for head in range(2)]
    dq_ref[...] = query_grads(chance_ref, grad_ref[...], k_ref[...], v_ref[...], deltas)


def grad_key_kernel(pieces, k_ref, v_ref, q_ref, *refs):
    g_refs = refs[:pieces]
    lse_refs, delta_refs = refs[pieces : 2 * pieces], refs[2 * pieces : 3 * pieces]
    mark_k, mark_q, dk_ref, dv_ref = refs[3 * pieces :]
    pair = pl.program_id(0)
    rows = g_refs[0].shape[0]
    parts = []
    for i in range(pieces):
        at = pl.ds(i * rows, rows)
        stats = [
            [ref[i][pl.ds(2 * pair + head, 1), :] for head in range(2)]
            for ref in (lse_refs, delta_refs)
        ]
        parts.append((q_ref[at, :], g_refs[i][...], mark_q[at, :], *stats))
    dk_ref[...], dv_ref[...] = key_grads(k_ref[...], v_ref[...], mark_k[...], parts)


def columns(rows, first):
    return pl.BlockSpec((rows, LANES), lambda t: (0, first + t))


def whole(array):
    return pl.BlockSpec(array.shape, lambda t: (0,) * array.ndim)


def kernel_call(kernel, name, grid, in_specs, out_specs, out_shape, scratch, flops, moved, **params):
    return pl.pallas_call(
        kernel,
        grid=grid,
        in_specs=in_specs,
        out_specs=out_specs,
        out_shape=out_shape,
        scratch_shapes=scratch,
        compiler_params=pltpu.CompilerParams(vmem_limit_bytes=VMEM_BYTES, **params),
        cost_estimate=pl.CostEstimate(flops=flops, bytes_accessed=moved, transcendentals=0),
        name=name,
    )


def attend(plan, own, projected, mark_q, mark_k, cotangent):
    rows, width = mark_q.shape[0], own.shape[1] // 3
    length, pairs = projected.shape[0], width // LANES
    stats = jax.ShapeDtypeStruct((STATS, rows), F32)
    anywhere = pl.BlockSpec(memory_space=pl.ANY)
    ways = plan.ways
    moving = [] if ways is None else [cotangent]
    params = {} if ways is None else {"collective_id": 1, "has_side_effects": True}
    results = kernel_call(
        functools.partial(attend_kernel, ways),
        "attend",
        (pairs,),
        [
            columns(rows, 0),
            columns(length, pairs),
            columns(length, 2 * pairs),
            whole(mark_q),
            whole(mark_k),
        ]
        + [anywhere] * len(moving),
        [
            columns(rows, 0),
            pl.BlockSpec((2, length, rows), lambda t: (t, 0, 0)),
            whole(stats),
        ]
        + [anywhere] * len(moving),
        [
            jax.ShapeDtypeStruct((rows, width), BF16),
            jax.ShapeDtypeStruct((2 * pairs, length, rows), BF16),
            stats,
        ]
        + [jax.ShapeDtypeStruct(array.shape, array.dtype) for array in moving],
        [pltpu.SemaphoreType.DMA] * (2 * len(moving)),
        24 * rows * length * width,
        4 * pairs * rows * length,
        **params,
    )(own, projected, projected, mark_q, mark_k, *moving)
    return tuple(results) if moving else tuple(results) + (cotangent,)


def grad_query(chances, grad, projected, deltas):
    rows, width = grad.shape
    length, pairs = projected.shape[0], width // LANES
    return kernel_call(
        grad_query_kernel,
        "grad_query",
        (pairs,),
        [
            pl.BlockSpec((2, length, rows), lambda t: (t, 0, 0)),
            columns(rows, 0),
            columns(length, pairs),
            columns(length, 2 * pairs),
            whole(deltas),
        ],
        columns(rows, 0),
        jax.ShapeDtypeStruct((rows, width), BF16),
        [],
        16 * rows * length * width,
        4 * pairs * rows * length,
    )(chances, grad, projected, projected, deltas)


def grad_key_value(own, projected, grads, log_totals, deltas, mark_k, mark_q):
    rows, width = grads[0].shape
    pieces, pairs = len(grads), width // LANES
    length = rows * pieces
    result = jax.ShapeDtypeStruct((rows, width), BF16)
    return kernel_call(
        functools.partial(grad_key_kernel, pieces),
        "grad_key_value",
        (pairs,),
        [columns(rows, pairs), columns(rows, 2 * pairs), columns(length, 0)]
        + [columns(rows, 0)] * pieces
        + [whole(log_totals[0])] * (2 * pieces)
        + [whole(mark_k), whole(mark_q)],
        [columns(rows, 0)] * 2,
        [result] * 2,
        [],
        32 * rows * length * width,
        8 * length * width,
    )(own, own, projected, *grads, *log_totals, *deltas, mark_k, mark_q)


class Chunk:
    stages = ("start", "near", "far", "along", "meet", "spread", "finish")

    def __init__(self, source, rows, columns, y_first, when, held=False, dtype=BF16):
        self.source, self.rows, self.columns = source, rows, columns
        self.shape = (rows[1], columns[1])
        self.blocks = ((2, 3), 1) if y_first else ((1, 3), 2)
        self.y_first, self.when, self.held, self.dtype = y_first, when, held, dtype

    def scratch(self):
        rows, columns = self.shape
        lead = [(4,), (2,), (), (), ()] if self.held else [(4,), (2,), (), (), (), (4,)]
        return [pltpu.VMEM(first + (rows, columns), self.dtype) for first in lead] + [
            pltpu.SemaphoreType.DMA((7,)),
            pltpu.SemaphoreType.DMA((8,)),
        ]

    def bind(self, source, out, scratch, devices):
        at = (pl.ds(*self.rows), pl.ds(*self.columns))
        kept = source.at[(pl.ds(0, 4),) + at]
        self.out = out.at[at]
        core, first, second, z1, z2, *rest = scratch
        *rest, sent, landed = rest
        self.keep = kept if self.held else rest[0]
        self.core, self.first, self.second, self.z1, self.z2 = core, first, second, z1, z2
        near, far = (devices["y"], devices["x"]) if self.y_first else (devices["x"], devices["y"])
        sends, last = self.blocks
        self.load = pltpu.make_async_copy(kept, self.keep, landed.at[7])
        self.to_core = remote(
            source.at[(pl.ds(4, 4),) + at], core, sent.at[0], landed.at[0], devices["core"]
        )
        self.to_near = [
            remote(self.keep.at[b], first.at[i], sent.at[1 + i], landed.at[1 + i], near)
            for i, b in enumerate(sends)
        ]
        self.to_far = remote(self.keep.at[last], second, sent.at[3], landed.at[3], far)
        self.inward = remote(self.keep.at[0], z1, sent.at[4], landed.at[4], devices["pair"])
        self.middle = remote(self.keep.at[0], z2, sent.at[5], landed.at[5], devices["mirror"])
        self.outward = remote(z1, self.out, sent.at[6], landed.at[6], devices["pair"])
        self.store = pltpu.make_async_copy(z1, self.out, landed.at[6])

    def add(self, target, one, other):
        size = 32 if self.shape[0] % 32 == 0 else 16

        def step(i, carry):
            at = pl.ds(pl.multiple_of(i * size, size), size)
            target[at, :] = one[at, :] + other[at, :]
            return carry

        lax.fori_loop(0, self.shape[0] // size, step, 0)

    def start(self):
        self.to_core.start()
        if not self.held:
            self.load.start()

    def near(self):
        if not self.held:
            self.load.wait()
        self.to_core.wait_recv()
        sends = self.blocks[0]
        for block in sends:
            self.add(self.keep.at[block], self.keep.at[block], self.core.at[block])
        for copy in self.to_near:
            copy.start()
        for block in range(4):
            if block not in sends:
                self.add(self.keep.at[block], self.keep.at[block], self.core.at[block])

    def far(self):
        stay = [b for b in range(4) if b not in self.blocks[0]]
        for i in (1, 0):
            self.to_near[i].wait_recv()
            self.add(self.keep.at[stay[i]], self.keep.at[stay[i]], self.first.at[i])
            if stay[i] == self.blocks[1]:
                self.to_far.start()

    def along(self):
        self.to_far.wait_recv()
        self.add(self.keep.at[0], self.keep.at[0], self.second)

        @pl.when(jnp.logical_not(inner()))
        def _():
            self.inward.start()

    def meet(self):
        @pl.when(inner())
        def _():
            self.inward.wait_recv()
            self.add(self.keep.at[0], self.keep.at[0], self.z1)
            self.middle.start()

    def spread(self):
        @pl.when(inner())
        def _():
            self.middle.wait_recv()
            self.add(self.z1, self.keep.at[0], self.z2)
            self.outward.start()
            self.store.start()

    def finish(self):
        @pl.when(jnp.logical_not(inner()))
        def _():
            self.outward.wait_recv()
            self.inward.wait_send()

        @pl.when(inner())
        def _():
            self.store.wait()
            self.middle.wait_send()
            self.outward.wait_send()

        self.to_core.wait_send()
        for copy in self.to_near:
            copy.wait_send()
        self.to_far.wait_send()


def inner():
    z = lax.axis_index("seq")
    return jnp.logical_and(z > 0, z < 3)


def ring_devices():
    dp, z = lax.axis_index("dp"), lax.axis_index("seq")
    core, pair, swap = neighbours()
    x = dp + 2 - 4 * lax.rem(lax.div(dp, jnp.int32(2)), jnp.int32(2))
    y = dp + 4 - 8 * lax.div(dp, jnp.int32(4))
    return {
        "core": core,
        "pair": pair,
        "swap": swap,
        "x": (x, z),
        "y": (y, z),
        "mirror": (dp, 3 - z),
    }


def relative_place(block):
    dp = lax.axis_index("dp")
    bits = [lax.rem(lax.div(dp, jnp.int32(1 << k)) + (block >> k) % 2, jnp.int32(2)) for k in range(3)]
    return bits[0] * 4 + bits[1] + bits[2] * 2


def store_blocks(target, columns, total):
    part = total.shape[0] // 8
    for block in range(8):
        target[relative_place(block), :, columns] = total[block * part : (block + 1) * part].astype(BF16)


VECTORS = 16


def backward_chunks(shapes, width, pairs):
    down, up, out = shapes
    third, share = down[1] // 3, up[2] // 3
    part = width // 8
    end = 4 * pairs

    def when(*steps):
        return tuple(at if isinstance(at, tuple) else (at, 0) for at in steps)

    tile = 2 * LANES
    ends = [tuple((end, i) for i in range(n)) for n in range(8)]
    return [
        Chunk("down", (0, third), (0, width), True, when(0, 2, 8, 14, 16, 18)),
        Chunk("down", (third, third), (0, width), False, when(0, 2, 8, 14, 16, 18)),
        Chunk("up", (0, part), (0, share), True, when(1, 4, 12, 17, 19, 21)),
        Chunk("up", (0, part), (share, share), False, when(1, 4, 12, 17, 19, 21)),
        Chunk("down", (2 * third, third), (0, width), True, when(3, 10, 16, 20, 21, 23)),
        Chunk("up", (0, part), (2 * share, share), False, when(3, 10, 16, 20, 21, 23)),
        Chunk("out", (0, part), (0, width), True, when(6, 13, 19, 22, 23, (end, 1))),
        Chunk("query", (0, part), (0, width), False, when(12, 13, 19, 22, 23, (end, 1)), True),
        Chunk("pair", (0, part), (0, 2 * tile), True, when(20, 21, 23, *ends[4][1:]), True),
        Chunk("pair", (0, part), (2 * tile, 2 * tile), False, when(22, 23, *ends[5][1:]), True),
        Chunk("pair", (0, part), (4 * tile, tile), True, when(23, *ends[6][1:]), True),
        Chunk("pair", (0, part), (5 * tile, tile), False, when((end, 0), *ends[7][2:]), True),
        Chunk(
            "vector",
            (0, VECTORS),
            (0, LANES),
            True,
            when((end, 0), *ends[7][2:]),
            True,
            F32,
        ),
    ]


def backward_kernel(
    shapes,
    pairs,
    chance_ref,
    grad_ref,
    attended_ref,
    k_ref,
    v_ref,
    q_ref,
    mark_k,
    mark_q,
    lse_ref,
    gain_ref,
    sums_ref,
    sum_up_ref,
    w_hbm,
    hidden_hbm,
    here_hbm,
    middle_hbm,
    grad_down,
    grad_up,
    grad_out,
    block_ref,
    home_ref,
    tokens_ref,
    down_ref,
    up_ref,
    out_ref,
    query_ref,
    pair_ref,
    vector_ref,
    grads,
    stats,
    own_stats,
    turned,
    dq,
    dkv,
    grad_hidden,
    query_grad,
    pair_grad,
    vector,
    late,
    tokens,
    weights,
    hidden_ref,
    here_ref,
    middle_ref,
    sent,
    landed,
    loaded,
    *scratch,
):
    step = pl.program_id(0)
    rows, width = grad_ref.shape
    held = ((hidden_hbm, hidden_ref), (w_hbm, weights), (here_hbm, here_ref), (middle_hbm, middle_ref))
    loads = [
        pltpu.make_async_copy(source, target, loaded.at[i])
        for i, (source, target) in enumerate(held)
    ]
    half = rows // 2
    first, steps = 2 * pairs, 4 * pairs
    devices = ring_devices()
    chunks = backward_chunks(shapes, width, pairs)
    sources = {
        "down": (grad_down, down_ref),
        "up": (grad_up, up_ref),
        "out": (grad_out, out_ref),
        "query": (query_grad, query_ref),
        "pair": (pair_grad, pair_ref),
        "vector": (vector, vector_ref),
    }
    scratch = list(scratch)
    for chunk in chunks:
        count = len(chunk.scratch())
        chunk.bind(*sources[chunk.source], scratch[:count], devices)
        del scratch[:count]
    block_move = (block_ref, home_ref, sent.at[12], landed.at[12])

    def token_move(part):
        at = pl.ds(part * half, half)
        return (tokens.at[at], tokens_ref.at[at], sent.at[13 + part], landed.at[13 + part])

    def grad_copy(i, part, source, device):
        at = pl.ds(part * half, half)
        n = 2 * i + part
        return remote(source.at[at], grads.at[i, at], sent.at[n], landed.at[n], device)

    def to_core(part):
        return grad_copy(1, part, grad_ref, devices["core"])

    def to_pair(part):
        return grad_copy(2, part, grad_ref, devices["pair"])

    def to_corner(part):
        return grad_copy(3, part, grads.at[2], devices["core"])

    def stat_copy(i, source, device):
        return remote(source, stats.at[i], sent.at[8 + i], landed.at[8 + i], device)

    stat_core = stat_copy(1, own_stats, devices["core"])
    stat_pair = stat_copy(2, own_stats, devices["pair"])
    stat_corner = stat_copy(3, stats.at[2], devices["core"])

    def begin():
        greet(list(devices.values()))
        for part in range(2):
            to_pair(part).start()
        for part in range(2):
            to_core(part).start()
        for load in loads:
            load.start()

    def begin_stats():
        product = grad_ref[...].astype(F32) * attended_ref[...].astype(F32)
        high = product.astype(BF16)
        low = (product - high.astype(F32)).astype(BF16)
        head = lax.broadcasted_iota(jnp.int32, (STATS, width), 0)
        column = lax.broadcasted_iota(jnp.int32, (STATS, width), 1)
        mine = jnp.where(
            jnp.logical_and(column >= head * HDIM, column < (head + 1) * HDIM), 1.0, 0.0
        ).astype(BF16)
        own_stats[0:STATS, :] = lse_ref[...]
        own_stats[STATS:, :] = dot_as(mine, high, NT) + dot_as(mine, low, NT)
        stats[0] = own_stats[...]
        grads[0] = grad_ref[...]
        stat_pair.start()
        stat_core.start()
        late[...] = jnp.zeros_like(late)

    def corner_stats():
        stat_pair.wait_recv()
        stat_corner.start()

    def corner(part):
        def run():
            to_pair(part).wait_recv()
            to_corner(part).start()

        return run

    def all_grads():
        stat_core.wait_recv()
        stat_corner.wait_recv()
        for part in range(2):
            to_core(part).wait_recv()
            to_corner(part).wait_recv()

    def query_done():
        for load in loads:
            load.wait()
        turned[...] = jnp.transpose(hidden_ref[...])
        store_blocks(query_grad, pl.ds(0, width), dot_as(turned[...], dq[...], NN))
        grad_hidden[...] = dot_as(dq[...], weights[:, 0:width], NT)
        late[0:1, :] = jnp.sum(dq[...].astype(F32), 0, keepdims=True)

    def first_norm(part):
        def run():
            at = pl.ds(part * half, half)
            _, unit, root = layer_norm(here_ref[at, :].astype(F32), 0.0, 0.0)
            grad = grad_hidden[at, :]
            scaled = grad * row_of(gain_ref)
            grad_in = root * (
                scaled
                - jnp.mean(scaled, -1, keepdims=True)
                - unit * jnp.mean(scaled * unit, -1, keepdims=True)
            )
            tokens[at, :] = (middle_ref[at, :] + grad_in).astype(BF16)
            move_start(*token_move(part))
            late[2:3, :] += jnp.sum(grad * unit, 0, keepdims=True)
            late[3:4, :] += jnp.sum(grad, 0, keepdims=True)

        return run

    def early_vectors():
        share = width // 8
        vector[...] = jnp.zeros_like(vector)
        for block in range(8):
            place = relative_place(block)
            vector[place, 0:4, 0:share] = sums_ref[0:4, block * share : (block + 1) * share]
            for i in range(4):
                first = (block * 4 + i) * share
                vector[place, 8 + i : 9 + i, 0:share] = sum_up_ref[0:1, first : first + share]

    def late_vectors():
        share = width // 8
        for block in range(8):
            vector[relative_place(block), 4:8, 0:share] = late[
                0:4, block * share : (block + 1) * share
            ]

    def finish_moves():
        for move in (block_move, token_move(0), token_move(1)):
            move_landed(*move)
            move_sent(*move)
        for copy in (stat_core, stat_pair, stat_corner):
            copy.wait_send()
        for part in range(2):
            to_core(part).wait_send()
            to_pair(part).wait_send()
            to_corner(part).wait_send()

    events = [
        ((0, -2), begin),
        ((0, 1), begin_stats),
        ((4, -1), corner_stats),
        ((4, 2), early_vectors),
        ((8, -1), corner(0)),
        ((first, -2), corner(1)),
        ((first, -1), query_done),
        ((first, 3), lambda: move_start(*block_move)),
        ((first, 4), all_grads),
        ((first + pairs, -1), first_norm(0)),
        ((steps, -2), first_norm(1)),
        ((steps, -1), late_vectors),
        ((steps, 9), finish_moves),
    ]
    for order in (2, 1, 0, 3, 4, 5, 6):
        for chunk in chunks:
            at = chunk.when[order] if order < 6 else (steps, 8)
            events.append((at, getattr(chunk, Chunk.stages[order])))
    events.sort(key=lambda event: event[0])

    def run(at):
        for (when, _), event in events:
            if when == at:
                event()

    for at in range(steps):
        if any(when == at for (when, _), _ in events):

            @pl.when(step == at)
            def _():
                run(at)

    @pl.when(step < first)
    def _():
        pair = lax.div(step, jnp.int32(2))
        at = pl.ds(pl.multiple_of(lax.rem(step, jnp.int32(2)) * half, half), half)
        tile = pl.ds(pl.multiple_of(pair * LANES, LANES), LANES)
        deltas = [own_stats[pl.ds(STATS + 2 * pair + head, 1), at] for head in range(2)]
        dq[at, tile] = query_grads(chance_ref, grad_ref[at, tile], k_ref[...], v_ref[...], deltas)

    @pl.when(step >= first)
    def _():
        pair = lax.rem(step, jnp.int32(pairs))
        at = pl.ds(pl.multiple_of((lax.div(step, jnp.int32(pairs)) - 2) * half, half), half)
        tile = pl.ds(pl.multiple_of(pair * LANES, LANES), LANES)
        double = pl.ds(pl.multiple_of(pair * (2 * LANES), 2 * LANES), 2 * LANES)

        def weight(part):
            return weights[:, pl.ds(pl.multiple_of(part * width + pair * LANES, LANES), LANES)]

        parts = []
        for i in range(4):
            span = pl.ds(i * rows, rows)
            rows_of = [
                [stats[i, pl.ds(start + 2 * pair + head, 1), :] for head in range(2)]
                for start in (0, STATS)
            ]
            parts.append((q_ref[span, :], grads[i, :, tile], mark_q[span, :], *rows_of))
        dk, dv = key_grads(k_ref[at, :], v_ref[at, :], mark_k[at, :], parts)
        both = jnp.concatenate([dk, dv], 1)
        dkv[at, double] = both
        grad_hidden[at, :] += dot_as(both, jnp.concatenate([weight(1), weight(2)], 1), NT)
        late[1:2, tile] += jnp.sum(dv.astype(F32), 0, keepdims=True)

        @pl.when(step >= first + pairs)
        def _():
            store_blocks(pair_grad, double, dot_as(turned[...], dkv[:, double], NN))

    @pl.when(step == steps - 1)
    def _():
        run(steps)


def once(array):
    return pl.BlockSpec(array.shape, lambda *t: (0,) * array.ndim, pipeline_mode=pl.Buffered(1))


def backward(
    chances,
    grad,
    attended,
    projected,
    mark_k,
    mark_q,
    log_totals,
    weight,
    hidden,
    here,
    grad_middle,
    gain,
    sums,
    sum_up,
    totals,
    block_out,
):
    rows, width = grad.shape
    length, pairs = projected.shape[0], width // LANES
    shapes = [total.shape for total in totals]
    part = width // 8
    anywhere = pl.BlockSpec(memory_space=pl.ANY)
    result = jax.ShapeDtypeStruct((rows, width), BF16)
    outs = [result, result] + [
        jax.ShapeDtypeStruct(shape, BF16)
        for shape in [shape[1:] for shape in shapes] + [(part, width), (part, 2 * width)]
    ]
    outs.append(jax.ShapeDtypeStruct((VECTORS, LANES), F32))

    def pair_at(t):
        return jnp.where(t < 2 * pairs, lax.div(t, 2), lax.rem(t, pairs))

    def tile(first):
        return pl.BlockSpec((length, LANES), lambda t: (0, first + pair_at(t)))

    def chance_at(t):
        t = jnp.minimum(t, 2 * pairs - 1)
        return lax.div(t, 2), 0, lax.rem(t, 2)

    fixed = [mark_k, mark_q, log_totals, gain, sums, sum_up]
    held = [weight, hidden, here, grad_middle]
    chunks = backward_chunks(shapes, width, pairs)
    stats = (2 * STATS, rows)
    return kernel_call(
        functools.partial(backward_kernel, shapes, pairs),
        "backward",
        (4 * pairs,),
        [
            pl.BlockSpec((2, length, rows // 2), chance_at),
            once(grad),
            once(attended),
            tile(pairs),
            tile(2 * pairs),
            pl.BlockSpec((length, LANES), lambda t: (0, lax.rem(jnp.maximum(t - 2 * pairs, 0), pairs))),
        ]
        + [once(array) for array in fixed]
        + [anywhere] * (len(held) + len(totals) + 1),
        [anywhere] * len(outs),
        outs,
        [
            pltpu.VMEM((4, rows, width), BF16),
            pltpu.VMEM((4,) + stats, F32),
            pltpu.VMEM(stats, F32),
            pltpu.VMEM((width, rows), BF16),
            pltpu.VMEM((rows, width), BF16),
            pltpu.VMEM((rows, 2 * width), BF16),
            pltpu.VMEM((rows, width), F32),
            pltpu.VMEM((8, part, width), BF16),
            pltpu.VMEM((8, part, 2 * width), BF16),
            pltpu.VMEM((8, VECTORS, LANES), F32),
            pltpu.VMEM((8, width), F32),
            pltpu.VMEM((rows, width), BF16),
        ]
        + [pltpu.VMEM(array.shape, array.dtype) for array in held]
        + [
            pltpu.SemaphoreType.DMA((15,)),
            pltpu.SemaphoreType.DMA((15,)),
            pltpu.SemaphoreType.DMA((len(held),)),
        ]
        + [entry for chunk in chunks for entry in chunk.scratch()],
        48 * rows * length * width,
        4 * pairs * rows * length,
        collective_id=2,
        has_side_effects=True,
    )(chances, grad, attended, projected, projected, projected, *fixed, *held, *totals, block_out)


def results_kernel(block, tokens, down, up, out, query, pair, vector, *outs):
    (
        block_ref,
        tokens_ref,
        ln1_gain,
        ln1_shift,
        w_qkv,
        bias_query,
        bias_value,
        w_out,
        bias_out,
        ln2_gain,
        ln2_shift,
        w_up,
        bias_up,
        w_down,
        bias_down,
    ) = outs
    block_ref[...] = block[...]
    tokens_ref[...] = tokens[...]
    width = query.shape[1]
    w_qkv[:, 0:width] = query[...].astype(F32)
    for i in range(width // LANES):
        for j in range(2):
            first = (2 * i + j) * LANES
            to = (1 + j) * width + i * LANES
            w_qkv[:, to : to + LANES] = pair[:, first : first + LANES].astype(F32)
    w_up[...] = up[...].astype(F32)
    w_down[...] = down[...].astype(F32)
    w_out[...] = out[...].astype(F32)
    share = width // 8
    order = (ln2_gain, ln2_shift, bias_out, bias_down, bias_query, bias_value, ln1_gain, ln1_shift)
    for i, ref in enumerate(order):
        ref[...] = vector[i, 0:share]
    bias_up[...] = jnp.concatenate([vector[8 + i : 9 + i, 0:share] for i in range(4)], 1)[0]


def results(block, tokens, down, up, out, query, pair, vector):
    part, width = query.shape
    vmem = pl.BlockSpec(memory_space=pltpu.VMEM)

    def line(size=part):
        return jax.ShapeDtypeStruct((size,), F32)

    def like(array):
        return jax.ShapeDtypeStruct(array.shape, F32)

    return pl.pallas_call(
        results_kernel,
        in_specs=[vmem] * 8,
        out_specs=[vmem] * 15,
        out_shape=[
            jax.ShapeDtypeStruct(block.shape, BF16),
            jax.ShapeDtypeStruct(tokens.shape, BF16),
            line(),
            line(),
            jax.ShapeDtypeStruct((part, 3 * width), F32),
            line(),
            line(),
            like(out),
            line(),
            line(),
            line(),
            like(up),
            line(4 * part),
            like(down),
            line(),
        ],
        compiler_params=pltpu.CompilerParams(vmem_limit_bytes=VMEM_BYTES),
        name="results",
    )(block, tokens, down, up, out, query, pair, vector)


def gelu_parts(pre_act):
    inside = 0.5 * (1.0 + lax.erf(pre_act * math.sqrt(0.5)))
    slope = inside + pre_act * jnp.exp(-0.5 * pre_act * pre_act) * (1.0 / math.sqrt(2.0 * math.pi))
    return pre_act * inside, slope


def relative(block, me):
    turned = block ^ me
    return (turned % 2) * 4 + turned // 2


def feed_kernel(
    sub,
    index_ref,
    here_ref,
    attended_ref,
    grad_ref,
    w_out_ref,
    bias_out_ref,
    gain_ref,
    shift_ref,
    w_up_ref,
    bias_up_ref,
    w_down_ref,
    bias_down_ref,
    block_ref,
    grad_attended_ref,
    grad_middle_ref,
    down_ref,
    up_ref,
    out_ref,
    sum_up_ref,
    sums_ref,
    middle,
    normed,
    inverse,
    hidden,
    turned,
    total,
    grad_hidden,
    activated,
    grad_upper,
):
    step, last = pl.program_id(0), pl.num_programs(0) - 1
    me = index_ref[0]
    rows, width = here_ref.shape
    blocks = rows // sub

    def span(i):
        return pl.ds(pl.multiple_of(i * sub, sub), sub)

    @pl.when(step == 0)
    def _():
        def norm(i, carry):
            at = span(i)
            values = (
                here_ref[at, :].astype(F32)
                + dot_as(attended_ref[at, :], w_out_ref[...], NN)
                + row_of(bias_out_ref)
            )
            out, unit, root = layer_norm(values, row_of(gain_ref), row_of(shift_ref))
            middle[at, :] = values
            normed[at, :] = unit
            inverse[at, :] = jnp.broadcast_to(root, (sub, LANES))
            hidden[at, :] = out.astype(BF16)
            total[at, :] = values + row_of(bias_down_ref)
            grad_hidden[at, :] = jnp.zeros((sub, width), F32)
            return carry

        lax.fori_loop(0, blocks, norm, 0)
        turned[...] = jnp.transpose(hidden[...])

    def tile(i, carry):
        at = span(i)
        upper = dot_as(hidden[at, :], w_up_ref[...], NN) + bias_up_ref[...]
        grad_activated = dot_as(grad_ref[at, :], w_down_ref[...], NT)
        active, slope = gelu_parts(upper)
        active = active.astype(BF16)
        grad_in = (grad_activated * slope).astype(BF16)
        activated[at, :] = active
        grad_upper[at, :] = grad_in
        total[at, :] += dot_as(active, w_down_ref[...], NN)
        grad_hidden[at, :] += dot_as(grad_in, w_up_ref[...], NT)
        return carry + jnp.sum(grad_in.astype(F32), 0, keepdims=True)

    sum_up_ref[...] = lax.fori_loop(0, blocks, tile, jnp.zeros(sum_up_ref.shape, F32))

    grad_up = dot_as(turned[...], grad_upper[...], NN)
    part = width // 8
    for block in range(8):
        up_ref[relative(block, me)] = grad_up[block * part : (block + 1) * part].astype(BF16)
    grad_down = inner_rows(activated[...], grad_ref[...])
    part = down_ref.shape[2]
    for i in range(2):
        down_ref[(i ^ me) % 2, 0] = grad_down[i * part : (i + 1) * part].astype(BF16)

    @pl.when(step == last)
    def _():
        def norm(i, carry):
            at = span(i)
            block_ref[at, :] = total[at, :].astype(BF16)
            grad, unit = grad_hidden[at, :], normed[at, :]
            scaled = grad * row_of(gain_ref)
            grad_in = inverse[at, 0:1] * (
                scaled
                - jnp.mean(scaled, -1, keepdims=True)
                - unit * jnp.mean(scaled * unit, -1, keepdims=True)
            )
            before = grad_ref[at, :].astype(F32)
            grad_in = before + grad_in
            branch = grad_in.astype(BF16)
            grad_middle_ref[at, :] = grad_in
            hidden[at, :] = branch
            grad_attended_ref[at, :] = dot_as(branch, w_out_ref[...], NT).astype(BF16)
            sums = [grad * unit, grad, branch.astype(F32), before]
            return tuple(
                old + jnp.sum(value, 0, keepdims=True) for old, value in zip(carry, sums)
            )

        zero = jnp.zeros((1, width), F32)
        sums = lax.fori_loop(0, blocks, norm, (zero,) * 4)
        sums_ref[...] = jnp.concatenate(list(sums) + [zero] * 4, 0)
        grad_out = inner_rows(attended_ref[...], hidden[...])
        part = width // 8
        for block in range(8):
            out_ref[relative(block, me)] = grad_out[block * part : (block + 1) * part].astype(BF16)


def feed(
    here, attended, grad, w_out, bias_out, gain, shift, w_up, bias_up, w_down, bias_down, me, sub=256
):
    rows, width = here.shape
    wide = w_up.shape[1]
    steps = 4
    tile = wide // steps
    part = width // 8

    def once(*shape):
        return pl.BlockSpec(shape, lambda f, at: (0,) * len(shape), pipeline_mode=pl.Buffered(1))

    act = once(rows, width)
    line = once(width)
    outs = [
        jax.ShapeDtypeStruct((rows, width), BF16),
        jax.ShapeDtypeStruct((rows, width), BF16),
        jax.ShapeDtypeStruct((rows, width), F32),
        jax.ShapeDtypeStruct((2, 4, wide // 8, width), BF16),
        jax.ShapeDtypeStruct((8, part, wide), BF16),
        jax.ShapeDtypeStruct((8, part, width), BF16),
        jax.ShapeDtypeStruct((1, wide), F32),
        jax.ShapeDtypeStruct((8, width), F32),
    ]
    return pl.pallas_call(
        functools.partial(feed_kernel, sub),
        grid_spec=pltpu.PrefetchScalarGridSpec(
            num_scalar_prefetch=1,
            grid=(steps,),
            in_specs=[
                act,
                act,
                act,
                once(width, width),
                line,
                line,
                line,
                pl.BlockSpec((width, tile), lambda f, at: (0, f)),
                pl.BlockSpec((1, tile), lambda f, at: (0, f)),
                pl.BlockSpec((tile, width), lambda f, at: (f, 0)),
                line,
            ],
            out_specs=[
                act,
                act,
                act,
                pl.BlockSpec((2, 1, wide // 8, width), lambda f, at: (0, f ^ (at[0] // 2), 0, 0)),
                pl.BlockSpec((8, part, tile), lambda f, at: (0, 0, f)),
                once(8, part, width),
                pl.BlockSpec((1, tile), lambda f, at: (0, f)),
                once(8, width),
            ],
            scratch_shapes=[
                pltpu.VMEM((rows, width), F32),
                pltpu.VMEM((rows, width), F32),
                pltpu.VMEM((rows, LANES), F32),
                pltpu.VMEM((rows, width), BF16),
                pltpu.VMEM((width, rows), BF16),
                pltpu.VMEM((rows, width), F32),
                pltpu.VMEM((rows, width), F32),
                pltpu.VMEM((rows, tile), BF16),
                pltpu.VMEM((rows, tile), BF16),
            ],
        ),
        out_shape=outs,
        compiler_params=pltpu.CompilerParams(vmem_limit_bytes=VMEM_BYTES),
        cost_estimate=pl.CostEstimate(
            flops=12 * rows * width * wide, bytes_accessed=8 * width * wide, transcendentals=0
        ),
        name="feed",
    )(
        me,
        here,
        attended,
        grad,
        w_out,
        bias_out,
        gain,
        shift,
        w_up,
        bias_up.reshape(1, -1),
        w_down,
        bias_down,
    )


def start_kernel(
    tokens_ref,
    lengths_ref,
    gain_ref,
    shift_ref,
    w_ref,
    bias_ref,
    projected_ref,
    hidden_ref,
    here_ref,
    found_ref,
    rows,
    staged,
    sent,
    landed,
    out_sem,
):
    core, across, swap = neighbours()
    parts = sent.shape[1]
    height = tokens_ref.shape[0]
    part = height // parts
    greet([core, across, swap])

    def span(i):
        return pl.ds(pl.multiple_of(i * part, part), part)

    def moved(i):
        return (tokens_ref.at[span(i)], rows.at[0, span(i)], sent.at[0, i], landed.at[0, i])

    def lengths():
        return remote(lengths_ref, found_ref, sent.at[4, 0], landed.at[4, 0], core)

    def forward(i, origin, piece, device):
        return remote(
            rows.at[origin, span(i)],
            rows.at[piece, span(i)],
            sent.at[piece, i],
            landed.at[piece, i],
            device,
        )

    def out_span(piece, i):
        return pl.ds(pl.multiple_of(piece * height + i * part, part), part)

    def to_hbm(piece, i):
        at = out_span(piece, i)
        return pltpu.make_async_copy(staged.at[at], projected_ref.at[at], out_sem.at[piece, i])

    def project(piece, i):
        values = rows[piece, span(i), :].astype(F32)
        hidden = layer_norm(values, row_of(gain_ref), row_of(shift_ref))[0].astype(BF16)
        staged[out_span(piece, i), :] = (
            dot_as(hidden, w_ref[...], NN) + row_of(bias_ref)
        ).astype(BF16)
        to_hbm(piece, i).start()
        return hidden

    for i in range(parts):
        move_start(*moved(i))
    lengths().start()

    def first(i, carry):
        move_landed(*moved(i))
        forward(i, 0, 2, across).start()
        forward(i, 0, 1, core).start()
        hidden_ref[span(i), :] = project(0, i)
        here_ref[span(i), :] = rows[0, span(i), :]
        return carry

    lax.fori_loop(0, parts, first, 0)

    def second(i, carry):
        forward(i, 0, 1, core).wait_recv()
        project(1, i)
        forward(i, 0, 2, across).wait_recv()
        forward(i, 2, 3, core).start()
        project(2, i)
        return carry

    lax.fori_loop(0, parts, second, 0)

    def third(i, carry):
        forward(i, 2, 3, core).wait_recv()
        project(3, i)
        return carry

    lax.fori_loop(0, parts, third, 0)
    lengths().wait()

    def last(i, carry):
        move_sent(*moved(i))
        forward(i, 0, 2, across).wait_send()
        forward(i, 0, 1, core).wait_send()
        forward(i, 2, 3, core).wait_send()
        for piece in range(4):
            to_hbm(piece, i).wait()
        return carry

    lax.fori_loop(0, parts, last, 0)


def start_work(tokens, clip_lengths, gain, shift, weight, bias):
    rows, width = tokens.shape
    vmem, anywhere = pl.BlockSpec(memory_space=pltpu.VMEM), pl.BlockSpec(memory_space=pl.ANY)
    projected, hidden, here, found = pl.pallas_call(
        start_kernel,
        in_specs=[anywhere] + [vmem] * 5,
        out_specs=[anywhere, vmem, vmem, vmem],
        out_shape=[
            jax.ShapeDtypeStruct((4 * rows, 3 * width), BF16),
            jax.ShapeDtypeStruct((rows, width), BF16),
            jax.ShapeDtypeStruct((rows, width), BF16),
            jax.ShapeDtypeStruct(clip_lengths.shape, jnp.int32),
        ],
        scratch_shapes=[
            pltpu.VMEM((4, rows, width), BF16),
            pltpu.VMEM((4 * rows, 3 * width), BF16),
            pltpu.SemaphoreType.DMA((5, 4)),
            pltpu.SemaphoreType.DMA((5, 4)),
            pltpu.SemaphoreType.DMA((4, 4)),
        ],
        compiler_params=pltpu.CompilerParams(
            vmem_limit_bytes=VMEM_BYTES, collective_id=0, has_side_effects=True
        ),
        cost_estimate=pl.CostEstimate(
            flops=24 * rows * width * width, bytes_accessed=32 * rows * width, transcendentals=0
        ),
        name="start_work",
    )(tokens, clip_lengths, gain, shift, weight, bias)
    return projected, hidden, here, jnp.where(stays(), clip_lengths, found)


class PairPlan:
    ways = True

    def start(self, tokens, clip_lengths, gain, shift, weight, bias):
        projected, hidden, here, lengths = start_work(
            tokens, clip_lengths, gain, shift, weight, bias
        )
        return projected, projected, hidden, here, lengths

    def positions(self, rows):
        core, z = lax.axis_index("dp") % 2, lax.axis_index("seq")
        found = []
        for piece in range(4):
            c, plane = core ^ (piece % 2), z ^ (piece // 2)
            shard = jnp.where(c == plane // 2, plane, plane ^ 2)
            found.append(shard * rows + jnp.arange(rows, dtype=jnp.int32))
        return jnp.concatenate(found)

    def own(self, gathered):
        return gathered[: gathered.shape[0] // 4]

    def backward(self, work, weights, attention):
        here, hidden1, grad_out, projected, own, mark_k, mark_q = work
        chances, attended, log_totals = attention
        me = lax.axis_index("dp").astype(jnp.int32).reshape(1)
        block_out, grad, grad_middle, down, up, out, sum_up, sums = feed(
            here, attended, grad_out, *weights[2:], me
        )
        return results(
            *backward(
                chances,
                grad,
                attended,
                projected,
                self.own(mark_k),
                mark_q,
                log_totals,
                weights[0],
                hidden1,
                here,
                grad_middle,
                weights[1],
                sums,
                sum_up,
                [down.reshape((8,) + down.shape[2:]), up, out],
                block_out,
            )
        )


class PlainPlan:
    ways = None

    def __init__(self, pieces):
        self.pieces = pieces

    def start(self, tokens, clip_lengths, gain, shift, weight, bias):
        hidden = layer_norm(tokens.astype(F32), gain, shift)[0].astype(BF16)
        own = (matmul(hidden, weight) + bias).astype(BF16)
        projected = lax.all_gather(own, "seq", axis=0, tiled=True)
        return projected, own, hidden, tokens, clip_lengths

    def gather(self, own):
        gathered = lax.all_gather(own, "seq", axis=0, tiled=False)
        return [gathered[i] for i in range(self.pieces)]

    def positions(self, rows):
        return jnp.arange(rows * self.pieces, dtype=jnp.int32)

    def own(self, gathered):
        rows = gathered.shape[0] // self.pieces
        return lax.dynamic_slice_in_dim(gathered, lax.axis_index("seq") * rows, rows, 0)

    def backward(self, work, weights, attention):
        here, hidden1, grad_out, projected, own, mark_k, mark_q = work
        chances, attended, log_totals = attention
        w_qkv, ln1_gain, w_out, bias_out, gain, shift, w_up, bias_up, w_down, bias_down = weights
        middle = here.astype(F32) + matmul(attended, w_out) + bias_out
        normed_out, normed, inverse = layer_norm(middle, gain, shift)
        hidden = normed_out.astype(BF16)
        activated, slope = gelu_parts(matmul(hidden, w_up) + bias_up)
        activated = activated.astype(BF16)
        grad_upper = (inner_cols(grad_out, w_down) * slope).astype(BF16)
        grad_hidden = inner_cols(grad_upper, w_up)
        grad_norm, grad_gain, grad_shift = norm_back(grad_hidden, normed, inverse, gain)
        grad_middle = grad_out.astype(F32) + grad_norm
        grad_branch = grad_middle.astype(BF16)
        grad = inner_cols(grad_branch, w_out).astype(BF16)
        block_out = (middle + matmul(activated, w_down) + bias_down).astype(BF16)

        product = (grad.astype(F32) * attended.astype(F32)).reshape(grad.shape[0], -1, HDIM)
        deltas = jnp.sum(product, -1).T
        deltas = jnp.pad(deltas, ((0, STATS - deltas.shape[0]), (0, 0)))
        dq = grad_query(chances, grad, projected, deltas)
        dk, dv = grad_key_value(
            own,
            projected,
            self.gather(grad),
            self.gather(log_totals),
            self.gather(deltas),
            self.own(mark_k),
            mark_q,
        )
        grad_projected = jnp.concatenate([dq, dk, dv], 1)
        grad_hidden1 = inner_cols(grad_projected, w_qkv)
        _, normed1, inverse1 = layer_norm(here.astype(F32), 0.0, 0.0)
        grad_norm1, grad_ln1_gain, grad_ln1_shift = norm_back(
            grad_hidden1, normed1, inverse1, ln1_gain
        )

        def total(values):
            return jnp.sum(values.astype(F32), 0)

        return (block_out, (grad_middle + grad_norm1).astype(BF16)) + tuple(
            self.reduce(value)
            for value in (
                grad_ln1_gain,
                grad_ln1_shift,
                inner_rows(hidden1, grad_projected),
                total(dq),
                total(dv),
                inner_rows(attended, grad_branch),
                total(grad_branch),
                grad_gain,
                grad_shift,
                inner_rows(hidden, grad_upper),
                total(grad_upper),
                inner_rows(activated, grad_out),
                total(grad_out),
            )
        )

    def reduce(self, total):
        return lax.psum(lax.psum_scatter(total, "dp", scatter_dimension=0, tiled=True), "seq")


def body(
    plan,
    tokens,
    clip_lengths,
    ln1_gain,
    ln1_shift,
    w_qkv,
    bias_query,
    bias_value,
    w_out,
    bias_out,
    ln2_gain,
    ln2_shift,
    w_up,
    bias_up,
    w_down,
    bias_down,
    cotangent,
):
    rows, width = tokens.shape
    bias = jnp.concatenate([bias_query, jnp.zeros_like(bias_query), bias_value])
    projected, own, hidden1, here, lengths = plan.start(
        tokens, clip_lengths, ln1_gain, ln1_shift, w_qkv, bias
    )

    clip_ends = jnp.cumsum(lengths.reshape(-1))
    position = plan.positions(rows)
    segment = jnp.sum((position[:, None] >= clip_ends[None, :]).astype(jnp.int32), 1)
    lane = jnp.arange(LANES, dtype=jnp.int32)[None, :]
    same = lane == segment[:, None]
    mark_k = same.astype(BF16)
    mark_q = jnp.where(same | (lane >= clip_ends.shape[0]), 0.0, masked_score).astype(BF16)

    attended, chances, log_totals, grad_out = attend(
        plan, own, projected, plan.own(mark_q), mark_k, cotangent
    )

    return tuple(
        plan.backward(
            (here, hidden1, grad_out, projected, own, mark_k, mark_q),
            (
                w_qkv,
                ln1_gain,
                w_out,
                bias_out,
                ln2_gain,
                ln2_shift,
                w_up,
                bias_up,
                w_down,
                bias_down,
            ),
            (chances, attended, log_totals),
        )
    )


def solution(mesh):
    sizes = dict(mesh.shape)
    plan = PairPlan() if sizes == {"dp": 8, "seq": 4} else PlainPlan(sizes["seq"])
    rows = P(("dp", "seq"), None)
    return jax.shard_map(
        functools.partial(body, plan),
        mesh=mesh,
        in_specs=(rows, P("dp", None)) + (P(),) * 13 + (rows,),
        out_specs=(
            rows,
            rows,
            P("dp"),
            P("dp"),
            P("dp", None),
            P("dp"),
            P("dp"),
            P("dp", None),
            P("dp"),
            P("dp"),
            P("dp"),
            P("dp", None),
            P("dp"),
            P("dp", None),
            P("dp"),
        ),
        check_vma=False,
    )
```

time: 316 us -> 235 us (0.74)
  waiting for transfers between devices: 47.5 us -> 0 us
  starting transfers between devices: 21.7 us -> 0 us
  local copies, waits for them, and re-layouts: 15.7 us -> 1.55 us
  Pallas kernels: 219 us -> 230 us
  other arithmetic: 7.77 us -> 2.3 us
    ppermute x19 -> x0, waiting for transfers between devices: 47.5 us -> none  [the longest x4 23.8 us: reduce_vectors(): lax.ppermute(packed, 'seq', [(i, i ^ bit) for i in range(4)])]
    ppermute x19 -> x0, starting transfers between devices: 21.7 us -> none  [the longest x11 14.2 us: swap(): return lax.ppermute(value, 'dp', [(i, i ^ bit) for i in range(8)])]
    pallas_call x1, Pallas kernels: 110 us -> 130 us  [backward(): kernel_call(functools.partial(backward_kernel, shapes, pairs), 'backward'...]
    pallas_call x2, Pallas kernels: 42.2 us -> 33.6 us  [the longest x1 29.3 us: attend(): kernel_call(functools.partial(attend_kernel, ways), 'attend', (pairs,), [...]
    unnamed x54 -> x6, local copies, waits for them, and re-layouts: 6.71 us -> 0.14 us
    reshape x7 -> x0, local copies, waits for them, and re-layouts: 5.49 us -> none  [the longest x4 2.35 us: row(): return vector.reshape(1, -1)]
    convert_element_type x9 -> x0, other arithmetic: 4.16 us -> none  [the longest x7 2.57 us: added(): return (one.astype(F32) + other.astype(F32)).astype(BF16)]
  transfers between devices with their start and end apart: 19 -> 0, of which waited for: 11 -> 0; matrix products, arithmetic and copies ran while one was open for 3% -> 0% of each run, Pallas kernels for 0% -> 0%
where the time goes in v3:
time: 235 us
  Pallas kernels  230 us (98%)
    pallas_call x1, Pallas kernels, backward(): kernel_call(functools.partial(backward_kernel, shapes, pairs), 'backward'...  130 us
    pallas_call x1, Pallas kernels, start_work(): pl.pallas_call(start_kernel, in_specs=[anywhere] + [vmem] * 5, out_specs=...  38.8 us
    pallas_call x1, Pallas kernels, attend(): kernel_call(functools.partial(attend_kernel, ways), 'attend', (pairs,), [...  29.3 us
    pallas_call x1, Pallas kernels, feed(): pl.pallas_call(functools.partial(feed_kernel, sub), grid_spec=pltpu.Prefe...  27.6 us

profile of v3, /device:TPU:0, one launch (start us, length us, event | category | flops | bytes accessed | tf_op | source)
XLA Modules:
  0.0 234.6 jit_solution(10942076361045033088)
XLA Ops:
  0.8 1.3 pad_maximum_fusion.bias_ref
  2.1 0.0 copy-start.2
  2.1 38.8 %start_work.1 = (bf16[2048,2304]{1,0:T(8,128)(2,1)}, bf16[512,768]{1,0:T(8,128)(2,1)}, bf16[512,768]{1,0:T(8,128)(2,1)}, s32[1,4]{1,0:T(1,128)}) custom-call(bf16[512,768]{1,0:T(8,128)(2,1)} %tokens_ref.1, s32[1,4]{1,0:T(1,128)} %lengths_ref.1, f32[768]{0:T(1024)} %gain_ref.5, f32[768]{0:T(1024)} %shift_ref.2, bf16[768,2304]{1,0:T(8,128)(2,1)} %w_hbm.1, ...), custom_call_target="tpu_custom_call" | custom-call | flops 7247757312 | bytes 12582912 | tf_op jit(solution)/shard_map/start_work/pallas_call | solution.py:1291
  40.9 0.0 copy-done.2
  40.9 0.2 reduce-window.8
  41.1 0.1 convert_reduce_fusion
  41.2 0.3 select_convert_fusion.mark_q
  41.6 0.0 copy-start
  41.6 0.7 slice.8.mark_q
  42.3 0.3 fusion.mark_k
  42.6 0.0 copy-start.1
  42.6 0.7 slice.9.mark_k
  43.3 0.1 copy-done.1
  43.5 29.3 %attend.1 = (bf16[512,768]{1,0:T(8,128)(2,1)}, bf16[12,2048,512]{2,1,0:T(8,128)(2,1)}, f32[16,512]{1,0:T(8,128)}, bf16[512,768]{1,0:T(8,128)(2,1)}) custom-call(bf16[2048,2304]{1,0:T(8,128)(2,1)} %get-tuple-element.39.q_ref.k_ref.v_ref, bf16[2048,2304]{1,0:T(8,128)(2,1)} %get-tuple-element.39.q_ref.k_ref.v_ref, ...), custom_call_target="tpu_custom_call" | custom-call | flops 19327352832 | bytes 25165824 | tf_op jit(solution)/shard_map/attend/pallas_call | solution.py:269
  72.8 0.0 copy-done
  72.8 27.6 %feed.1 = (bf16[512,768]{1,0:T(8,128)(2,1)}, bf16[512,768]{1,0:T(8,128)(2,1)}, f32[512,768]{1,0:T(8,128)}, bf16[2,4,384,768]{3,2,1,0:T(8,128)(2,1)}, bf16[8,96,3...) custom-call(s32[1]{0:T(128)} %bitcast.2.index_ref, ...), custom_call_target="tpu_custom_call" | custom-call | flops 14495514624 | bytes 18874368 | tf_op jit(solution)/shard_map/feed/pallas_call | solution.py:1125
  100.3 129.8 %backward.1 = (bf16[512,768]{1,0:T(8,128)(2,1)}, bf16[512,768]{1,0:T(8,128)(2,1)}, bf16[384,768]{1,0:T(8,128)(2,1)}, bf16[96,3072]{1,0:T(8,128)(2,1)}, bf16[96,7...) custom-call(bf16[12,2048,512]{2,1,0:T(8,128)(2,1)} %get-tuple-element.41.chance_ref, ...), custom_call_target="tpu_custom_call" | custom-call | flops 38654705664 | bytes 25165824 | tf_op jit(solution)/shard_map/backward/pallas_call | solution.py:856
  230.2 4.3 %results.1 = (bf16[512,768]{1,0:T(8,128)(2,1)}, bf16[512,768]{1,0:T(8,128)(2,1)}, f32[96]{0:T(128)}, f32[96]{0:T(128)}, f32[96,2304]{1,0:T(8,128)}, /*index=5*/f...) custom-call(bf16[512,768]{1,0:T(8,128)(2,1)} %get-tuple-element.55.b, ...), custom_call_target="tpu_custom_call" | custom-call | tf_op jit(solution)/shard_map/results/pallas_call | solution.py:947
  (6 shorter events, 0.0 us)
Async XLA Ops:
  2.1 38.8 %copy-start.2 = (s32[1,4]{1,0:T(1,128)S(1)}, s32[1,4]{1,0:T(1,128)}, u32[]{:S(2)}) copy-start(s32[1,4]{1,0:T(1,128)} %lengths_ref.1) | copy-start | bytes 52
  41.6 31.2 %copy-start = (bf16[2048,128]{1,0:T(8,128)(2,1)}, bf16[2048,128]{1,0:T(8,128)(2,1)S(1)}, u32[]{:S(2)}) copy-start(bf16[2048,128]{1,0:T(8,128)(2,1)S(1)} %select_convert_fusion.mark_q) | copy-start | bytes 1572868
  42.6 0.8 copy-start.1

commit v4 on v3

--- a/solution.py
+++ b/solution.py
@@ -181,7 +181,7 @@
             move_sent(*move)
 
 
-def query_grads(chance_ref, grad, keys, values, deltas, sub=1024):
+def query_grads(chance_ref, grad, keys, values, deltas, sub=512):
     turned, grads = jnp.transpose(keys), two_heads(grad)
     delta = jnp.concatenate(deltas, 1)
     total = jnp.zeros((LANES, grads.shape[0]), F32)
@@ -194,7 +194,7 @@
     return scaled_down(own_rows(total)).astype(BF16)
 
 
-def key_grads(key, value, mark_k, parts):
+def key_sums(key, value, mark_k, parts):
     rows = key.shape[0]
     keys = jnp.concatenate([two_heads(key), jnp.concatenate([mark_k, mark_k], 0)], 1)
     values = two_heads(value)
@@ -210,7 +210,7 @@
             grad_scores.append((powers * (grad_chances[at] - deltas[head])).astype(BF16))
         dv += dot_as(jnp.concatenate(chances, 0), grads, NN)
         dk += dot_as(jnp.concatenate(grad_scores, 0), queries, NN)
-    return scaled_down(own_columns(dk)).astype(BF16), own_columns(dv).astype(BF16)
+    return own_columns(dk), own_columns(dv)
 
 
 def grad_query_kernel(chance_ref, grad_ref, k_ref, v_ref, delta_ref, dq_ref):
@@ -233,7 +233,8 @@
             for ref in (lse_refs, delta_refs)
         ]
         parts.append((q_ref[at, :], g_refs[i][...], mark_q[at, :], *stats))
-    dk_ref[...], dv_ref[...] = key_grads(k_ref[...], v_ref[...], mark_k[...], parts)
+    dk, dv = key_sums(k_ref[...], v_ref[...], mark_k[...], parts)
+    dk_ref[...], dv_ref[...] = scaled_down(dk).astype(BF16), dv.astype(BF16)
 
 
 def columns(rows, first):
@@ -259,7 +260,7 @@
 
 
 def attend(plan, own, projected, mark_q, mark_k, cotangent):
-    rows, width = mark_q.shape[0], own.shape[1] // 3
+    rows, width = cotangent.shape
     length, pairs = projected.shape[0], width // LANES
     stats = jax.ShapeDtypeStruct((STATS, rows), F32)
     anywhere = pl.BlockSpec(memory_space=pl.ANY)
@@ -274,7 +275,7 @@
             columns(rows, 0),
             columns(length, pairs),
             columns(length, 2 * pairs),
-            whole(mark_q),
+            pl.BlockSpec((rows, LANES), lambda t: (0, 0)),
             whole(mark_k),
         ]
         + [anywhere] * len(moving),
@@ -377,20 +378,17 @@
             for i, b in enumerate(sends)
         ]
         self.to_far = remote(self.keep.at[last], second, sent.at[3], landed.at[3], far)
-        self.inward = remote(self.keep.at[0], z1, sent.at[4], landed.at[4], devices["pair"])
-        self.middle = remote(self.keep.at[0], z2, sent.at[5], landed.at[5], devices["mirror"])
-        self.outward = remote(z1, self.out, sent.at[6], landed.at[6], devices["pair"])
+        self.bind_along(sent, landed, devices)
+
+    def bind_along(self, sent, landed, devices):
+        pair, z1 = devices["pair"], self.z1
+        self.inward = remote(self.keep.at[0], z1, sent.at[4], landed.at[4], pair)
+        self.middle = remote(self.keep.at[0], self.z2, sent.at[5], landed.at[5], devices["mirror"])
+        self.outward = remote(z1, self.out, sent.at[6], landed.at[6], pair)
         self.store = pltpu.make_async_copy(z1, self.out, landed.at[6])
 
     def add(self, target, one, other):
-        size = 32 if self.shape[0] % 32 == 0 else 16
-
-        def step(i, carry):
-            at = pl.ds(pl.multiple_of(i * size, size), size)
-            target[at, :] = one[at, :] + other[at, :]
-            return carry
-
-        lax.fori_loop(0, self.shape[0] // size, step, 0)
+        target[...] = one[...] + other[...]
 
     def start(self):
         self.to_core.start()
@@ -410,13 +408,16 @@
             if block not in sends:
                 self.add(self.keep.at[block], self.keep.at[block], self.core.at[block])
 
+    def join(self, block):
+        stay = [b for b in range(4) if b not in self.blocks[0]]
+        i = stay.index(block)
+        self.to_near[i].wait_recv()
+        self.add(self.keep.at[block], self.keep.at[block], self.first.at[i])
+
     def far(self):
-        stay = [b for b in range(4) if b not in self.blocks[0]]
-        for i in (1, 0):
-            self.to_near[i].wait_recv()
-            self.add(self.keep.at[stay[i]], self.keep.at[stay[i]], self.first.at[i])
-            if stay[i] == self.blocks[1]:
-                self.to_far.start()
+        self.join(self.blocks[1])
+        self.to_far.start()
+        self.join(0)
 
     def along(self):
         self.to_far.wait_recv()
@@ -453,12 +454,77 @@
             self.middle.wait_send()
             self.outward.wait_send()
 
+        self.settle()
+
+    def settle(self):
         self.to_core.wait_send()
         for copy in self.to_near:
             copy.wait_send()
         self.to_far.wait_send()
 
 
+class DirectChunk:
+    stages = ("start", "near", "far")
+
+    def __init__(self, source, rows, columns, when, dtype=BF16):
+        self.source, self.rows, self.columns = source, rows, columns
+        self.shape = (rows[1], columns[1])
+        self.when, self.dtype = when, dtype
+
+    def scratch(self):
+        rows, columns = self.shape
+        return [pltpu.VMEM(first + (rows, columns), self.dtype) for first in ((8,), (3,), ())] + [
+            pltpu.SemaphoreType.DMA((10,)),
+            pltpu.SemaphoreType.DMA((11,)),
+        ]
+
+    def bind(self, source, out, scratch, devices):
+        at = (pl.ds(*self.rows), pl.ds(*self.columns))
+        self.mine = source.at[(0,) + at]
+        self.landing, self.others, self.total, sent, landed = scratch
+        self.around = [
+            remote(
+                source.at[(place,) + at],
+                self.landing.at[place],
+                sent.at[place - 1],
+                landed.at[place - 1],
+                devices["block"][place],
+            )
+            for place in range(1, 8)
+        ]
+        self.along_z = [
+            remote(self.total, self.others.at[i], sent.at[7 + i], landed.at[7 + i], devices[name])
+            for i, name in enumerate(("pair", "mirror", "opposite"))
+        ]
+        self.store = pltpu.make_async_copy(self.landing.at[0], out.at[at], landed.at[10])
+
+    def start(self):
+        for copy in self.around:
+            copy.start()
+
+    def near(self):
+        total = self.mine[...].astype(F32)
+        for i, copy in enumerate(self.around):
+            copy.wait_recv()
+            total = total + self.landing[1 + i].astype(F32)
+        self.total[...] = total.astype(self.dtype)
+        for copy in self.along_z:
+            copy.start()
+
+    def far(self):
+        for copy in self.along_z:
+            copy.wait_recv()
+        total = self.total[...].astype(F32) + self.others[0].astype(F32)
+        total = total + (self.others[1].astype(F32) + self.others[2].astype(F32))
+        self.landing[0] = total.astype(self.dtype)
+        self.store.start()
+
+    def finish(self):
+        self.store.wait()
+        for copy in self.around + self.along_z:
+            copy.wait_send()
+
+
 def inner():
     z = lax.axis_index("seq")
     return jnp.logical_and(z > 0, z < 3)
@@ -467,66 +533,81 @@
 def ring_devices():
     dp, z = lax.axis_index("dp"), lax.axis_index("seq")
     core, pair, swap = neighbours()
-    x = dp + 2 - 4 * lax.rem(lax.div(dp, jnp.int32(2)), jnp.int32(2))
-    y = dp + 4 - 8 * lax.div(dp, jnp.int32(4))
+
+    def flip(index, bit):
+        size = 1 << bit
+        return index + size - 2 * size * lax.rem(lax.div(index, jnp.int32(size)), jnp.int32(2))
+
+    blocks = []
+    for place in range(8):
+        index = dp
+        for bit, flips in enumerate((place // 4, place % 2, place // 2 % 2)):
+            if flips:
+                index = flip(index, bit)
+        blocks.append((index, z))
     return {
         "core": core,
         "pair": pair,
         "swap": swap,
-        "x": (x, z),
-        "y": (y, z),
+        "x": blocks[1],
+        "y": blocks[2],
         "mirror": (dp, 3 - z),
+        "opposite": (dp, lax.rem(z + 2, jnp.int32(4))),
+        "block": blocks,
     }
 
 
-def relative_place(block):
+def relative_place(*bits):
     dp = lax.axis_index("dp")
-    bits = [lax.rem(lax.div(dp, jnp.int32(1 << k)) + (block >> k) % 2, jnp.int32(2)) for k in range(3)]
-    return bits[0] * 4 + bits[1] + bits[2] * 2
+    turned = [
+        lax.rem(lax.div(dp, jnp.int32(1 << k)) + bit, jnp.int32(2)) for k, bit in enumerate(bits)
+    ]
+    return turned[0] * 4 + turned[1] + turned[2] * 2
+
+
+def bits_of(block):
+    return [(block >> k) % 2 for k in range(3)]
 
 
 def store_blocks(target, columns, total):
     part = total.shape[0] // 8
     for block in range(8):
-        target[relative_place(block), :, columns] = total[block * part : (block + 1) * part].astype(BF16)
+        target[relative_place(*bits_of(block)), :, columns] = total[block * part : (block + 1) * part].astype(BF16)
 
 
 VECTORS = 16
 
 
 def backward_chunks(shapes, width, pairs):
-    down, up, out = shapes
-    third, share = down[1] // 3, up[2] // 3
-    part = width // 8
+    down, up, _ = shapes
+    part, quarter, share = width // 8, down[1] // 4, up[2] // 4
     end = 4 * pairs
+    tile = LANES
 
     def when(*steps):
         return tuple(at if isinstance(at, tuple) else (at, 0) for at in steps)
 
-    tile = 2 * LANES
-    ends = [tuple((end, i) for i in range(n)) for n in range(8)]
+    rows, whole_width = (0, part), (0, width)
+    downs = [((i * quarter, quarter), whole_width, i % 2 == 0) for i in range(4)]
+    ups = [(rows, (i * share, share), i % 2 == 0) for i in range(4)]
     return [
-        Chunk("down", (0, third), (0, width), True, when(0, 2, 8, 14, 16, 18)),
-        Chunk("down", (third, third), (0, width), False, when(0, 2, 8, 14, 16, 18)),
-        Chunk("up", (0, part), (0, share), True, when(1, 4, 12, 17, 19, 21)),
-        Chunk("up", (0, part), (share, share), False, when(1, 4, 12, 17, 19, 21)),
-        Chunk("down", (2 * third, third), (0, width), True, when(3, 10, 16, 20, 21, 23)),
-        Chunk("up", (0, part), (2 * share, share), False, when(3, 10, 16, 20, 21, 23)),
-        Chunk("out", (0, part), (0, width), True, when(6, 13, 19, 22, 23, (end, 1))),
-        Chunk("query", (0, part), (0, width), False, when(12, 13, 19, 22, 23, (end, 1)), True),
-        Chunk("pair", (0, part), (0, 2 * tile), True, when(20, 21, 23, *ends[4][1:]), True),
-        Chunk("pair", (0, part), (2 * tile, 2 * tile), False, when(22, 23, *ends[5][1:]), True),
-        Chunk("pair", (0, part), (4 * tile, tile), True, when(23, *ends[6][1:]), True),
-        Chunk("pair", (0, part), (5 * tile, tile), False, when((end, 0), *ends[7][2:]), True),
-        Chunk(
-            "vector",
-            (0, VECTORS),
-            (0, LANES),
-            True,
-            when((end, 0), *ends[7][2:]),
-            True,
-            F32,
-        ),
+        Chunk("down", *downs[0], when(0, 1, 4, 8, 12, 15)),
+        Chunk("down", *downs[1], when(0, 1, 4, 8, 12, 15)),
+        Chunk("down", *downs[2], when(1, 3, 6, 10, 13, 16)),
+        Chunk("down", *downs[3], when(1, 3, 6, 10, 13, 16)),
+        Chunk("up", *ups[0], when(3, 5, 8, 12, 15, 18)),
+        Chunk("up", *ups[1], when(3, 5, 8, 12, 15, 18)),
+        Chunk("up", *ups[2], when(5, 7, 11, 14, 17, 20)),
+        Chunk("up", *ups[3], when(5, 7, 11, 14, 17, 20)),
+        Chunk("out", rows, whole_width, True, when(7, 10, 13, 16, 19, 21)),
+        Chunk("pair", rows, (0 * tile, 4 * tile), False, when(14, 15, 17, 19, 21, 23), True),
+        Chunk("pair", rows, (4 * tile, 4 * tile), True, when(16, 17, 19, 21, 23, (end, 0)), True),
+        Chunk("pair", rows, (8 * tile, 4 * tile), False, when(18, 19, 21, 23, (end, 0), (end, 1)), True),
+        Chunk("query", rows, (0, 2 * tile), True, when(20, 21, 23, (end, 0), (end, 1), (end, 2)), True),
+        Chunk("query", rows, (2 * tile, 2 * tile), False, when(22, 23, (end, 0), (end, 1), (end, 2), (end, 3)), True),
+        DirectChunk("query", rows, (4 * tile, tile), when(23, (end, 0), (end, 2))),
+        DirectChunk("query", rows, (5 * tile, tile), when((end, 0), (end, 1), (end, 3))),
+        DirectChunk("vector", (0, VECTORS), (0, LANES), when((end, 0), (end, 1), (end, 3)), F32),
     ]
 
 
@@ -566,13 +647,13 @@
     own_stats,
     turned,
     dq,
-    dkv,
     grad_hidden,
     query_grad,
     pair_grad,
     vector,
     late,
     tokens,
+    partial,
     weights,
     hidden_ref,
     here_ref,
@@ -590,7 +671,7 @@
         for i, (source, target) in enumerate(held)
     ]
     half = rows // 2
-    first, steps = 2 * pairs, 4 * pairs
+    steps = 4 * pairs
     devices = ring_devices()
     chunks = backward_chunks(shapes, width, pairs)
     sources = {
@@ -615,7 +696,7 @@
     def grad_copy(i, part, source, device):
         at = pl.ds(part * half, half)
         n = 2 * i + part
-        return remote(source.at[at], grads.at[i, at], sent.at[n], landed.at[n], device)
+        return remote(source.at[at], grads.at[i - 1, at], sent.at[n], landed.at[n], device)
 
     def to_core(part):
         return grad_copy(1, part, grad_ref, devices["core"])
@@ -624,7 +705,7 @@
         return grad_copy(2, part, grad_ref, devices["pair"])
 
     def to_corner(part):
-        return grad_copy(3, part, grads.at[2], devices["core"])
+        return grad_copy(3, part, grads.at[1], devices["core"])
 
     def stat_copy(i, source, device):
         return remote(source, stats.at[i], sent.at[8 + i], landed.at[8 + i], device)
@@ -634,7 +715,7 @@
     stat_corner = stat_copy(3, stats.at[2], devices["core"])
 
     def begin():
-        greet(list(devices.values()))
+        greet(devices["block"][1:] + [devices[name] for name in ("pair", "swap", "mirror", "opposite")])
         for part in range(2):
             to_pair(part).start()
         for part in range(2):
@@ -654,10 +735,18 @@
         own_stats[0:STATS, :] = lse_ref[...]
         own_stats[STATS:, :] = dot_as(mine, high, NT) + dot_as(mine, low, NT)
         stats[0] = own_stats[...]
-        grads[0] = grad_ref[...]
         stat_pair.start()
         stat_core.start()
         late[...] = jnp.zeros_like(late)
+        grad_hidden[...] = jnp.zeros_like(grad_hidden)
+        stat_core.wait_recv()
+        for part in range(2):
+            to_core(part).wait_recv()
+
+    def loaded_all():
+        for load in loads:
+            load.wait()
+        turned[...] = jnp.transpose(hidden_ref[...])
 
     def corner_stats():
         stat_pair.wait_recv()
@@ -670,20 +759,10 @@
 
         return run
 
-    def all_grads():
-        stat_core.wait_recv()
+    def far_grads():
         stat_corner.wait_recv()
         for part in range(2):
-            to_core(part).wait_recv()
             to_corner(part).wait_recv()
-
-    def query_done():
-        for load in loads:
-            load.wait()
-        turned[...] = jnp.transpose(hidden_ref[...])
-        store_blocks(query_grad, pl.ds(0, width), dot_as(turned[...], dq[...], NN))
-        grad_hidden[...] = dot_as(dq[...], weights[:, 0:width], NT)
-        late[0:1, :] = jnp.sum(dq[...].astype(F32), 0, keepdims=True)
 
     def first_norm(part):
         def run():
@@ -707,7 +786,7 @@
         share = width // 8
         vector[...] = jnp.zeros_like(vector)
         for block in range(8):
-            place = relative_place(block)
+            place = relative_place(*bits_of(block))
             vector[place, 0:4, 0:share] = sums_ref[0:4, block * share : (block + 1) * share]
             for i in range(4):
                 first = (block * 4 + i) * share
@@ -716,7 +795,7 @@
     def late_vectors():
         share = width // 8
         for block in range(8):
-            vector[relative_place(block), 4:8, 0:share] = late[
+            vector[relative_place(*bits_of(block)), 4:8, 0:share] = late[
                 0:4, block * share : (block + 1) * share
             ]
 
@@ -733,23 +812,24 @@
 
     events = [
         ((0, -2), begin),
-        ((0, 1), begin_stats),
-        ((4, -1), corner_stats),
-        ((4, 2), early_vectors),
+        ((0, -1), begin_stats),
+        ((1, 1), early_vectors),
+        ((2, -1), corner_stats),
         ((8, -1), corner(0)),
-        ((first, -2), corner(1)),
-        ((first, -1), query_done),
-        ((first, 3), lambda: move_start(*block_move)),
-        ((first, 4), all_grads),
-        ((first + pairs, -1), first_norm(0)),
+        ((5, 1), loaded_all),
+        ((4, 3), lambda: move_start(*block_move)),
+        ((11, -1), corner(1)),
+        ((2 * pairs, 1), far_grads),
+        ((3 * pairs, -1), first_norm(0)),
         ((steps, -2), first_norm(1)),
         ((steps, -1), late_vectors),
-        ((steps, 9), finish_moves),
+        ((steps, 99), finish_moves),
     ]
-    for order in (2, 1, 0, 3, 4, 5, 6):
+    for order in (2, 1, 0, 3, 4, 5):
         for chunk in chunks:
-            at = chunk.when[order] if order < 6 else (steps, 8)
-            events.append((at, getattr(chunk, Chunk.stages[order])))
+            if order < len(chunk.when):
+                events.append((chunk.when[order], getattr(chunk, chunk.stages[order])))
+    events += [((steps, 98), chunk.finish) for chunk in chunks]
     events.sort(key=lambda event: event[0])
 
     def run(at):
@@ -764,41 +844,52 @@
             def _():
                 run(at)
 
-    @pl.when(step < first)
-    def _():
-        pair = lax.div(step, jnp.int32(2))
-        at = pl.ds(pl.multiple_of(lax.rem(step, jnp.int32(2)) * half, half), half)
-        tile = pl.ds(pl.multiple_of(pair * LANES, LANES), LANES)
-        deltas = [own_stats[pl.ds(STATS + 2 * pair + head, 1), at] for head in range(2)]
-        dq[at, tile] = query_grads(chance_ref, grad_ref[at, tile], k_ref[...], v_ref[...], deltas)
-
-    @pl.when(step >= first)
-    def _():
-        pair = lax.rem(step, jnp.int32(pairs))
-        at = pl.ds(pl.multiple_of((lax.div(step, jnp.int32(pairs)) - 2) * half, half), half)
-        tile = pl.ds(pl.multiple_of(pair * LANES, LANES), LANES)
-        double = pl.ds(pl.multiple_of(pair * (2 * LANES), 2 * LANES), 2 * LANES)
-
-        def weight(part):
-            return weights[:, pl.ds(pl.multiple_of(part * width + pair * LANES, LANES), LANES)]
-
+    pair = lax.rem(step, jnp.int32(pairs))
+    tile = pl.ds(pl.multiple_of(pair * LANES, LANES), LANES)
+    double = pl.ds(pl.multiple_of(pair * (2 * LANES), 2 * LANES), 2 * LANES)
+
+    def weight(part):
+        return weights[:, pl.ds(pl.multiple_of(part * width + pair * LANES, LANES), LANES)]
+
+    def keys_of(pieces):
         parts = []
-        for i in range(4):
-            span = pl.ds(i * rows, rows)
+        for i, first in [(i, first) for i in pieces for first in (0, half)]:
+            span, at = pl.ds(i * rows + first, half), pl.ds(first, half)
             rows_of = [
-                [stats[i, pl.ds(start + 2 * pair + head, 1), :] for head in range(2)]
+                [stats[i, pl.ds(start + 2 * pair + head, 1), at] for head in range(2)]
                 for start in (0, STATS)
             ]
-            parts.append((q_ref[span, :], grads[i, :, tile], mark_q[span, :], *rows_of))
-        dk, dv = key_grads(k_ref[at, :], v_ref[at, :], mark_k[at, :], parts)
-        both = jnp.concatenate([dk, dv], 1)
-        dkv[at, double] = both
-        grad_hidden[at, :] += dot_as(both, jnp.concatenate([weight(1), weight(2)], 1), NT)
-        late[1:2, tile] += jnp.sum(dv.astype(F32), 0, keepdims=True)
-
-        @pl.when(step >= first + pairs)
+            piece = grad_ref if i == 0 else grads.at[i - 1]
+            parts.append((q_ref[span, :], piece[at, tile], mark_q[span, :], *rows_of))
+        return key_sums(k_ref[0:rows, :], v_ref[0:rows, :], mark_k[...], parts)
+
+    @pl.when(step < pairs)
+    def _():
+        partial[pair, 0], partial[pair, 1] = keys_of((0, 1))
+
+    @pl.when(jnp.logical_and(step >= 2 * pairs, step < 3 * pairs))
+    def _():
+        dk, dv = keys_of((2, 3))
+        dk = scaled_down(dk + partial[pair, 0]).astype(BF16)
+        dv = dv + partial[pair, 1]
+        late[1:2, tile] = jnp.sum(dv.astype(BF16).astype(F32), 0, keepdims=True)
+        both = jnp.concatenate([dk, dv.astype(BF16)], 1)
+        store_blocks(pair_grad, double, dot_as(turned[...], both, NN))
+        grad_hidden[...] += dot_as(both, jnp.concatenate([weight(1), weight(2)], 1), NT)
+
+    @pl.when(lax.rem(lax.div(step, jnp.int32(pairs)), jnp.int32(2)) == 1)
+    def _():
+        part = lax.div(step, jnp.int32(2 * pairs))
+        at = pl.ds(pl.multiple_of(part * half, half), half)
+        deltas = [own_stats[pl.ds(STATS + 2 * pair + head, 1), at] for head in range(2)]
+        found = query_grads(chance_ref, grad_ref[at, tile], k_ref[...], v_ref[...], deltas)
+        dq[at, tile] = found
+        late[0:1, tile] += jnp.sum(found.astype(F32), 0, keepdims=True)
+        grad_hidden[at, :] += dot_as(found, weight(0), NT)
+
+        @pl.when(part == 1)
         def _():
-            store_blocks(pair_grad, double, dot_as(turned[...], dkv[:, double], NN))
+            store_blocks(query_grad, tile, dot_as(turned[...], dq[:, tile], NN))
 
     @pl.when(step == steps - 1)
     def _():
@@ -839,15 +930,15 @@
     ]
     outs.append(jax.ShapeDtypeStruct((VECTORS, LANES), F32))
 
-    def pair_at(t):
-        return jnp.where(t < 2 * pairs, lax.div(t, 2), lax.rem(t, pairs))
-
     def tile(first):
-        return pl.BlockSpec((length, LANES), lambda t: (0, first + pair_at(t)))
+        return pl.BlockSpec((length, LANES), lambda t: (0, first + lax.rem(t, pairs)))
 
     def chance_at(t):
-        t = jnp.minimum(t, 2 * pairs - 1)
-        return lax.div(t, 2), 0, lax.rem(t, 2)
+        phase = lax.div(t, pairs)
+        return jnp.where(lax.rem(phase, 2) == 1, lax.rem(t, pairs), 0), 0, lax.div(phase, 2)
+
+    def query_at(t):
+        return 0, jnp.where(lax.rem(lax.div(t, pairs), 2) == 0, lax.rem(t, pairs), pairs - 1)
 
     fixed = [mark_k, mark_q, log_totals, gain, sums, sum_up]
     held = [weight, hidden, here, grad_middle]
@@ -863,25 +954,26 @@
             once(attended),
             tile(pairs),
             tile(2 * pairs),
-            pl.BlockSpec((length, LANES), lambda t: (0, lax.rem(jnp.maximum(t - 2 * pairs, 0), pairs))),
+            pl.BlockSpec((length, LANES), query_at),
         ]
-        + [once(array) for array in fixed]
+        + [pl.BlockSpec((rows, LANES), lambda t: (0, 0), pipeline_mode=pl.Buffered(1))]
+        + [once(array) for array in fixed[1:]]
         + [anywhere] * (len(held) + len(totals) + 1),
         [anywhere] * len(outs),
         outs,
         [
-            pltpu.VMEM((4, rows, width), BF16),
+            pltpu.VMEM((3, rows, width), BF16),
             pltpu.VMEM((4,) + stats, F32),
             pltpu.VMEM(stats, F32),
             pltpu.VMEM((width, rows), BF16),
             pltpu.VMEM((rows, width), BF16),
-            pltpu.VMEM((rows, 2 * width), BF16),
             pltpu.VMEM((rows, width), F32),
             pltpu.VMEM((8, part, width), BF16),
             pltpu.VMEM((8, part, 2 * width), BF16),
             pltpu.VMEM((8, VECTORS, LANES), F32),
             pltpu.VMEM((8, width), F32),
             pltpu.VMEM((rows, width), BF16),
+            pltpu.VMEM((pairs, 2, rows, LANES), F32),
         ]
         + [pltpu.VMEM(array.shape, array.dtype) for array in held]
         + [
@@ -1335,7 +1427,7 @@
         return jnp.concatenate(found)
 
     def own(self, gathered):
-        return gathered[: gathered.shape[0] // 4]
+        return gathered
 
     def backward(self, work, weights, attention):
         here, hidden1, grad_out, projected, own, mark_k, mark_q = work

time: 235 us -> 233 us (level)
  no operation moved by 1% of the time
where the time goes in v4:
time: 233 us; the launch traced here: 232 us
  Pallas kernels  228 us (98%)
  other arithmetic  3.89 us (2%)
    pallas_call x1, Pallas kernels, backward(): kernel_call(functools.partial(backward_kernel, shapes, pairs), 'backward'...  128 us
    pallas_call x1, Pallas kernels, start_work(): pl.pallas_call(start_kernel, in_specs=[anywhere] + [vmem] * 5, out_specs=...  38.8 us
    pallas_call x1, Pallas kernels, attend(): kernel_call(functools.partial(attend_kernel, ways), 'attend', (pairs,), [...  29.3 us
    pallas_call x1, Pallas kernels, feed(): pl.pallas_call(functools.partial(feed_kernel, sub), grid_spec=pltpu.Prefe...  27.6 us

profile of v4, /device:TPU:0, one launch (start us, length us, event | category | flops | bytes accessed | tf_op | source)
XLA Modules:
  0.0 232.4 jit_solution(7571174713349179302)
XLA Ops:
  0.8 1.3 pad_maximum_fusion.bias_ref
  2.1 0.0 copy-start
  2.1 38.8 %start_work.1 = (bf16[2048,2304]{1,0:T(8,128)(2,1)}, bf16[512,768]{1,0:T(8,128)(2,1)}, bf16[512,768]{1,0:T(8,128)(2,1)}, s32[1,4]{1,0:T(1,128)}) custom-call(bf16[512,768]{1,0:T(8,128)(2,1)} %tokens_ref.1, s32[1,4]{1,0:T(1,128)} %lengths_ref.1, f32[768]{0:T(1024)} %gain_ref.5, f32[768]{0:T(1024)} %shift_ref.2, bf16[768,2304]{1,0:T(8,128)(2,1)} %w_hbm.1, ...), custom_call_target="tpu_custom_call" | custom-call | flops 7247757312 | bytes 12582912 | tf_op jit(solution)/shard_map/start_work/pallas_call | solution.py:1383
  40.9 0.0 copy-done
  40.9 0.2 reduce-window.8
  41.1 0.1 convert_reduce_fusion
  41.2 1.1 select_convert_fusion.mark_q
  42.3 1.1 fusion.mark_k
  43.5 29.3 %attend.1 = (bf16[512,768]{1,0:T(8,128)(2,1)}, bf16[12,2048,512]{2,1,0:T(8,128)(2,1)}, f32[16,512]{1,0:T(8,128)}, bf16[512,768]{1,0:T(8,128)(2,1)}) custom-call(bf16[2048,2304]{1,0:T(8,128)(2,1)} %get-tuple-element.39.q_ref.k_ref.v_ref, bf16[2048,2304]{1,0:T(8,128)(2,1)} %get-tuple-element.39.q_ref.k_ref.v_ref, ...), custom_call_target="tpu_custom_call" | custom-call | flops 19327352832 | bytes 25165824 | tf_op jit(solution)/shard_map/attend/pallas_call | solution.py:270
  72.7 27.6 %feed.1 = (bf16[512,768]{1,0:T(8,128)(2,1)}, bf16[512,768]{1,0:T(8,128)(2,1)}, f32[512,768]{1,0:T(8,128)}, bf16[2,4,384,768]{3,2,1,0:T(8,128)(2,1)}, bf16[8,96,3...) custom-call(s32[1]{0:T(128)} %bitcast.2.index_ref, ...), custom_call_target="tpu_custom_call" | custom-call | flops 14495514624 | bytes 18874368 | tf_op jit(solution)/shard_map/feed/pallas_call | solution.py:1217
  100.3 127.7 %backward.1 = (bf16[512,768]{1,0:T(8,128)(2,1)}, bf16[512,768]{1,0:T(8,128)(2,1)}, bf16[384,768]{1,0:T(8,128)(2,1)}, bf16[96,3072]{1,0:T(8,128)(2,1)}, bf16[96,7...) custom-call(bf16[12,2048,512]{2,1,0:T(8,128)(2,1)} %get-tuple-element.41.chance_ref, ...), custom_call_target="tpu_custom_call" | custom-call | flops 38654705664 | bytes 25165824 | tf_op jit(solution)/shard_map/backward/pallas_call | solution.py:947
  228.0 4.3 %results.1 = (bf16[512,768]{1,0:T(8,128)(2,1)}, bf16[512,768]{1,0:T(8,128)(2,1)}, f32[96]{0:T(128)}, f32[96]{0:T(128)}, f32[96,2304]{1,0:T(8,128)}, /*index=5*/f...) custom-call(bf16[512,768]{1,0:T(8,128)(2,1)} %get-tuple-element.55.b, ...), custom_call_target="tpu_custom_call" | custom-call | tf_op jit(solution)/shard_map/results/pallas_call | solution.py:1039
  (6 shorter events, 0.0 us)
Async XLA Ops:
  2.1 38.8 %copy-start = (s32[1,4]{1,0:T(1,128)S(1)}, s32[1,4]{1,0:T(1,128)}, u32[]{:S(2)}) copy-start(s32[1,4]{1,0:T(1,128)} %lengths_ref.1) | copy-start | bytes 52

commit v5 on v4

--- a/solution.py
+++ b/solution.py
@@ -1282,7 +1282,8 @@
     gain_ref,
     shift_ref,
     w_ref,
-    bias_ref,
+    query_ref,
+    value_ref,
     projected_ref,
     hidden_ref,
     here_ref,
@@ -1294,6 +1295,8 @@
     out_sem,
 ):
     core, across, swap = neighbours()
+    query = row_of(query_ref)
+    bias = jnp.concatenate([query, jnp.zeros_like(query), row_of(value_ref)], 1)
     parts = sent.shape[1]
     height = tokens_ref.shape[0]
     part = height // parts
@@ -1328,7 +1331,7 @@
         values = rows[piece, span(i), :].astype(F32)
         hidden = layer_norm(values, row_of(gain_ref), row_of(shift_ref))[0].astype(BF16)
         staged[out_span(piece, i), :] = (
-            dot_as(hidden, w_ref[...], NN) + row_of(bias_ref)
+            dot_as(hidden, w_ref[...], NN) + bias
         ).astype(BF16)
         to_hbm(piece, i).start()
         return hidden
@@ -1377,12 +1380,12 @@
     lax.fori_loop(0, parts, last, 0)
 
 
-def start_work(tokens, clip_lengths, gain, shift, weight, bias):
+def start_work(tokens, clip_lengths, gain, shift, weight, query, value):
     rows, width = tokens.shape
     vmem, anywhere = pl.BlockSpec(memory_space=pltpu.VMEM), pl.BlockSpec(memory_space=pl.ANY)
     projected, hidden, here, found = pl.pallas_call(
         start_kernel,
-        in_specs=[anywhere] + [vmem] * 5,
+        in_specs=[anywhere] + [vmem] * 6,
         out_specs=[anywhere, vmem, vmem, vmem],
         out_shape=[
             jax.ShapeDtypeStruct((4 * rows, 3 * width), BF16),
@@ -1404,16 +1407,16 @@
             flops=24 * rows * width * width, bytes_accessed=32 * rows * width, transcendentals=0
         ),
         name="start_work",
-    )(tokens, clip_lengths, gain, shift, weight, bias)
+    )(tokens, clip_lengths, gain, shift, weight, query, value)
     return projected, hidden, here, jnp.where(stays(), clip_lengths, found)
 
 
 class PairPlan:
     ways = True
 
-    def start(self, tokens, clip_lengths, gain, shift, weight, bias):
+    def start(self, tokens, clip_lengths, gain, shift, weight, query, value):
         projected, hidden, here, lengths = start_work(
-            tokens, clip_lengths, gain, shift, weight, bias
+            tokens, clip_lengths, gain, shift, weight, query, value
         )
         return projected, projected, hidden, here, lengths
 
@@ -1464,8 +1467,9 @@
     def __init__(self, pieces):
         self.pieces = pieces
 
-    def start(self, tokens, clip_lengths, gain, shift, weight, bias):
+    def start(self, tokens, clip_lengths, gain, shift, weight, query, value):
         hidden = layer_norm(tokens.astype(F32), gain, shift)[0].astype(BF16)
+        bias = jnp.concatenate([query, jnp.zeros_like(query), value])
         own = (matmul(hidden, weight) + bias).astype(BF16)
         projected = lax.all_gather(own, "seq", axis=0, tiled=True)
         return projected, own, hidden, tokens, clip_lengths
@@ -1564,9 +1568,8 @@
     cotangent,
 ):
     rows, width = tokens.shape
-    bias = jnp.concatenate([bias_query, jnp.zeros_like(bias_query), bias_value])
     projected, own, hidden1, here, lengths = plan.start(
-        tokens, clip_lengths, ln1_gain, ln1_shift, w_qkv, bias
+        tokens, clip_lengths, ln1_gain, ln1_shift, w_qkv, bias_query, bias_value
     )
 
     clip_ends = jnp.cumsum(lengths.reshape(-1))

time: 233 us -> 231 us (level)
  no operation moved by 1% of the time
where the time goes in v5:
time: 231 us
  Pallas kernels  228 us (99%)
  other arithmetic  2.58 us (1%)
    pallas_call x1, Pallas kernels, backward(): kernel_call(functools.partial(backward_kernel, shapes, pairs), 'backward'...  128 us
    pallas_call x1, Pallas kernels, start_work(): pl.pallas_call(start_kernel, in_specs=[anywhere] + [vmem] * 6, out_specs=...  38.8 us
    pallas_call x1, Pallas kernels, attend(): kernel_call(functools.partial(attend_kernel, ways), 'attend', (pairs,), [...  29.3 us
    pallas_call x1, Pallas kernels, feed(): pl.pallas_call(functools.partial(feed_kernel, sub), grid_spec=pltpu.Prefe...  27.6 us

profile of v5, /device:TPU:0, one launch (start us, length us, event | category | flops | bytes accessed | tf_op | source)
XLA Modules:
  0.0 231.1 jit_solution(5826244841793386792)
XLA Ops:
  0.8 0.0 copy-start
  0.8 38.8 %start_work.1 = (bf16[2048,2304]{1,0:T(8,128)(2,1)}, bf16[512,768]{1,0:T(8,128)(2,1)}, bf16[512,768]{1,0:T(8,128)(2,1)}, s32[1,4]{1,0:T(1,128)}) custom-call(bf16[512,768]{1,0:T(8,128)(2,1)} %tokens_ref.1, s32[1,4]{1,0:T(1,128)} %lengths_ref.1, f32[768]{0:T(1024)} %gain_ref.5, f32[768]{0:T(1024)} %shift_ref.2, bf16[768,2304]{1,0:T(8,128)(2,1)} %w_hbm.1, ...), custom_call_target="tpu_custom_call" | custom-call | flops 7247757312 | bytes 12582912 | tf_op jit(solution)/shard_map/start_work/pallas_call | solution.py:1386
  39.6 0.0 copy-done
  39.6 0.2 reduce-window.8
  39.8 0.1 convert_reduce_fusion
  39.9 1.1 select_convert_fusion.mark_q
  41.0 1.1 fusion.mark_k
  42.2 29.3 %attend.1 = (bf16[512,768]{1,0:T(8,128)(2,1)}, bf16[12,2048,512]{2,1,0:T(8,128)(2,1)}, f32[16,512]{1,0:T(8,128)}, bf16[512,768]{1,0:T(8,128)(2,1)}) custom-call(bf16[2048,2304]{1,0:T(8,128)(2,1)} %get-tuple-element.39.q_ref.k_ref.v_ref, bf16[2048,2304]{1,0:T(8,128)(2,1)} %get-tuple-element.39.q_ref.k_ref.v_ref, ...), custom_call_target="tpu_custom_call" | custom-call | flops 19327352832 | bytes 25165824 | tf_op jit(solution)/shard_map/attend/pallas_call | solution.py:270
  71.4 27.6 %feed.1 = (bf16[512,768]{1,0:T(8,128)(2,1)}, bf16[512,768]{1,0:T(8,128)(2,1)}, f32[512,768]{1,0:T(8,128)}, bf16[2,4,384,768]{3,2,1,0:T(8,128)(2,1)}, bf16[8,96,3...) custom-call(s32[1]{0:T(128)} %bitcast.2.index_ref, ...), custom_call_target="tpu_custom_call" | custom-call | flops 14495514624 | bytes 18874368 | tf_op jit(solution)/shard_map/feed/pallas_call | solution.py:1217
  99.0 127.7 %backward.1 = (bf16[512,768]{1,0:T(8,128)(2,1)}, bf16[512,768]{1,0:T(8,128)(2,1)}, bf16[384,768]{1,0:T(8,128)(2,1)}, bf16[96,3072]{1,0:T(8,128)(2,1)}, bf16[96,7...) custom-call(bf16[12,2048,512]{2,1,0:T(8,128)(2,1)} %get-tuple-element.41.chance_ref, ...), custom_call_target="tpu_custom_call" | custom-call | flops 38654705664 | bytes 25165824 | tf_op jit(solution)/shard_map/backward/pallas_call | solution.py:947
  226.7 4.3 %results.1 = (bf16[512,768]{1,0:T(8,128)(2,1)}, bf16[512,768]{1,0:T(8,128)(2,1)}, f32[96]{0:T(128)}, f32[96]{0:T(128)}, f32[96,2304]{1,0:T(8,128)}, /*index=5*/f...) custom-call(bf16[512,768]{1,0:T(8,128)(2,1)} %get-tuple-element.55.b, ...), custom_call_target="tpu_custom_call" | custom-call | tf_op jit(solution)/shard_map/results/pallas_call | solution.py:1039
  (5 shorter events, 0.0 us)
Async XLA Ops:
  0.8 38.8 %copy-start = (s32[1,4]{1,0:T(1,128)S(1)}, s32[1,4]{1,0:T(1,128)}, u32[]{:S(2)}) copy-start(s32[1,4]{1,0:T(1,128)} %lengths_ref.1) | copy-start | bytes 52
